TPU v7x, 1024 devices: a whole 4x8x16 slice. The times are simulated.
1024 devices in a mesh: row: 32 (over z, y_lo), col: 16 (over y_hi, x), feat: 2 (over core).
Axes of the slice: x: 4, y: 8 (y_hi: 4, y_lo: 2; y = y_hi * 2 + y_lo), z: 16, core: 2. Of those that a mesh axis runs over, the one named last changes fastest.
Arguments:
- features: bfloat16 [262144, 256], P(('row', 'col'), 'feat'), may hold values from -6 to 6
- adj: bfloat16 [2048, 8, 128, 128], P(('row', 'col')), as said below
- col_index: int32 [2048, 8], P(('row', 'col')), may hold values from 0 to 2047, as said below
- weight: bfloat16 [256, 256], replicated, may hold values from -0.375 to 0.375
- centroid: bfloat16 [1024, 256], P(None, 'feat'), may hold values from -5 to 5
- labels: int32 [262144], P(('row', 'col')), may hold values from 0 to 1023
Outputs:
- weight_grad: float32 [256, 256], P('feat')
- feature_grad: bfloat16 [262144, 256], P(('row', 'col'), 'feat')
Inputs may be any that keep to these rules, and one draw needn't show every extreme that they name: `col_index`: every column index of block row i lies in its aligned group of 64 block rows, from i - i % 64 to i - i % 64 + 63; indices may repeat within a block row. `adj`: A is symmetric: the blocks of all rows pair one to one so that block s of block row i, at column j = col_index[i, s], is the transpose of a block of block row j at column i.
All inputs are finite; a program needn't handle non-finite values.
Results may differ from a plain program's by a relative error of at most 0.0057.
Values may be sent and summed in bfloat16 or wider, within the bound.
No kernel may reach another device: no remote copies, remote signals or barrier semaphores. Data moves between devices by JAX's collectives and lax.ppermute only.
A program may use at most 32 MiB of HBM per device.

v0:
```python
import math

import jax
import jax.numpy as jnp
from jax import lax
from jax.sharding import PartitionSpec as P


def silu_slope(value):
    logistic = jax.nn.sigmoid(value)
    return logistic * (1.0 + value * (1.0 - logistic))


def block_product(grouped, local_cols, blocks):
    panels = grouped[local_cols]
    return jnp.einsum("rkij,rkjf->rif", blocks, panels, preferred_element_type=jnp.float32)


def per_device(features, adj, col_index, weight, centroid, labels):
    block_rows, nonzero, block_size, _ = adj.shape
    row_count, in_half = features.shape
    out_half = centroid.shape[1]
    feat_index = lax.axis_index("feat")
    group_blocks = block_rows * lax.axis_size("col")
    local_cols = col_index % group_blocks
    node_count = row_count * lax.axis_size("row") * lax.axis_size("col")
    gathered = lax.all_gather(features, "col", axis=0, tiled=True)
    aggregated = block_product(gathered.reshape(group_blocks, block_size, in_half), local_cols, adj)
    aggregated = aggregated.reshape(row_count, in_half).astype(jnp.bfloat16)
    in_rows = lax.dynamic_slice_in_dim(weight, feat_index * in_half, in_half, 0)
    joined = lax.all_gather(aggregated, "feat", axis=1, tiled=True)
    out_cols = lax.dynamic_slice_in_dim(weight, feat_index * out_half, out_half, 1)
    logits = jnp.dot(joined, out_cols, preferred_element_type=jnp.float32)
    label_table = (
        labels[:, None] == jnp.arange(centroid.shape[0], dtype=jnp.int32)[None, :]
    ).astype(jnp.bfloat16)
    target = jnp.dot(label_table, centroid, preferred_element_type=jnp.float32)
    grad_out = ((jax.nn.silu(logits) - target) * silu_slope(logits)).astype(jnp.bfloat16)
    grad_full = lax.all_gather(grad_out, "feat", axis=1, tiled=True)
    partial_weight = lax.dot_general(
        aggregated, grad_full, (((0,), (0,)), ((), ())), preferred_element_type=jnp.float32
    )
    weight_grad = lax.psum(partial_weight, ("row", "col")) / math.sqrt(node_count)
    back_projected = lax.dot_general(
        grad_full, in_rows, (((1,), (1,)), ((), ())), preferred_element_type=jnp.float32
    ).astype(jnp.bfloat16)
    contrib = jnp.einsum(
        "rkji,rjf->rkif",
        adj,
        back_projected.reshape(block_rows, block_size, in_half),
        preferred_element_type=jnp.float32,
    )
    owner_table = (
        local_cols.reshape(-1)[:, None] == jnp.arange(group_blocks, dtype=jnp.int32)[None, :]
    ).astype(jnp.float32)
    partial_grad = jnp.einsum(
        "ng,nx->gx",
        owner_table,
        contrib.reshape(block_rows * nonzero, block_size * in_half),
        precision=lax.Precision.HIGHEST,
    )
    summed = lax.psum_scatter(
        partial_grad.reshape(group_blocks * block_size, in_half),
        "col",
        scatter_dimension=0,
        tiled=True,
    )
    return (weight_grad, summed.astype(jnp.bfloat16))


def solution(mesh):
    placed = (
        P(("row", "col"), "feat"),
        P(("row", "col"), None, None, None),
        P(("row", "col"), None),
        P(),
        P(None, "feat"),
        P(("row", "col")),
    )
    return jax.shard_map(
        per_device,
        mesh=mesh,
        in_specs=placed,
        out_specs=(P("feat", None), P(("row", "col"), "feat")),
        check_vma=False,
    )
```

profile of v0, /device:TPU:1, one launch (start us, length us, event | category | flops | bytes accessed | tf_op | source)
XLA Modules:
  0.0 630.4 jit_solution(16017310803679342715)
XLA Ops:
  7.2 0.0 all-gather.2.cloned.1.call-start
  7.2 0.7 all-gather.2.cloned.1.call-update
  7.9 0.0 all-reduce.2.cloned.1.call-start
  8.0 0.7 compare_select_fusion
  8.7 0.1 reshape.26
  8.7 0.1 eq.33
  8.8 87.5 %all-gather.2.cloned.1.call-done = bf16[8192,128]{1,0:T(8,128)(2,1)} async-done(((bf16[512,128]{1,0:T(8,128)(2,1)}), bf16[8192,128]{1,0:T(8,128)(2,1)}) %all-gather.2.cloned.1.call-update) | async-done | bytes 2097168 | tf_op jit(solution)/shard_map/all_gather | solution.py:27
  96.3 2.4 gather_fusion
  98.7 0.4 fusion.7
  99.2 2.4 all_gather.10
  101.6 0.2 fusion.10
  101.9 0.5 fusion.6
  102.4 2.0 all_gather.11
  104.4 0.9 fusion.16
  105.3 0.2 convolution_convert_fusion
  105.5 0.0 reduce-scatter.2.cloned.1.call-start
  105.6 1.8 convolution_bitcast_fusion
  107.4 1.9 copy.10
  109.3 5.2 fusion
  114.6 4.9 reshape.23
  119.5 382.2 %all-reduce.2.cloned.1.call-done = f32[128,256]{1,0:T(8,128)} async-done(((f32[128,256]{1,0:T(8,128)}), f32[128,256]{1,0:T(8,128)}) %all-reduce.2.cloned.1.call-update) | async-done | bytes 131088 | tf_op jit(solution)/shard_map/psum | solution.py:43
  501.7 1.6 broadcast_multiply_fusion
  503.2 119.0 %reduce-scatter.2.cloned.1.call-done = f32[512,128]{1,0:T(8,128)} async-done(((f32[8192,128]{1,0:T(8,128)}), f32[512,128]{1,0:T(8,128)}) %reduce-scatter.2.cloned.1.call-update) | async-done | bytes 262160 | tf_op jit(solution)/shard_map/reduce_scatter | solution.py:62
  622.3 1.6 convert_element_type.25
  (11 shorter events, 0.1 us)
Async XLA Ops:
  7.2 91.6 %copy-start = (bf16[4,8,128,128]{3,2,1,0:T(8,128)(2,1)S(1)}, bf16[4,8,128,128]{3,2,1,0:T(8,128)(2,1)}, u32[]{:S(2)}) copy-start(bf16[4,8,128,128]{3,2,1,0:T(8,128)(2,1)} %param.7) | copy-start | bytes 3145732
  7.2 89.1 %all-gather.2.cloned.1.call-start = ((), (), s32[]{:S(2)}) async-start(), calls=%async_computation.1 | async-start | bytes 2228224 | tf_op jit(solution)/shard_map/all_gather | solution.py:27
  7.9 493.8 %all-reduce.2.cloned.1.call-start = ((), (), s32[]{:S(2)}) async-start(), calls=%async_computation.2 | async-start | bytes 262144 | tf_op jit(solution)/shard_map/psum | solution.py:43
  96.3 5.3 copy-start.1
  98.7 3.1 copy-start.2
  98.7 3.1 copy-start.3
  105.5 516.7 %reduce-scatter.2.cloned.1.call-start = ((), (), s32[]{:S(2)}) async-start(), calls=%async_computation.3 | async-start | bytes 4456448 | tf_op jit(solution)/shard_map/reduce_scatter | solution.py:62
Sparse Core Ops, SparseCore 0:
  12.2 84.0 all-gather.1
  105.7 395.9 all-reduce.1
  507.0 115.1 reduce-scatter.1
where the time goes:
time: 631 us; the launch traced here: 630 us
  waiting for transfers between devices  589 us (93%)
  between operations  13.8 us (2%)
  local copies, waits for them, and re-layouts  9.35 us (1%)
  matrix products  9.32 us (1%)
    psum x1, waiting for transfers between devices, per_device(): lax.psum(partial_weight, ('row', 'col')) / math.sqrt(node_count)  382 us
    reduce_scatter x1, waiting for transfers between devices, per_device(): lax.psum_scatter(partial_grad.reshape(group_blocks * block_size, in_half)...  119 us
    all_gather x1, waiting for transfers between devices, per_device(): gathered = lax.all_gather(features, 'col', axis=0, tiled=True)  87.5 us
  transfers between devices with their start and end apart: 3, of which 3 were waited for; matrix products, arithmetic and copies ran while one was open for 3% of the time, Pallas kernels for 0%

commit v1 on v0

v1 whole, which is shorter than its diff:
```python
import math

import jax
import jax.numpy as jnp
from jax import lax
from jax.experimental import pallas as pl
from jax.experimental.pallas import tpu as pltpu
from jax.sharding import PartitionSpec as P

SIDE = 4


def product_kernel(offset_ref, adj_ref, *rest):
    parts = rest[:-5]
    out_ref, adj_held, panels, adj_sem, part_sems = rest[-5:]
    block_rows, nonzero, block, _ = adj_held.shape
    adj_copy = pltpu.make_async_copy(adj_ref, adj_held, adj_sem)
    adj_copy.start()
    copies = []
    start = 0
    for index, part in enumerate(parts):
        rows = part.shape[0]
        copy = pltpu.make_async_copy(part, panels.at[pl.ds(start, rows)], part_sems.at[index])
        copy.start()
        copies.append(copy)
        start += rows
    adj_copy.wait()
    for copy in copies:
        copy.wait()
    for r in range(block_rows):
        left = jnp.concatenate([adj_held[r, k] for k in range(nonzero)], axis=1)
        right = jnp.concatenate(
            [panels[pl.ds(pl.multiple_of(offset_ref[r, k], block), block), :] for k in range(nonzero)],
            axis=0,
        )
        total = jnp.dot(left, right, preferred_element_type=jnp.float32)
        out_ref[pl.ds(r * block, block), :] = total.astype(out_ref.dtype)


def block_product(offsets, adj, parts):
    block_rows, nonzero, block, _ = adj.shape
    width = parts[0].shape[1]
    held = sum(part.shape[0] for part in parts)
    return pl.pallas_call(
        product_kernel,
        out_shape=jax.ShapeDtypeStruct((block_rows * block, width), jnp.bfloat16),
        in_specs=[pl.BlockSpec(memory_space=pltpu.SMEM)]
        + [pl.BlockSpec(memory_space=pl.ANY)] * (1 + len(parts)),
        out_specs=pl.BlockSpec(memory_space=pltpu.VMEM),
        scratch_shapes=[
            pltpu.VMEM(adj.shape, adj.dtype),
            pltpu.VMEM((held, width), jnp.bfloat16),
            pltpu.SemaphoreType.DMA,
            pltpu.SemaphoreType.DMA((len(parts),)),
        ],
        cost_estimate=pl.CostEstimate(
            flops=2 * block_rows * nonzero * block * block * width,
            bytes_accessed=2 * (adj.size + held * width),
            transcendentals=0,
        ),
        name="block_product",
    )(offsets, adj, *parts)


def middle_kernel(own_ref, other_ref, weight_ref, mine_ref, theirs_ref, partial_ref, back_ref):
    half = own_ref.shape[1]
    own = own_ref[...]
    logits = jnp.dot(own, weight_ref[:half, :], preferred_element_type=jnp.float32)
    logits += jnp.dot(other_ref[...], weight_ref[half:, :], preferred_element_type=jnp.float32)
    target = jnp.concatenate([mine_ref[...], theirs_ref[...]], axis=1).astype(jnp.float32)
    logistic = jax.nn.sigmoid(logits)
    slope = logistic * (1.0 + logits * (1.0 - logistic))
    grad_out = ((logits * logistic - target) * slope).astype(jnp.bfloat16)
    partial_ref[...] = lax.dot_general(
        own, grad_out, (((0,), (0,)), ((), ())), preferred_element_type=jnp.float32
    )
    back_ref[...] = lax.dot_general(
        grad_out, weight_ref[:half, :], (((1,), (1,)), ((), ())), preferred_element_type=jnp.float32
    ).astype(jnp.bfloat16)


def middle(own, other, weight, mine, theirs):
    rows, half = own.shape
    return pl.pallas_call(
        middle_kernel,
        out_shape=(
            jax.ShapeDtypeStruct((half, weight.shape[1]), jnp.float32),
            jax.ShapeDtypeStruct((rows, half), jnp.bfloat16),
        ),
        cost_estimate=pl.CostEstimate(
            flops=2 * rows * weight.size * 2, bytes_accessed=8 * rows * half, transcendentals=rows * weight.shape[1]
        ),
        name="middle",
    )(own, other, weight, mine, theirs)


def from_col(value, dy, dx):
    pairs = []
    for y in range(SIDE):
        for x in range(SIDE):
            pairs.append((((y + dy) % SIDE) * SIDE + (x + dx) % SIDE, y * SIDE + x))
    return lax.ppermute(value, "col", pairs)


def swap_x(value, bits):
    return lax.ppermute(value, "col", [(c, c ^ bits) for c in range(SIDE * SIDE)])


def gather_group(value):
    rows = value.shape[0]
    far = from_col(value, 2, 0)
    column = jnp.concatenate([value, from_col(value, 1, 0), far, from_col(value, 3, 0)], axis=0)
    right = from_col(column, 0, 1)
    left = from_col(column, 0, 3)
    low = from_col(right[: 2 * rows], 0, 1)
    high = from_col(left[2 * rows :], 0, 3)
    return [column, right, low, high, left]


def sum_weight(partial, row_size):
    x = lax.axis_index("col") % SIDE
    first = (x ^ (x >> 1)) & 1
    second = x >> 1
    for bits, bit in ((1, first), (3, second)):
        rows = partial.shape[0] // 2
        kept = lax.dynamic_slice_in_dim(partial, bit * rows, rows, 0)
        sent = lax.dynamic_slice_in_dim(partial, (1 - bit) * rows, rows, 0)
        partial = kept + swap_x(sent, bits)
    for bits in (SIDE, 3 * SIDE):
        partial = partial + swap_x(partial, bits)
    step = 1
    while step < row_size:
        partial = partial + lax.ppermute(partial, "row", [(r, r ^ step) for r in range(row_size)])
        step *= 2
    for bits, bit in ((3, second), (1, first)):
        other = swap_x(partial, bits)
        partial = jnp.where(
            bit == 0,
            jnp.concatenate([partial, other], axis=0),
            jnp.concatenate([other, partial], axis=0),
        )
    return partial


def per_device(features, adj, col_index, weight, centroid, labels):
    block_rows, nonzero, block, _ = adj.shape
    row_count, half = features.shape
    feat = lax.axis_index("feat")
    col = lax.axis_index("col")
    row_size, col_size = lax.axis_size("row"), lax.axis_size("col")
    node_count = row_count * row_size * col_size
    local = col_index % (block_rows * col_size)
    owner = local // block_rows
    down = (owner // SIDE - col // SIDE) % SIDE
    along = (owner % SIDE - col % SIDE) % SIDE
    offsets = ((along * SIDE + down) * block_rows + local % block_rows) * block

    parts = gather_group(features)
    label_table = (
        labels[:, None] == jnp.arange(centroid.shape[0], dtype=jnp.int32)[None, :]
    ).astype(jnp.bfloat16)
    mine = jnp.dot(label_table, centroid, preferred_element_type=jnp.float32).astype(jnp.bfloat16)
    theirs = lax.ppermute(mine, "feat", [(0, 1), (1, 0)])
    swapped = jnp.roll(weight, (half, centroid.shape[1]), (0, 1))
    turned = jnp.where(feat == 0, weight, swapped)

    own = block_product(offsets, adj, parts)
    other = lax.ppermute(own, "feat", [(0, 1), (1, 0)])
    partial, back = middle(own, other, turned, mine, theirs)
    feature_grad = block_product(offsets, adj, gather_group(back))
    total = sum_weight(partial, row_size) * (1.0 / math.sqrt(node_count))
    weight_grad = jnp.where(feat == 0, total, jnp.roll(total, half, 1))
    return (weight_grad, feature_grad)


def solution(mesh):
    placed = (
        P(("row", "col"), "feat"),
        P(("row", "col"), None, None, None),
        P(("row", "col"), None),
        P(),
        P(None, "feat"),
        P(("row", "col")),
    )
    return jax.shard_map(
        per_device,
        mesh=mesh,
        in_specs=placed,
        out_specs=(P("feat", None), P(("row", "col"), "feat")),
        check_vma=False,
    )
```

time: 631 us -> 194 us (0.31)
  the two profiles are of different devices: /device:TPU:1 before, /device:TPU:8 now
where the time goes in v1:
time: 194 us; the launch traced here: 192 us
  starting transfers between devices  120 us (62%)
  waiting for transfers between devices  52.8 us (27%)
  Pallas kernels  9.86 us (5%)
  local copies, waits for them, and re-layouts  5.03 us (3%)
  other arithmetic  2.91 us (2%)
    ppermute x14, starting transfers between devices, from_col(): return lax.ppermute(value, 'col', pairs)  58.2 us
    ppermute x5, starting transfers between devices, sum_weight(): lax.ppermute(partial, 'row', [(r, r ^ step) for r in range(row_size)])  38.1 us
    ppermute x14, waiting for transfers between devices, from_col(): return lax.ppermute(value, 'col', pairs)  29.5 us
    ppermute x6, starting transfers between devices, swap_x(): lax.ppermute(value, 'col', [(c, c ^ bits) for c in range(SIDE * SIDE)])  19.7 us
    ppermute x5, waiting for transfers between devices, sum_weight(): lax.ppermute(partial, 'row', [(r, r ^ step) for r in range(row_size)])  11.5 us
    ppermute x6, waiting for transfers between devices, swap_x(): lax.ppermute(value, 'col', [(c, c ^ bits) for c in range(SIDE * SIDE)])  11 us
    pallas_call x2, Pallas kernels, block_product(): pl.pallas_call(product_kernel, out_shape=jax.ShapeDtypeStruct((block_rows...  7.31 us
    unnamed x40, local copies, waits for them, and re-layouts  4.03 us
  transfers between devices with their start and end apart: 27, of which 17 were waited for; matrix products, arithmetic and copies ran while one was open for 2% of the time, Pallas kernels for 2%

profile of v1, /device:TPU:8, one launch (start us, length us, event | category | flops | bytes accessed | tf_op | source)
XLA Modules:
  0.0 192.4 jit_solution(3199363245976575024)
XLA Ops:
  0.7 5.4 %collective-permute-start = (bf16[512,128]{1,0:T(8,128)(2,1)}, bf16[512,128]{1,0:T(8,128)(2,1)S(1)}, u32[]{:S(2)}, u32[]{:S(2)}) collective-permute-start(bf16[512,128]{1,0:T(8,128)(2,1)} %param.6), channel_id=1, source_target_pairs={{8,0},{10,2},{12,4},{14,6},{16,8},{18,10},{20,12},{22,14},{24,16},... | collective-permute-start | bytes 393224 | tf_op jit(solution)/shard_map/ppermute | solution.py:102
  6.1 4.7 %collective-permute-start.1 = (bf16[512,128]{1,0:T(8,128)(2,1)}, bf16[512,128]{1,0:T(8,128)(2,1)S(1)}, u32[]{:S(2)}, u32[]{:S(2)}) collective-permute-start(bf16[512,128]{1,0:T(8,128)(2,1)} %param.6), channel_id=1, source_target_pairs={{16,0},{18,2},{20,4},{22,6},{24,8},{26,10},{28,12},{30,14},{0,16},... | collective-permute-start | bytes 393224 | tf_op jit(solution)/shard_map/ppermute | solution.py:102
  15.4 6.4 %collective-permute-done.1 = bf16[512,128]{1,0:T(8,128)(2,1)S(1)} collective-permute-done((bf16[512,128]{1,0:T(8,128)(2,1)}, bf16[512,128]{1,0:T(8,128)(2,1)S(1)}, u32[]{:S(2)}, u32[]{:S(2)}) %collective-permute-start.1) | collective-permute-done | bytes 131104 | tf_op jit(solution)/shard_map/ppermute | solution.py:102
  21.8 6.5 %collective-permute-start.3 = (bf16[2048,128]{1,0:T(8,128)(2,1)S(1)}, bf16[2048,128]{1,0:T(8,128)(2,1)S(1)}, u32[]{:S(2)}, u32[]{:S(2)}) collective-permute-start(bf16[2048,128]{1,0:T(8,128)(2,1)S(1)} %constant_dynamic-update-slice_fusion.rest_0_), channel_id=1, source_target_pairs={{2,0},{4,2},{6,4},{0,6},{10,8},{12,10},{14,12},{8,14},{18,16},{20,... | collective-permute-start | bytes 1572872 | tf_op jit(solution)/shard_map/ppermute | solution.py:102
  32.8 6.6 %collective-permute-done.3.rest_1_ = bf16[2048,128]{1,0:T(8,128)(2,1)S(1)} collective-permute-done((bf16[2048,128]{1,0:T(8,128)(2,1)S(1)}, bf16[2048,128]{1,0:T(8,128)(2,1)S(1)}, u32[]{:S(2)}, u32[]{:S(2)}) %collective-permute-start.3) | collective-permute-done | bytes 524320 | tf_op jit(solution)/shard_map/ppermute | solution.py:102
  39.5 5.6 %collective-permute-start.4 = (bf16[1024,128]{1,0:T(8,128)(2,1)S(1)}, bf16[1024,128]{1,0:T(8,128)(2,1)S(1)}, u32[]{:S(2)}, u32[]{:S(2)}) collective-permute-start(bf16[1024,128]{1,0:T(8,128)(2,1)S(1)} %slice.46), channel_id=1, source_target_pairs={{2,0},{4,2},{6,4},{0,6},{10,8},{12,10},{14,12},{8,14},{18,16},{20,... | collective-permute-start | bytes 786440 | tf_op jit(solution)/shard_map/ppermute | solution.py:102
  49.8 5.4 %collective-permute-done.6.rest_3_ = bf16[1024,128]{1,0:T(8,128)(2,1)S(1)} collective-permute-done((bf16[1024,128]{1,0:T(8,128)(2,1)S(1)}, bf16[1024,128]{1,0:T(8,128)(2,1)S(1)}, u32[]{:S(2)}, u32[]{:S(2)}) %collective-permute-start.6) | collective-permute-done | bytes 262176 | tf_op jit(solution)/shard_map/ppermute | solution.py:102
  69.0 4.3 %collective-permute-done.9 = f32[64,256]{1,0:T(8,128)S(1)} collective-permute-done((f32[64,256]{1,0:T(8,128)S(1)}, f32[64,256]{1,0:T(8,128)S(1)}, u32[]{:S(2)}, u32[]{:S(2)}) %collective-permute-start.9) | collective-permute-done | bytes 65568 | tf_op jit(solution)/shard_map/ppermute | solution.py:106
  77.0 5.5 %collective-permute-start.20 = (bf16[512,128]{1,0:T(8,128)(2,1)}, bf16[512,128]{1,0:T(8,128)(2,1)S(1)}, u32[]{:S(2)}, u32[]{:S(2)}) collective-permute-start(bf16[512,128]{1,0:T(8,128)(2,1)} %get-tuple-element.5), channel_id=1, source_target_pairs={{8,0},{10,2},{12,4},{14,6},{16,8},{18,10},{20,12},{22,14},{24,16},... | collective-permute-start | bytes 393224 | tf_op jit(solution)/shard_map/ppermute | solution.py:102
  82.5 3.8 %collective-permute-start.21 = (bf16[512,128]{1,0:T(8,128)(2,1)}, bf16[512,128]{1,0:T(8,128)(2,1)S(1)}, u32[]{:S(2)}, u32[]{:S(2)}) collective-permute-start(bf16[512,128]{1,0:T(8,128)(2,1)} %get-tuple-element.5), channel_id=1, source_target_pairs={{16,0},{18,2},{20,4},{22,6},{24,8},{26,10},{28,12},{30,14},{0,16},... | collective-permute-start | bytes 393224 | tf_op jit(solution)/shard_map/ppermute | solution.py:102
  86.3 4.4 %collective-permute-start.22 = (bf16[512,128]{1,0:T(8,128)(2,1)}, bf16[512,128]{1,0:T(8,128)(2,1)S(1)}, u32[]{:S(2)}, u32[]{:S(2)}) collective-permute-start(bf16[512,128]{1,0:T(8,128)(2,1)} %get-tuple-element.5), channel_id=1, source_target_pairs={{24,0},{26,2},{28,4},{30,6},{0,8},{2,10},{4,12},{6,14},{8,16},{10,... | collective-permute-start | bytes 393224 | tf_op jit(solution)/shard_map/ppermute | solution.py:102
  90.7 4.0 %collective-permute-start.11 = (f32[32,256]{1,0:T(8,128)S(1)}, f32[32,256]{1,0:T(8,128)S(1)}, u32[]{:S(2)}, u32[]{:S(2)}) collective-permute-start(f32[32,256]{1,0:T(8,128)S(1)} %dynamic-slice_add_fusion.1), channel_id=1, source_target_pairs={{0,8},{2,10},{4,12},{6,14},{8,0},{10,2},{12,4},{14,6},{16,24},{18,... | collective-permute-start | bytes 98312 | tf_op jit(solution)/shard_map/ppermute | solution.py:106
  97.7 4.7 %collective-permute-start.12 = (f32[32,256]{1,0:T(8,128)S(1)}, f32[32,256]{1,0:T(8,128)S(1)}, u32[]{:S(2)}, u32[]{:S(2)}) collective-permute-start(f32[32,256]{1,0:T(8,128)S(1)} %add.89), channel_id=1, source_target_pairs={{0,24},{2,26},{4,28},{6,30},{8,16},{10,18},{12,20},{14,22},{16,8},... | collective-permute-start | bytes 98312 | tf_op jit(solution)/shard_map/ppermute | solution.py:106
  102.5 5.2 %collective-permute-start.23 = (bf16[2048,128]{1,0:T(8,128)(2,1)S(1)}, bf16[2048,128]{1,0:T(8,128)(2,1)S(1)}, u32[]{:S(2)}, u32[]{:S(2)}) collective-permute-start(bf16[2048,128]{1,0:T(8,128)(2,1)S(1)} %constant_dynamic-update-slice_fusion.4.rest_0_), channel_id=1, source_target_pairs={{2,0},{4,2},{6,4},{0,6},{10,8},{12,10},{14,12},{8,14},{18,16},{20,... | collective-permute-start | bytes 1572872 | tf_op jit(solution)/shard_map/ppermute | solution.py:102
  111.6 3.9 %collective-permute-done.13 = f32[32,256]{1,0:T(8,128)S(1)} collective-permute-done((f32[32,256]{1,0:T(8,128)S(1)}, f32[32,256]{1,0:T(8,128)S(1)}, u32[]{:S(2)}, u32[]{:S(2)}) %collective-permute-start.13) | collective-permute-done | bytes 32800 | tf_op jit(solution)/shard_map/ppermute | solution.py:133
  115.5 4.6 %collective-permute-start.14 = (f32[32,256]{1,0:T(8,128)S(1)}, f32[32,256]{1,0:T(8,128)S(1)}, u32[]{:S(2)}, u32[]{:S(2)}) collective-permute-start(f32[32,256]{1,0:T(8,128)S(1)} %add.91), channel_id=1, source_target_pairs={{0,64},{32,96},{64,0},{96,32},{128,192},{160,224},{192,128},{224,1... | collective-permute-start | bytes 98312 | tf_op jit(solution)/shard_map/ppermute | solution.py:133
  121.9 6.1 %collective-permute-start.15 = (f32[32,256]{1,0:T(8,128)S(1)}, f32[32,256]{1,0:T(8,128)S(1)}, u32[]{:S(2)}, u32[]{:S(2)}) collective-permute-start(f32[32,256]{1,0:T(8,128)S(1)} %add.92), channel_id=1, source_target_pairs={{0,128},{32,160},{64,192},{96,224},{128,0},{160,32},{192,64},{224,... | collective-permute-start | bytes 98312 | tf_op jit(solution)/shard_map/ppermute | solution.py:133
  129.9 10.9 %collective-permute-start.16 = (f32[32,256]{1,0:T(8,128)S(1)}, f32[32,256]{1,0:T(8,128)S(1)}, u32[]{:S(2)}, u32[]{:S(2)}) collective-permute-start(f32[32,256]{1,0:T(8,128)S(1)} %add.93), channel_id=1, source_target_pairs={{0,256},{32,288},{64,320},{96,352},{128,384},{160,416},{192,448},{... | collective-permute-start | bytes 98312 | tf_op jit(solution)/shard_map/ppermute | solution.py:133
  142.7 14.6 %collective-permute-start.17 = (f32[32,256]{1,0:T(8,128)S(1)}, f32[32,256]{1,0:T(8,128)S(1)}, u32[]{:S(2)}, u32[]{:S(2)}) collective-permute-start(f32[32,256]{1,0:T(8,128)S(1)} %add.94), channel_id=1, source_target_pairs={{0,512},{32,544},{64,576},{96,608},{128,640},{160,672},{192,704},{... | collective-permute-start | bytes 98312 | tf_op jit(solution)/shard_map/ppermute | solution.py:133
  159.3 5.2 %collective-permute-start.18 = (f32[32,256]{1,0:T(8,128)S(1)}, f32[32,256]{1,0:T(8,128)S(1)}, u32[]{:S(2)}, u32[]{:S(2)}) collective-permute-start(f32[32,256]{1,0:T(8,128)S(1)} %add.95), channel_id=1, source_target_pairs={{0,6},{2,4},{4,2},{6,0},{8,14},{10,12},{12,10},{14,8},{16,22},{18,... | collective-permute-start | bytes 98312 | tf_op jit(solution)/shard_map/ppermute | solution.py:106
  168.3 4.2 %collective-permute-done.19 = f32[64,256]{1,0:T(8,128)S(1)} collective-permute-done((f32[64,256]{1,0:T(8,128)S(1)}, f32[64,256]{1,0:T(8,128)S(1)}, u32[]{:S(2)}, u32[]{:S(2)}) %collective-permute-start.19) | collective-permute-done | bytes 65568 | tf_op jit(solution)/shard_map/ppermute | solution.py:106
  172.6 5.9 %collective-permute-start.24 = (bf16[1024,128]{1,0:T(8,128)(2,1)S(1)}, bf16[1024,128]{1,0:T(8,128)(2,1)S(1)}, u32[]{:S(2)}, u32[]{:S(2)}) collective-permute-start(bf16[1024,128]{1,0:T(8,128)(2,1)S(1)} %slice.52), channel_id=1, source_target_pairs={{2,0},{4,2},{6,4},{0,6},{10,8},{12,10},{14,12},{8,14},{18,16},{20,... | collective-permute-start | bytes 786440 | tf_op jit(solution)/shard_map/ppermute | solution.py:102
  182.3 5.7 %collective-permute-done.26.rest_3_ = bf16[1024,128]{1,0:T(8,128)(2,1)S(1)} collective-permute-done((bf16[1024,128]{1,0:T(8,128)(2,1)S(1)}, bf16[1024,128]{1,0:T(8,128)(2,1)S(1)}, u32[]{:S(2)}, u32[]{:S(2)}) %collective-permute-start.26) | collective-permute-done | bytes 262176 | tf_op jit(solution)/shard_map/ppermute | solution.py:102
  188.7 3.7 %block_product.3 = bf16[512,128]{1,0:T(8,128)(2,1)} custom-call(s32[4,8]{1,0:T(4,128)} %fusion.14.offset_ref, bf16[4,8,128,128]{3,2,1,0:T(8,128)(2,1)} %adj_ref.3, bf16[2048,128]{1,0:T(8,128)(2,1)} %copy-done.5, bf16[2048,128]{1,0:T(8,128)(2,1)} %copy-done.1, bf16[1024,128]{1,0:T(8,128)(2,1)} %copy-done.10, bf16[1024,128]{1,0:T(8,128)(2,1)} %copy-done.11, ...), custom_call_target="tpu_custom_call" | custom-call | flops 134217728 | bytes 3145728 | tf_op jit(solution)/shard_map/block_product/pallas_call | solution.py:44
  (99 shorter events, 54.0 us)
Async XLA Ops:
  0.7 14.7 %collective-permute-start = (bf16[512,128]{1,0:T(8,128)(2,1)}, bf16[512,128]{1,0:T(8,128)(2,1)S(1)}, u32[]{:S(2)}, u32[]{:S(2)}) collective-permute-start(bf16[512,128]{1,0:T(8,128)(2,1)} %param.6), channel_id=1, source_target_pairs={{8,0},{10,2},{12,4},{14,6},{16,8},{18,10},{20,12},{22,14},{24,16},... | collective-permute-start | bytes 393224 | tf_op jit(solution)/shard_map/ppermute | solution.py:102
  6.1 15.6 %collective-permute-start.1 = (bf16[512,128]{1,0:T(8,128)(2,1)}, bf16[512,128]{1,0:T(8,128)(2,1)S(1)}, u32[]{:S(2)}, u32[]{:S(2)}) collective-permute-start(bf16[512,128]{1,0:T(8,128)(2,1)} %param.6), channel_id=1, source_target_pairs={{16,0},{18,2},{20,4},{22,6},{24,8},{26,10},{28,12},{30,14},{0,16},... | collective-permute-start | bytes 393224 | tf_op jit(solution)/shard_map/ppermute | solution.py:102
  10.8 10.9 %collective-permute-start.2 = (bf16[512,128]{1,0:T(8,128)(2,1)}, bf16[512,128]{1,0:T(8,128)(2,1)S(1)}, u32[]{:S(2)}, u32[]{:S(2)}) collective-permute-start(bf16[512,128]{1,0:T(8,128)(2,1)} %param.6), channel_id=1, source_target_pairs={{24,0},{26,2},{28,4},{30,6},{0,8},{2,10},{4,12},{6,14},{8,16},{10,... | collective-permute-start | bytes 393224 | tf_op jit(solution)/shard_map/ppermute | solution.py:102
  21.8 17.7 %collective-permute-start.3 = (bf16[2048,128]{1,0:T(8,128)(2,1)S(1)}, bf16[2048,128]{1,0:T(8,128)(2,1)S(1)}, u32[]{:S(2)}, u32[]{:S(2)}) collective-permute-start(bf16[2048,128]{1,0:T(8,128)(2,1)S(1)} %constant_dynamic-update-slice_fusion.rest_0_), channel_id=1, source_target_pairs={{2,0},{4,2},{6,4},{0,6},{10,8},{12,10},{14,12},{8,14},{18,16},{20,... | collective-permute-start | bytes 1572872 | tf_op jit(solution)/shard_map/ppermute | solution.py:102
  28.2 16.8 %collective-permute-start.5 = (bf16[2048,128]{1,0:T(8,128)(2,1)S(1)}, bf16[2048,128]{1,0:T(8,128)(2,1)S(1)}, u32[]{:S(2)}, u32[]{:S(2)}) collective-permute-start(bf16[2048,128]{1,0:T(8,128)(2,1)S(1)} %constant_dynamic-update-slice_fusion.rest_0_), channel_id=1, source_target_pairs={{6,0},{0,2},{2,4},{4,6},{14,8},{8,10},{10,12},{12,14},{22,16},{16,... | collective-permute-start | bytes 1572872 | tf_op jit(solution)/shard_map/ppermute | solution.py:102
  30.7 31.4 %collective-permute-start.8 = (bf16[512,128]{1,0:T(8,128)(2,1)S(1)}, bf16[512,128]{1,0:T(8,128)(2,1)S(1)}, u32[]{:S(2)}, u32[]{:S(2)}) collective-permute-start(bf16[512,128]{1,0:T(8,128)(2,1)S(1)} %fusion.1.mine_ref), channel_id=1, source_target_pairs={{0,1},{1,0},{2,3},{3,2},{4,5},{5,4},{6,7},{7,6},{8,9},{9,8},{10,11... | collective-permute-start | bytes 393224 | tf_op jit(solution)/shard_map/ppermute | solution.py:163
  39.5 10.3 %collective-permute-start.4 = (bf16[1024,128]{1,0:T(8,128)(2,1)S(1)}, bf16[1024,128]{1,0:T(8,128)(2,1)S(1)}, u32[]{:S(2)}, u32[]{:S(2)}) collective-permute-start(bf16[1024,128]{1,0:T(8,128)(2,1)S(1)} %slice.46), channel_id=1, source_target_pairs={{2,0},{4,2},{6,4},{0,6},{10,8},{12,10},{14,12},{8,14},{18,16},{20,... | collective-permute-start | bytes 786440 | tf_op jit(solution)/shard_map/ppermute | solution.py:102
  45.1 10.0 %collective-permute-start.6 = (bf16[1024,128]{1,0:T(8,128)(2,1)S(1)}, bf16[1024,128]{1,0:T(8,128)(2,1)S(1)}, u32[]{:S(2)}, u32[]{:S(2)}) collective-permute-start(bf16[1024,128]{1,0:T(8,128)(2,1)S(1)} %slice.47), channel_id=1, source_target_pairs={{6,0},{0,2},{2,4},{4,6},{14,8},{8,10},{10,12},{12,14},{22,16},{16,... | collective-permute-start | bytes 786440 | tf_op jit(solution)/shard_map/ppermute | solution.py:102
  67.1 6.2 %collective-permute-start.9 = (f32[64,256]{1,0:T(8,128)S(1)}, f32[64,256]{1,0:T(8,128)S(1)}, u32[]{:S(2)}, u32[]{:S(2)}) collective-permute-start(f32[64,256]{1,0:T(8,128)S(1)} %constant_dynamic-slice_fusion.1), channel_id=1, source_target_pairs={{0,2},{2,0},{4,6},{6,4},{8,10},{10,8},{12,14},{14,12},{16,18},{18,... | collective-permute-start | bytes 196616 | tf_op jit(solution)/shard_map/ppermute | solution.py:106
  74.1 16.6 %collective-permute-start.10 = (f32[32,256]{1,0:T(8,128)S(1)}, f32[32,256]{1,0:T(8,128)S(1)}, u32[]{:S(2)}, u32[]{:S(2)}) collective-permute-start(f32[32,256]{1,0:T(8,128)S(1)} %constant_dynamic-slice_fusion), channel_id=1, source_target_pairs={{0,6},{2,4},{4,2},{6,0},{8,14},{10,12},{12,10},{14,8},{16,22},{18,... | collective-permute-start | bytes 98312 | tf_op jit(solution)/shard_map/ppermute | solution.py:106
  77.0 17.8 %collective-permute-start.20 = (bf16[512,128]{1,0:T(8,128)(2,1)}, bf16[512,128]{1,0:T(8,128)(2,1)S(1)}, u32[]{:S(2)}, u32[]{:S(2)}) collective-permute-start(bf16[512,128]{1,0:T(8,128)(2,1)} %get-tuple-element.5), channel_id=1, source_target_pairs={{8,0},{10,2},{12,4},{14,6},{16,8},{18,10},{20,12},{22,14},{24,16},... | collective-permute-start | bytes 393224 | tf_op jit(solution)/shard_map/ppermute | solution.py:102
  82.5 14.5 %collective-permute-start.21 = (bf16[512,128]{1,0:T(8,128)(2,1)}, bf16[512,128]{1,0:T(8,128)(2,1)S(1)}, u32[]{:S(2)}, u32[]{:S(2)}) collective-permute-start(bf16[512,128]{1,0:T(8,128)(2,1)} %get-tuple-element.5), channel_id=1, source_target_pairs={{16,0},{18,2},{20,4},{22,6},{24,8},{26,10},{28,12},{30,14},{0,16},... | collective-permute-start | bytes 393224 | tf_op jit(solution)/shard_map/ppermute | solution.py:102
  86.3 16.2 %collective-permute-start.22 = (bf16[512,128]{1,0:T(8,128)(2,1)}, bf16[512,128]{1,0:T(8,128)(2,1)S(1)}, u32[]{:S(2)}, u32[]{:S(2)}) collective-permute-start(bf16[512,128]{1,0:T(8,128)(2,1)} %get-tuple-element.5), channel_id=1, source_target_pairs={{24,0},{26,2},{28,4},{30,6},{0,8},{2,10},{4,12},{6,14},{8,16},{10,... | collective-permute-start | bytes 393224 | tf_op jit(solution)/shard_map/ppermute | solution.py:102
  90.7 7.0 %collective-permute-start.11 = (f32[32,256]{1,0:T(8,128)S(1)}, f32[32,256]{1,0:T(8,128)S(1)}, u32[]{:S(2)}, u32[]{:S(2)}) collective-permute-start(f32[32,256]{1,0:T(8,128)S(1)} %dynamic-slice_add_fusion.1), channel_id=1, source_target_pairs={{0,8},{2,10},{4,12},{6,14},{8,0},{10,2},{12,4},{14,6},{16,24},{18,... | collective-permute-start | bytes 98312 | tf_op jit(solution)/shard_map/ppermute | solution.py:106
  97.7 11.9 %collective-permute-start.12 = (f32[32,256]{1,0:T(8,128)S(1)}, f32[32,256]{1,0:T(8,128)S(1)}, u32[]{:S(2)}, u32[]{:S(2)}) collective-permute-start(f32[32,256]{1,0:T(8,128)S(1)} %add.89), channel_id=1, source_target_pairs={{0,24},{2,26},{4,28},{6,30},{8,16},{10,18},{12,20},{14,22},{16,8},... | collective-permute-start | bytes 98312 | tf_op jit(solution)/shard_map/ppermute | solution.py:106
  102.5 70.1 %collective-permute-start.23 = (bf16[2048,128]{1,0:T(8,128)(2,1)S(1)}, bf16[2048,128]{1,0:T(8,128)(2,1)S(1)}, u32[]{:S(2)}, u32[]{:S(2)}) collective-permute-start(bf16[2048,128]{1,0:T(8,128)(2,1)S(1)} %constant_dynamic-update-slice_fusion.4.rest_0_), channel_id=1, source_target_pairs={{2,0},{4,2},{6,4},{0,6},{10,8},{12,10},{14,12},{8,14},{18,16},{20,... | collective-permute-start | bytes 1572872 | tf_op jit(solution)/shard_map/ppermute | solution.py:102
  107.7 70.8 %collective-permute-start.25 = (bf16[2048,128]{1,0:T(8,128)(2,1)S(1)}, bf16[2048,128]{1,0:T(8,128)(2,1)S(1)}, u32[]{:S(2)}, u32[]{:S(2)}) collective-permute-start(bf16[2048,128]{1,0:T(8,128)(2,1)S(1)} %constant_dynamic-update-slice_fusion.4.rest_0_), channel_id=1, source_target_pairs={{6,0},{0,2},{2,4},{4,6},{14,8},{8,10},{10,12},{12,14},{22,16},{16,... | collective-permute-start | bytes 1572872 | tf_op jit(solution)/shard_map/ppermute | solution.py:102
  115.5 6.5 %collective-permute-start.14 = (f32[32,256]{1,0:T(8,128)S(1)}, f32[32,256]{1,0:T(8,128)S(1)}, u32[]{:S(2)}, u32[]{:S(2)}) collective-permute-start(f32[32,256]{1,0:T(8,128)S(1)} %add.91), channel_id=1, source_target_pairs={{0,64},{32,96},{64,0},{96,32},{128,192},{160,224},{192,128},{224,1... | collective-permute-start | bytes 98312 | tf_op jit(solution)/shard_map/ppermute | solution.py:133
  121.9 8.0 %collective-permute-start.15 = (f32[32,256]{1,0:T(8,128)S(1)}, f32[32,256]{1,0:T(8,128)S(1)}, u32[]{:S(2)}, u32[]{:S(2)}) collective-permute-start(f32[32,256]{1,0:T(8,128)S(1)} %add.92), channel_id=1, source_target_pairs={{0,128},{32,160},{64,192},{96,224},{128,0},{160,32},{192,64},{224,... | collective-permute-start | bytes 98312 | tf_op jit(solution)/shard_map/ppermute | solution.py:133
  129.9 12.8 %collective-permute-start.16 = (f32[32,256]{1,0:T(8,128)S(1)}, f32[32,256]{1,0:T(8,128)S(1)}, u32[]{:S(2)}, u32[]{:S(2)}) collective-permute-start(f32[32,256]{1,0:T(8,128)S(1)} %add.93), channel_id=1, source_target_pairs={{0,256},{32,288},{64,320},{96,352},{128,384},{160,416},{192,448},{... | collective-permute-start | bytes 98312 | tf_op jit(solution)/shard_map/ppermute | solution.py:133
  142.7 16.6 %collective-permute-start.17 = (f32[32,256]{1,0:T(8,128)S(1)}, f32[32,256]{1,0:T(8,128)S(1)}, u32[]{:S(2)}, u32[]{:S(2)}) collective-permute-start(f32[32,256]{1,0:T(8,128)S(1)} %add.94), channel_id=1, source_target_pairs={{0,512},{32,544},{64,576},{96,608},{128,640},{160,672},{192,704},{... | collective-permute-start | bytes 98312 | tf_op jit(solution)/shard_map/ppermute | solution.py:133
  159.3 7.1 %collective-permute-start.18 = (f32[32,256]{1,0:T(8,128)S(1)}, f32[32,256]{1,0:T(8,128)S(1)}, u32[]{:S(2)}, u32[]{:S(2)}) collective-permute-start(f32[32,256]{1,0:T(8,128)S(1)} %add.95), channel_id=1, source_target_pairs={{0,6},{2,4},{4,2},{6,0},{8,14},{10,12},{12,10},{14,8},{16,22},{18,... | collective-permute-start | bytes 98312 | tf_op jit(solution)/shard_map/ppermute | solution.py:106
  172.6 9.7 %collective-permute-start.24 = (bf16[1024,128]{1,0:T(8,128)(2,1)S(1)}, bf16[1024,128]{1,0:T(8,128)(2,1)S(1)}, u32[]{:S(2)}, u32[]{:S(2)}) collective-permute-start(bf16[1024,128]{1,0:T(8,128)(2,1)S(1)} %slice.52), channel_id=1, source_target_pairs={{2,0},{4,2},{6,4},{0,6},{10,8},{12,10},{14,12},{8,14},{18,16},{20,... | collective-permute-start | bytes 786440 | tf_op jit(solution)/shard_map/ppermute | solution.py:102
  178.5 9.5 %collective-permute-start.26 = (bf16[1024,128]{1,0:T(8,128)(2,1)S(1)}, bf16[1024,128]{1,0:T(8,128)(2,1)S(1)}, u32[]{:S(2)}, u32[]{:S(2)}) collective-permute-start(bf16[1024,128]{1,0:T(8,128)(2,1)S(1)} %slice.53), channel_id=1, source_target_pairs={{6,0},{0,2},{2,4},{4,6},{14,8},{8,10},{10,12},{12,14},{22,16},{16,... | collective-permute-start | bytes 786440 | tf_op jit(solution)/shard_map/ppermute | solution.py:102
  (20 other events, 317.9 us)

commit v2 on v1

v2 whole, which is shorter than its diff:
```python
import math

import jax
import jax.numpy as jnp
from jax import lax
from jax.experimental import pallas as pl
from jax.experimental.pallas import tpu as pltpu
from jax.sharding import PartitionSpec as P

SIDE = 4


def product_kernel(offset_ref, adj_ref, panel_ref, *rest):
    out_ref, adj_held, held, adj_sems, panel_sems = rest[-5:]
    block_rows, nonzero, block, _ = adj_held.shape

    def fetch(r, k):
        start = pl.multiple_of(offset_ref[r, k], block)
        return pltpu.make_async_copy(
            panel_ref.at[pl.ds(start, block)], held.at[r, pl.ds(k * block, block)], panel_sems.at[r, k]
        )

    adj_copies = []
    for r in range(block_rows):
        copy = pltpu.make_async_copy(adj_ref.at[r], adj_held.at[r], adj_sems.at[r])
        copy.start()
        adj_copies.append(copy)
        for k in range(nonzero):
            fetch(r, k).start()
    if len(rest) == 6:
        out_ref[pl.ds(block_rows * block, rest[0].shape[0]), :] = rest[0][...]
    for r in range(block_rows):
        adj_copies[r].wait()
        for k in range(nonzero):
            fetch(r, k).wait()
        left = jnp.concatenate([adj_held[r, k] for k in range(nonzero)], axis=1)
        total = jnp.dot(left, held[r], preferred_element_type=jnp.float32)
        out_ref[pl.ds(r * block, block), :] = total.astype(out_ref.dtype)


def block_product(offsets, adj, panels, carried=(), place=pl.ANY):
    block_rows, nonzero, block, _ = adj.shape
    width = panels.shape[1]
    rows = block_rows * block + sum(array.shape[0] for array in carried)
    return pl.pallas_call(
        product_kernel,
        out_shape=jax.ShapeDtypeStruct((rows, width), jnp.bfloat16),
        in_specs=[
            pl.BlockSpec(memory_space=pltpu.SMEM),
            pl.BlockSpec(memory_space=pl.ANY),
            pl.BlockSpec(memory_space=place),
        ]
        + [pl.BlockSpec(memory_space=pltpu.VMEM)] * len(carried),
        out_specs=pl.BlockSpec(memory_space=pltpu.VMEM),
        scratch_shapes=[
            pltpu.VMEM(adj.shape, adj.dtype),
            pltpu.VMEM((block_rows, nonzero * block, width), jnp.bfloat16),
            pltpu.SemaphoreType.DMA((block_rows,)),
            pltpu.SemaphoreType.DMA((block_rows, nonzero)),
        ],
        compiler_params=pltpu.CompilerParams(vmem_limit_bytes=12 << 20),
        cost_estimate=pl.CostEstimate(
            flops=2 * block_rows * nonzero * block * block * width,
            bytes_accessed=2 * (adj.size + block_rows * nonzero * block * width),
            transcendentals=0,
        ),
        name="block_product",
    )(offsets, adj, panels, *carried)


def middle_kernel(here_ref, there_ref, weight_ref, partial_ref, back_ref):
    rows, half = back_ref.shape
    own = here_ref[:rows, :]
    logits = jnp.dot(own, weight_ref[:half, :], preferred_element_type=jnp.float32)
    logits += jnp.dot(there_ref[:rows, :], weight_ref[half:, :], preferred_element_type=jnp.float32)
    target = jnp.concatenate([here_ref[rows:, :], there_ref[rows:, :]], axis=1).astype(jnp.float32)
    logistic = jax.nn.sigmoid(logits)
    slope = logistic * (1.0 + logits * (1.0 - logistic))
    grad_out = ((logits * logistic - target) * slope).astype(jnp.bfloat16)
    back_ref[...] = lax.dot_general(
        grad_out, weight_ref[:half, :], (((1,), (1,)), ((), ())), preferred_element_type=jnp.float32
    ).astype(jnp.bfloat16)
    partial_ref[...] = lax.dot_general(
        own, grad_out, (((0,), (0,)), ((), ())), preferred_element_type=jnp.float32
    )


def middle(here, there, weight):
    rows, half = here.shape[0] // 2, here.shape[1]
    return pl.pallas_call(
        middle_kernel,
        out_shape=(
            jax.ShapeDtypeStruct((half, weight.shape[1]), jnp.float32),
            jax.ShapeDtypeStruct((rows, half), jnp.bfloat16),
        ),
        compiler_params=pltpu.CompilerParams(vmem_limit_bytes=12 << 20),
        cost_estimate=pl.CostEstimate(
            flops=4 * rows * weight.size, bytes_accessed=12 * rows * half, transcendentals=rows * weight.shape[1]
        ),
        name="middle",
    )(here, there, weight)


def to_all(value, axis, count, groups=None):
    copies = jnp.broadcast_to(value[None], (count, *value.shape))
    return lax.all_to_all(copies, axis, 0, 0, axis_index_groups=groups)


def gather_group(value):
    along_y = [[y * SIDE + x for y in range(SIDE)] for x in range(SIDE)]
    along_x = [[y * SIDE + x for x in range(SIDE)] for y in range(SIDE)]
    column = to_all(value, "col", SIDE, along_y).reshape(-1, value.shape[1])
    return to_all(column, "col", SIDE, along_x).reshape(-1, value.shape[1])


def sum_weight(partial, row_size, col_size):
    rows, width = partial.shape
    pieces = lax.all_to_all(partial.reshape(col_size, rows // col_size, width), "col", 0, 0)
    piece = to_all(pieces.sum(0), "row", row_size).sum(0)
    return to_all(piece, "col", col_size).reshape(rows, width)


def per_device(features, adj, col_index, weight, centroid, labels):
    block_rows, nonzero, block, _ = adj.shape
    row_count, half = features.shape
    feat = lax.axis_index("feat")
    row_size, col_size = lax.axis_size("row"), lax.axis_size("col")
    node_count = row_count * row_size * col_size
    local = col_index % (block_rows * col_size)
    owner = local // block_rows
    turned_offsets = (((owner % SIDE) * SIDE + owner // SIDE) * block_rows + local % block_rows) * block

    label_table = (
        labels[:, None] == jnp.arange(centroid.shape[0], dtype=jnp.int32)[None, :]
    ).astype(jnp.bfloat16)
    target = jnp.dot(label_table, centroid, preferred_element_type=jnp.float32).astype(jnp.bfloat16)
    swapped = jnp.roll(weight, (half, centroid.shape[1]), (0, 1))
    turned = jnp.where(feat == 0, weight, swapped)

    here = block_product(turned_offsets, adj, gather_group(features), (target,))
    there = lax.ppermute(here, "feat", [(0, 1), (1, 0)])
    partial, back = middle(here, there, turned)
    gathered = lax.all_gather(back, "col", axis=0, tiled=True)
    feature_grad = block_product(local * block, adj, gathered, place=pltpu.HBM)
    total = sum_weight(partial, row_size, col_size) * (1.0 / math.sqrt(node_count))
    weight_grad = jnp.where(feat == 0, total, jnp.roll(total, half, 1))
    return (weight_grad, feature_grad)


def solution(mesh):
    placed = (
        P(("row", "col"), "feat"),
        P(("row", "col"), None, None, None),
        P(("row", "col"), None),
        P(),
        P(None, "feat"),
        P(("row", "col")),
    )
    return jax.shard_map(
        per_device,
        mesh=mesh,
        in_specs=placed,
        out_specs=(P("feat", None), P(("row", "col"), "feat")),
        check_vma=False,
    )
```

time: 194 us -> 166 us (0.86)
  the two profiles are of different devices: /device:TPU:8 before, /device:TPU:1 now
where the time goes in v2:
time: 166 us; the launch traced here: 165 us
  blocking collectives  83.4 us (50%)
  waiting for transfers between devices  35 us (21%)
  starting transfers between devices  15.4 us (9%)
  between operations  14.2 us (9%)
  Pallas kernels  10.3 us (6%)
  local copies, waits for them, and re-layouts  4.94 us (3%)
    all_to_all x3, blocking collectives, to_all(): return lax.all_to_all(copies, axis, 0, 0, axis_index_groups=groups)  69.6 us
    all_to_all x1, waiting for transfers between devices, to_all(): return lax.all_to_all(copies, axis, 0, 0, axis_index_groups=groups)  19.4 us
    all_gather x1, waiting for transfers between devices, per_device(): gathered = lax.all_gather(back, 'col', axis=0, tiled=True)  15.1 us
    all_to_all x1, blocking collectives, sum_weight(): lax.all_to_all(partial.reshape(col_size, rows // col_size, width), 'col',...  13.8 us
    ppermute x1, starting transfers between devices, per_device(): there = lax.ppermute(here, 'feat', [(0, 1), (1, 0)])  8.54 us
    pallas_call x2, Pallas kernels, block_product(): pl.pallas_call(product_kernel, out_shape=jax.ShapeDtypeStruct((rows, widt...  8.13 us
    all_to_all x1, starting transfers between devices, to_all(): return lax.all_to_all(copies, axis, 0, 0, axis_index_groups=groups)  6.88 us
  transfers between devices with their start and end apart: 3, of which 3 were waited for; matrix products, arithmetic and copies ran while one was open for 2% of the time, Pallas kernels for 0%

profile of v2, /device:TPU:1, one launch (start us, length us, event | category | flops | bytes accessed | tf_op | source)
XLA Modules:
  0.0 165.3 jit_solution(14768759662599034131)
XLA Ops:
  7.2 0.0 copy-start
  7.2 1.0 broadcast_in_dim.10
  8.2 19.9 %all_to_all.25 = bf16[4,512,128]{2,1,0:T(8,128)(2,1)S(1)} all-to-all(bf16[4,512,128]{2,1,0:T(8,128)(2,1)S(1)} %broadcast_in_dim.10), channel_id=1, replica_groups={{0,8,16,24},{2,10,18,26},{4,12,20,28},{6,14,22,30},{1,9,17,25},{3,11,19..., dimensions={0} | all-to-all | bytes 1048576 | tf_op jit(solution)/shard_map/all_to_all | solution.py:106
  28.1 1.6 broadcast_in_dim.12
  29.7 6.9 %all-to-all-start.1 = ((bf16[4,2048,128]{2,1,0:T(8,128)(2,1)}), bf16[4,2048,128]{2,1,0:T(8,128)(2,1)S(1)}, u32[]{:S(2)}, u32[]{:S(2)}) async-start(bf16[4,2048,128]{2,1,0:T(8,128)(2,1)} %broadcast_in_dim.12), calls=%async_computation.1 | async-start | bytes 4194304 | tf_op jit(solution)/shard_map/all_to_all | solution.py:106
  36.5 0.0 all-gather.2.cloned.1.call-start
  36.6 0.0 copy-done.6
  36.6 0.7 fusion.16
  37.3 0.0 copy-done.7
  37.3 0.5 fusion.1.rest_0_
  37.8 19.4 %all-to-all-done.1 = bf16[4,2048,128]{2,1,0:T(8,128)(2,1)S(1)} async-done(((bf16[4,2048,128]{2,1,0:T(8,128)(2,1)}), bf16[4,2048,128]{2,1,0:T(8,128)(2,1)S(1)}, u32[]{:S(2)}, u32[]{:S(2)}) %all-to-all-start.1) | async-done | bytes 2097184 | tf_op jit(solution)/shard_map/all_to_all | solution.py:106
  57.2 4.1 %block_product.2.here_ref = bf16[1024,128]{1,0:T(8,128)(2,1)} custom-call(s32[4,8]{1,0:T(4,128)S(1)} %get-tuple-element.11.offset_ref, bf16[4,8,128,128]{3,2,1,0:T(8,128)(2,1)S(1)} %copy-done.1, bf16[8192,128]{1,0:T(8,128)(2,1)S(1)} %bitcast.8, bf16[512,128]{1,0:T(8,128)(2,1)S(1)} %fusion.1.rest_0_), custom_call_target="tpu_custom_call" | custom-call | flops 134217728 | bytes 2097152 | tf_op jit(solution)/shard_map/block_product/pallas_call | solution.py:45
  61.3 8.5 %collective-permute-start = (bf16[1024,128]{1,0:T(8,128)(2,1)}, bf16[1024,128]{1,0:T(8,128)(2,1)S(1)}, u32[]{:S(2)}, u32[]{:S(2)}) collective-permute-start(bf16[1024,128]{1,0:T(8,128)(2,1)} %block_product.2.here_ref), channel_id=1, source_target_pairs={{0,1},{1,0},{2,3},{3,2},{4,5},{5,4},{6,7},{7,6},{8,9},{9,8},{10,11... | collective-permute-start | bytes 786440 | tf_op jit(solution)/shard_map/ppermute | solution.py:141
  69.9 0.8 fusion.4.weight_ref
  70.7 0.5 collective-permute-done.there_ref
  71.2 2.2 %middle.1 = (f32[128,256]{1,0:T(8,128)S(1)}, bf16[512,128]{1,0:T(8,128)(2,1)}) custom-call(bf16[1024,128]{1,0:T(8,128)(2,1)} %block_product.2.here_ref, bf16[1024,128]{1,0:T(8,128)(2,1)S(1)} %collective-permute-done.there_ref, bf16[256,256]{1,0:T(8,128)(2,1)S(1)} %fusion.4.weight_ref), custom_call_target="tpu_custom_call" | custom-call | flops 134217728 | bytes 786432 | tf_op jit(solution)/shard_map/middle/pallas_call | solution.py:90
  73.4 0.0 all-gather.2.cloned.1.call-update
  73.4 13.8 %all_to_all.26 = f32[16,8,256]{2,1,0:T(8,128)S(1)} all-to-all(f32[16,8,256]{2,1,0:T(8,128)S(1)} %bitcast.9), channel_id=1, replica_groups=mesh['row'=32,'col'=16,'feat'=2] {'col'}, dimensions={0} | all-to-all | bytes 262144 | tf_op jit(solution)/shard_map/all_to_all | solution.py:118
  87.3 37.7 %all_to_all.27 = f32[32,8,256]{2,1,0:T(8,128)S(1)} all-to-all(f32[32,8,256]{2,1,0:T(8,128)S(1)} %broadcast_in_dim.13), channel_id=1, replica_groups=mesh['row'=32,'col'=16,'feat'=2] {'row'}, dimensions={0} | all-to-all | bytes 524288 | tf_op jit(solution)/shard_map/all_to_all | solution.py:106
  125.0 12.0 %all_to_all.28 = f32[16,8,256]{2,1,0:T(8,128)S(1)} all-to-all(f32[16,8,256]{2,1,0:T(8,128)S(1)} %broadcast_in_dim.14), channel_id=1, replica_groups=mesh['row'=32,'col'=16,'feat'=2] {'col'}, dimensions={0} | all-to-all | bytes 262144 | tf_op jit(solution)/shard_map/all_to_all | solution.py:106
  137.1 0.7 maximum_select_fusion
  137.7 15.1 %all-gather.2.cloned.1.call-done.panel_ref = bf16[8192,128]{1,0:T(8,128)(2,1)} async-done(((bf16[512,128]{1,0:T(8,128)(2,1)}), bf16[8192,128]{1,0:T(8,128)(2,1)}) %all-gather.2.cloned.1.call-update) | async-done | bytes 2097168 | tf_op jit(solution)/shard_map/all_gather | solution.py:143
  152.8 1.6 copy-done.2
  154.4 4.0 %block_product.3 = bf16[512,128]{1,0:T(8,128)(2,1)} custom-call(s32[4,8]{1,0:T(4,128)S(1)} %get-tuple-element.10.offset_ref, bf16[4,8,128,128]{3,2,1,0:T(8,128)(2,1)S(1)} %copy-done.1, bf16[8192,128]{1,0:T(8,128)(2,1)S(1)} %copy-done.2), custom_call_target="tpu_custom_call" | custom-call | flops 134217728 | bytes 2097152 | tf_op jit(solution)/shard_map/block_product/pallas_call | solution.py:45
  (20 shorter events, 0.2 us)
Async XLA Ops:
  7.2 30.1 %copy-start = (bf16[1024,128]{1,0:T(8,128)(2,1)S(1)}, bf16[1024,128]{1,0:T(8,128)(2,1)}, u32[]{:S(2)}) copy-start(bf16[1024,128]{1,0:T(8,128)(2,1)} %param.10) | copy-start | bytes 786436
  29.7 6.9 %copy-start.6 = (s32[4,8]{1,0:T(4,128)S(1)}, s32[4,8]{1,0:T(4,128)}, u32[]{:S(2)}) copy-start(s32[4,8]{1,0:T(4,128)} %param.8) | copy-start | bytes 388
  29.7 6.9 %copy-start.5 = (bf16[256,256]{1,0:T(8,128)(2,1)S(1)}, bf16[256,256]{1,0:T(8,128)(2,1)}, u32[]{:S(2)}) copy-start(bf16[256,256]{1,0:T(8,128)(2,1)} %param.9) | copy-start | bytes 393220
  29.7 7.6 %copy-start.7 = (s32[512]{0:T(512)S(1)}, s32[512]{0:T(512)}, u32[]{:S(2)}) copy-start(s32[512]{0:T(512)} %param.11) | copy-start | bytes 6148
  29.7 27.5 %copy-start.1 = (bf16[4,8,128,128]{3,2,1,0:T(8,128)(2,1)S(1)}, bf16[4,8,128,128]{3,2,1,0:T(8,128)(2,1)}, u32[]{:S(2)}) copy-start(bf16[4,8,128,128]{3,2,1,0:T(8,128)(2,1)} %adj_ref.3) | copy-start | bytes 3145732
  29.7 27.5 %all-to-all-start.1 = ((bf16[4,2048,128]{2,1,0:T(8,128)(2,1)}), bf16[4,2048,128]{2,1,0:T(8,128)(2,1)S(1)}, u32[]{:S(2)}, u32[]{:S(2)}) async-start(bf16[4,2048,128]{2,1,0:T(8,128)(2,1)} %broadcast_in_dim.12), calls=%async_computation.1 | async-start | bytes 4194304 | tf_op jit(solution)/shard_map/all_to_all | solution.py:106
  36.5 116.3 %all-gather.2.cloned.1.call-start = ((), (), s32[]{:S(2)}) async-start(), calls=%async_computation.5 | async-start | bytes 2228224 | tf_op jit(solution)/shard_map/all_gather | solution.py:143
  57.2 12.7 %copy-start.3 = (bf16[128,256]{1,0:T(8,128)(2,1)S(1)}, bf16[128,256]{1,0:T(8,128)(2,1)}, u32[]{:S(2)}) copy-start(bf16[128,256]{1,0:T(8,128)(2,1)} %get-tuple-element.8) | copy-start | bytes 196612
  57.2 12.7 %copy-start.4 = (bf16[128,256]{1,0:T(8,128)(2,1)S(1)}, bf16[128,256]{1,0:T(8,128)(2,1)}, u32[]{:S(2)}) copy-start(bf16[128,256]{1,0:T(8,128)(2,1)} %get-tuple-element.9) | copy-start | bytes 196612
  61.3 9.9 %collective-permute-start = (bf16[1024,128]{1,0:T(8,128)(2,1)}, bf16[1024,128]{1,0:T(8,128)(2,1)S(1)}, u32[]{:S(2)}, u32[]{:S(2)}) collective-permute-start(bf16[1024,128]{1,0:T(8,128)(2,1)} %block_product.2.here_ref), channel_id=1, source_target_pairs={{0,1},{1,0},{2,3},{3,2},{4,5},{5,4},{6,7},{7,6},{8,9},{9,8},{10,11... | collective-permute-start | bytes 786440 | tf_op jit(solution)/shard_map/ppermute | solution.py:141
  152.8 1.6 copy-start.2
Sparse Core Ops, SparseCore 0:
  73.5 79.2 all-gather.1

commit v3 on v2

v3 whole, which is shorter than its diff:
```python
import functools
import math

import jax
import jax.numpy as jnp
from jax import lax
from jax.experimental import pallas as pl
from jax.experimental.pallas import tpu as pltpu
from jax.sharding import PartitionSpec as P

SIDE = 4
Y_LO = 2


def product_kernel(count, which_ref, offset_ref, adj_ref, *rest):
    parts, carried = rest[:count], rest[count:-2]
    out_ref, held = rest[-2:]
    block_rows, nonzero, block, _ = adj_ref.shape

    def place(part, r, k, start):
        held[r, pl.ds(k * block, block), :] = part[pl.ds(start, block), :]

    for r in range(block_rows):
        for k in range(nonzero):
            start = pl.multiple_of(offset_ref[r, k], block)
            if count == 1:
                place(parts[0], r, k, start)
            else:
                for index, part in enumerate(parts):
                    pl.when(which_ref[r, k] == index)(functools.partial(place, part, r, k, start))
    for array in carried:
        out_ref[pl.ds(block_rows * block, array.shape[0]), :] = array[...]
    for r in range(block_rows):
        left = jnp.concatenate([adj_ref[r, k] for k in range(nonzero)], axis=1)
        total = jnp.dot(left, held[r], preferred_element_type=jnp.float32)
        out_ref[pl.ds(r * block, block), :] = total.astype(out_ref.dtype)


def block_product(which, offsets, adj, parts, carried=()):
    block_rows, nonzero, block, _ = adj.shape
    width = parts[0].shape[1]
    rows = block_rows * block + sum(array.shape[0] for array in carried)
    whole = pl.BlockSpec(memory_space=pltpu.VMEM)
    return pl.pallas_call(
        functools.partial(product_kernel, len(parts)),
        out_shape=jax.ShapeDtypeStruct((rows, width), jnp.bfloat16),
        in_specs=[pl.BlockSpec(memory_space=pltpu.SMEM)] * 2 + [whole] * (1 + len(parts) + len(carried)),
        out_specs=whole,
        scratch_shapes=[pltpu.VMEM((block_rows, nonzero * block, width), jnp.bfloat16)],
        compiler_params=pltpu.CompilerParams(vmem_limit_bytes=14 << 20),
        cost_estimate=pl.CostEstimate(
            flops=2 * block_rows * nonzero * block * block * width,
            bytes_accessed=2 * (adj.size + block_rows * nonzero * block * width),
            transcendentals=0,
        ),
        name="block_product",
    )(which, offsets, adj, *parts, *carried)


def middle_kernel(here_ref, there_ref, weight_ref, parcel_ref):
    half = here_ref.shape[1]
    rows = here_ref.shape[0] // 2
    own = here_ref[:rows, :]
    logits = jnp.dot(own, weight_ref[:half, :], preferred_element_type=jnp.float32)
    logits += jnp.dot(there_ref[:rows, :], weight_ref[half:, :], preferred_element_type=jnp.float32)
    target = jnp.concatenate([here_ref[rows:, :], there_ref[rows:, :]], axis=1).astype(jnp.float32)
    logistic = jax.nn.sigmoid(logits)
    slope = logistic * (1.0 + logits * (1.0 - logistic))
    grad_out = ((logits * logistic - target) * slope).astype(jnp.bfloat16)
    back = lax.dot_general(
        grad_out, weight_ref[:half, :], (((1,), (1,)), ((), ())), preferred_element_type=jnp.float32
    ).astype(jnp.bfloat16)
    partial = lax.dot_general(own, grad_out, (((0,), (0,)), ((), ())), preferred_element_type=jnp.float32)
    head = partial.astype(jnp.bfloat16)
    rest = (partial - head.astype(jnp.float32)).astype(jnp.bfloat16)
    count = parcel_ref.shape[0]
    quarter = half // count
    width = partial.shape[1]
    for y in range(count):
        parcel_ref[y, :rows, :] = back
        start = rows
        for values in (head, rest):
            for first in range(0, width, half):
                parcel_ref[y, start : start + quarter, :] = values[y * quarter : (y + 1) * quarter, first : first + half]
                start += quarter


def middle(here, there, weight):
    rows, half = here.shape[0] // 2, here.shape[1]
    extra = 2 * weight.shape[1] // SIDE
    return pl.pallas_call(
        middle_kernel,
        out_shape=jax.ShapeDtypeStruct((SIDE, rows + extra, half), jnp.bfloat16),
        compiler_params=pltpu.CompilerParams(vmem_limit_bytes=14 << 20),
        cost_estimate=pl.CostEstimate(
            flops=4 * rows * weight.size, bytes_accessed=12 * rows * half, transcendentals=rows * weight.shape[1]
        ),
        name="middle",
    )(here, there, weight)


WHOLE = pl.BlockSpec(memory_space=pltpu.VMEM)
SMALL = pltpu.CompilerParams(vmem_limit_bytes=4 << 20)


def open_kernel(skip, parcels_ref, out_ref):
    count, rows, _ = parcels_ref.shape
    pieces = parcels_ref[:, skip:, :].astype(jnp.float32)
    both = pieces[:, : (rows - skip) // 2, :] + pieces[:, (rows - skip) // 2 :, :]
    out_ref[...] = both.sum(0)


def open_parcels(parcels, skip):
    return pl.pallas_call(
        functools.partial(open_kernel, skip),
        out_shape=jax.ShapeDtypeStruct(((parcels.shape[1] - skip) // 2, parcels.shape[2]), jnp.float32),
        in_specs=[WHOLE],
        out_specs=WHOLE,
        compiler_params=SMALL,
        name="open_parcels",
    )(parcels)


def spread_kernel(pieces_ref, *rest):
    out_ref = rest[-1]
    total = pieces_ref[...].sum(0)
    for index in range(out_ref.shape[0]):
        out_ref[index] = total


def spread_sum(pieces, count, after):
    return pl.pallas_call(
        spread_kernel,
        out_shape=jax.ShapeDtypeStruct((count, *pieces.shape[1:]), pieces.dtype),
        in_specs=[WHOLE] + [pl.BlockSpec(memory_space=pl.ANY)] * len(after),
        out_specs=WHOLE,
        compiler_params=SMALL,
        name="spread_sum",
    )(pieces, *after)


def settle_kernel(scale, feat_ref, pieces_ref, out_ref):
    halves, half = out_ref.shape[1] // pieces_ref.shape[2], pieces_ref.shape[2]
    per_half = pieces_ref.shape[0] // halves
    for index in range(halves):
        values = pieces_ref[pl.ds((index ^ feat_ref[0]) * per_half, per_half)] * scale
        out_ref[:, index * half : (index + 1) * half] = values.reshape(out_ref.shape[0], half)


def settle(feat, pieces, scale):
    count, rows, half = pieces.shape
    return pl.pallas_call(
        functools.partial(settle_kernel, scale),
        out_shape=jax.ShapeDtypeStruct((count * rows // 2, 2 * half), pieces.dtype),
        in_specs=[pl.BlockSpec(memory_space=pltpu.SMEM), WHOLE],
        out_specs=WHOLE,
        compiler_params=SMALL,
        name="settle",
    )(feat.reshape(1), pieces)


def to_all(value, axis, count, groups=None):
    copies = jnp.broadcast_to(value[None], (count, *value.shape))
    return lax.all_to_all(copies, axis, 0, 0, axis_index_groups=groups)


ALONG_Y = [[y * SIDE + x for y in range(SIDE)] for x in range(SIDE)]
ALONG_X = [[y * SIDE + x for x in range(SIDE)] for y in range(SIDE)]


def from_x(value, dx):
    pairs = [(y * SIDE + (x + dx) % SIDE, y * SIDE + x) for y in range(SIDE) for x in range(SIDE)]
    return lax.ppermute(value, "col", pairs)


def sum_weight(quarter, row_size, sides, far):
    both = ("row", "col")
    col_size = SIDE * SIDE
    layers = row_size // Y_LO
    near = Y_LO * col_size
    mates = [
        [(z * Y_LO + lo) * col_size + y * SIDE + x for lo in range(Y_LO) for x in range(SIDE)]
        for z in range(layers)
        for y in range(SIDE)
    ]
    depth = [[z * near + i for z in range(layers)] for i in range(near)]
    plane = [[z * near + i for i in range(near)] for z in range(layers)]
    pieces = quarter.reshape(Y_LO * SIDE, -1, quarter.shape[1])
    pieces = lax.all_to_all(pieces, both, 0, 0, axis_index_groups=mates)
    pieces = lax.all_to_all(spread_sum(pieces, layers, sides), both, 0, 0, axis_index_groups=depth)
    return lax.all_to_all(spread_sum(pieces, near, far), both, 0, 0, axis_index_groups=plane)


def per_device(features, adj, col_index, weight, centroid, labels):
    block_rows, nonzero, block, _ = adj.shape
    row_count, half = features.shape
    feat = lax.axis_index("feat")
    row_size, col_size = lax.axis_size("row"), lax.axis_size("col")
    node_count = row_count * row_size * col_size
    local = col_index % (block_rows * col_size)
    owner = local // block_rows
    owner_y, owner_x = owner // SIDE, owner % SIDE
    within = (local % block_rows) * block

    label_table = (
        labels[:, None] == jnp.arange(centroid.shape[0], dtype=jnp.int32)[None, :]
    ).astype(jnp.bfloat16)
    target = jnp.dot(label_table, centroid, preferred_element_type=jnp.float32).astype(jnp.bfloat16)
    swapped = jnp.roll(weight, (half, centroid.shape[1]), (0, 1))
    turned = jnp.where(feat == 0, weight, swapped)

    column = to_all(features, "col", SIDE, ALONG_Y).reshape(-1, half)
    panels = to_all(column, "col", SIDE, ALONG_X).reshape(-1, half)
    offsets = (owner_x * SIDE + owner_y) * row_count + within
    here = block_product(offsets, offsets, adj, [panels], (target,))
    there = lax.ppermute(here, "feat", [(0, 1), (1, 0)])

    parcels = lax.all_to_all(middle(here, there, turned), "col", 0, 0, axis_index_groups=ALONG_Y)
    stride = parcels.shape[1]
    column = parcels.reshape(-1, half)
    parts = [column] + [from_x(column, dx) for dx in range(1, SIDE)]
    which = (owner_x - lax.axis_index("col")) % SIDE
    feature_grad = block_product(which, owner_y * stride + within, adj, parts)

    sides, far = (parts[1], parts[3]), (parts[2],)
    pieces = sum_weight(open_parcels(parcels, row_count), row_size, sides, far)
    weight_grad = settle(feat, pieces, 1.0 / math.sqrt(node_count))
    return (weight_grad, feature_grad)


def solution(mesh):
    placed = (
        P(("row", "col"), "feat"),
        P(("row", "col"), None, None, None),
        P(("row", "col"), None),
        P(),
        P(None, "feat"),
        P(("row", "col")),
    )
    return jax.shard_map(
        per_device,
        mesh=mesh,
        in_specs=placed,
        out_specs=(P("feat", None), P(("row", "col"), "feat")),
        check_vma=False,
    )
```

time: 166 us -> 170 us (1.024); the launches traced: 165 us -> 167 us
  starting transfers between devices: 15.4 us -> 48.8 us
  blocking collectives: 83.4 us -> 66.4 us
  between operations: 14.2 us -> 0.77 us
  waiting for transfers between devices: 35 us -> 36.9 us
    all_to_all x3 -> x1, blocking collectives: 69.6 us -> 19.9 us  [to_all(): return lax.all_to_all(copies, axis, 0, 0, axis_index_groups=groups)]
    all_to_all x1 -> x2, blocking collectives: 13.8 us -> 46.6 us  [the longest x1 26.1 us: sum_weight(): pieces = lax.all_to_all(pieces, both, 0, 0, axis_index_groups=mates)]
    all_to_all x0 -> x2, starting transfers between devices: none -> 25.6 us  [the longest x1 18.6 us: sum_weight(): lax.all_to_all(spread_sum(pieces, layers, sides), both, 0, 0, axis_index_...]
    all_to_all x0 -> x2, waiting for transfers between devices: none -> 17.7 us  [the longest x1 11.6 us: sum_weight(): lax.all_to_all(spread_sum(pieces, layers, sides), both, 0, 0, axis_index_...]
    all_gather x1 -> x0, waiting for transfers between devices: 15.1 us -> none  [per_device(): gathered = lax.all_gather(back, 'col', axis=0, tiled=True)]
    ppermute x0 -> x3, starting transfers between devices: none -> 7.8 us  [from_x(): return lax.ppermute(value, 'col', pairs)]
    pallas_call x3 -> x7, Pallas kernels: 10.3 us -> 8.72 us  [the longest x2 5.12 us: block_product(): pl.pallas_call(functools.partial(product_kernel, len(parts)), out_shape=j...]
  transfers between devices with their start and end apart: 3 -> 7, of which waited for: 3 -> 4; matrix products, arithmetic and copies ran while one was open for 2% -> 2% of each run, Pallas kernels for 0% -> 2%
where the time goes in v3:
time: 170 us; the launch traced here: 167 us
  blocking collectives  66.4 us (39%)
  starting transfers between devices  48.8 us (29%)
  waiting for transfers between devices  36.9 us (22%)
  Pallas kernels  8.72 us (5%)
  local copies, waits for them, and re-layouts  3.31 us (2%)
    all_to_all x1, blocking collectives, sum_weight(): pieces = lax.all_to_all(pieces, both, 0, 0, axis_index_groups=mates)  26.1 us
    all_to_all x1, blocking collectives, per_device(): lax.all_to_all(middle(here, there, turned), 'col', 0, 0, axis_index_group...  20.5 us
    all_to_all x1, blocking collectives, to_all(): return lax.all_to_all(copies, axis, 0, 0, axis_index_groups=groups)  19.9 us
    all_to_all x1, waiting for transfers between devices, to_all(): return lax.all_to_all(copies, axis, 0, 0, axis_index_groups=groups)  18.7 us
    all_to_all x1, starting transfers between devices, sum_weight(): lax.all_to_all(spread_sum(pieces, layers, sides), both, 0, 0, axis_index_...  18.6 us
    all_to_all x1, waiting for transfers between devices, sum_weight(): lax.all_to_all(spread_sum(pieces, layers, sides), both, 0, 0, axis_index_...  11.6 us
    ppermute x1, starting transfers between devices, per_device(): there = lax.ppermute(here, 'feat', [(0, 1), (1, 0)])  8.53 us
    ppermute x3, starting transfers between devices, from_x(): return lax.ppermute(value, 'col', pairs)  7.8 us
  transfers between devices with their start and end apart: 7, of which 4 were waited for; matrix products, arithmetic and copies ran while one was open for 2% of the time, Pallas kernels for 2%

profile of v3, /device:TPU:1, one launch (start us, length us, event | category | flops | bytes accessed | tf_op | source)
XLA Modules:
  0.0 167.0 jit_solution(3392022687241481899)
XLA Ops:
  0.6 1.0 broadcast_in_dim.6
  1.7 19.9 %all_to_all.30 = bf16[4,512,128]{2,1,0:T(8,128)(2,1)S(1)} all-to-all(bf16[4,512,128]{2,1,0:T(8,128)(2,1)S(1)} %broadcast_in_dim.6), channel_id=1, replica_groups={{0,8,16,24},{2,10,18,26},{4,12,20,28},{6,14,22,30},{1,9,17,25},{3,11,19..., dimensions={0} | all-to-all | bytes 1048576 | tf_op jit(solution)/shard_map/all_to_all | solution.py:164
  21.5 1.6 broadcast_in_dim.8
  23.1 6.9 %all-to-all-start.1 = ((bf16[4,2048,128]{2,1,0:T(8,128)(2,1)}), bf16[4,2048,128]{2,1,0:T(8,128)(2,1)S(1)}, u32[]{:S(2)}, u32[]{:S(2)}) async-start(bf16[4,2048,128]{2,1,0:T(8,128)(2,1)} %broadcast_in_dim.8), calls=%async_computation.1 | async-start | bytes 4194304 | tf_op jit(solution)/shard_map/all_to_all | solution.py:164
  30.1 0.7 fusion.11
  30.7 1.2 fusion.1.rest_1_
  31.9 18.7 %all-to-all-done.1 = bf16[4,2048,128]{2,1,0:T(8,128)(2,1)S(1)} async-done(((bf16[4,2048,128]{2,1,0:T(8,128)(2,1)}), bf16[4,2048,128]{2,1,0:T(8,128)(2,1)S(1)}, u32[]{:S(2)}, u32[]{:S(2)}) %all-to-all-start.1) | async-done | bytes 2097184 | tf_op jit(solution)/shard_map/all_to_all | solution.py:164
  50.7 1.8 %block_product.2.here_ref = bf16[1024,128]{1,0:T(8,128)(2,1)} custom-call(s32[4,8]{1,0:T(4,128)S(1)} %get-tuple-element.7.which_ref.offset_ref, s32[4,8]{1,0:T(4,128)S(1)} %get-tuple-element.7.which_ref.offset_ref, bf16[4,8,128,128]{3,2,1,0:T(8,128)(2,1)S(1)} %copy-done.1, bf16[8192,128]{1,0:T(8,128)(2,1)S(1)} %bitcast.6, bf16[512,128]{1,0:T(8,128)(2,1)S(1)} %fusion.1.rest_1_), custom_call_target="tpu_custom_call" | custom-call | flops 134217728 | bytes 2097152 | tf_op jit(solution)/shard_map/block_product/pallas_call | solution.py:44
  52.5 8.5 %collective-permute-start = (bf16[1024,128]{1,0:T(8,128)(2,1)}, bf16[1024,128]{1,0:T(8,128)(2,1)S(1)}, u32[]{:S(2)}, u32[]{:S(2)}) collective-permute-start(bf16[1024,128]{1,0:T(8,128)(2,1)} %block_product.2.here_ref), channel_id=1, source_target_pairs={{0,1},{1,0},{2,3},{3,2},{4,5},{5,4},{6,7},{7,6},{8,9},{9,8},{10,11... | collective-permute-start | bytes 786440 | tf_op jit(solution)/shard_map/ppermute | solution.py:216
  61.1 0.8 fusion.4.weight_ref
  62.4 1.6 middle.1
  64.0 20.5 %all_to_all.31.parcels_ref = bf16[4,640,128]{2,1,0:T(8,128)(2,1)S(1)} all-to-all(bf16[4,640,128]{2,1,0:T(8,128)(2,1)S(1)} %middle.1), channel_id=1, replica_groups={{0,8,16,24},{2,10,18,26},{4,12,20,28},{6,14,22,30},{1,9,17,25},{3,11,19..., dimensions={0} | all-to-all | bytes 1310720 | tf_op jit(solution)/shard_map/all_to_all | solution.py:218
  84.5 2.8 %collective-permute-start.1 = (bf16[2560,128]{1,0:T(8,128)(2,1)S(1)}, bf16[2560,128]{1,0:T(8,128)(2,1)S(1)}, u32[]{:S(2)}, u32[]{:S(2)}) collective-permute-start(bf16[2560,128]{1,0:T(8,128)(2,1)S(1)} %bitcast.7), channel_id=1, source_target_pairs={{2,0},{4,2},{6,4},{0,6},{10,8},{12,10},{14,12},{8,14},{18,16},{20,... | collective-permute-start | bytes 1966088 | tf_op jit(solution)/shard_map/ppermute | solution.py:173
  87.3 2.5 %collective-permute-start.2 = (bf16[2560,128]{1,0:T(8,128)(2,1)S(1)}, bf16[2560,128]{1,0:T(8,128)(2,1)S(1)}, u32[]{:S(2)}, u32[]{:S(2)}) collective-permute-start(bf16[2560,128]{1,0:T(8,128)(2,1)S(1)} %bitcast.8), channel_id=1, source_target_pairs={{6,0},{0,2},{2,4},{4,6},{14,8},{8,10},{10,12},{12,14},{22,16},{16,... | collective-permute-start | bytes 1966088 | tf_op jit(solution)/shard_map/ppermute | solution.py:173
  89.8 2.5 %collective-permute-start.3 = (bf16[2560,128]{1,0:T(8,128)(2,1)S(1)}, bf16[2560,128]{1,0:T(8,128)(2,1)}, u32[]{:S(2)}, u32[]{:S(2)}) collective-permute-start(bf16[2560,128]{1,0:T(8,128)(2,1)S(1)} %bitcast.9), channel_id=1, source_target_pairs={{4,0},{6,2},{0,4},{2,6},{12,8},{14,10},{8,12},{10,14},{20,16},{22,... | collective-permute-start | bytes 1966088 | tf_op jit(solution)/shard_map/ppermute | solution.py:173
  92.3 26.1 %all_to_all.32.pieces_ref = f32[8,8,128]{2,1,0:T(8,128)S(1)} all-to-all(f32[8,8,128]{2,1,0:T(8,128)S(1)} %bitcast.11), channel_id=1, replica_groups={{0,2,4,6,32,34,36,38},{8,10,12,14,40,42,44,46},{16,18,20,22,48,50,52,54..., dimensions={0} | all-to-all | bytes 65536 | tf_op jit(solution)/shard_map/all_to_all | solution.py:189
  118.4 0.6 spread_sum.2
  119.1 18.6 %all-to-all-start.4 = ((f32[16,8,128]{2,1,0:T(8,128)}), f32[16,8,128]{2,1,0:T(8,128)S(1)}, u32[]{:S(2)}, u32[]{:S(2)}) async-start(f32[16,8,128]{2,1,0:T(8,128)} %spread_sum.2), calls=%async_computation.4 | async-start | bytes 131072 | tf_op jit(solution)/shard_map/all_to_all | solution.py:190
  137.7 11.6 %all-to-all-done.4.pieces_ref = f32[16,8,128]{2,1,0:T(8,128)S(1)} async-done(((f32[16,8,128]{2,1,0:T(8,128)}), f32[16,8,128]{2,1,0:T(8,128)S(1)}, u32[]{:S(2)}, u32[]{:S(2)}) %all-to-all-start.4) | async-done | bytes 65568 | tf_op jit(solution)/shard_map/all_to_all | solution.py:190
  149.2 0.7 spread_sum.3
  149.9 7.0 %all-to-all-start.5 = ((f32[32,8,128]{2,1,0:T(8,128)}), f32[32,8,128]{2,1,0:T(8,128)S(1)}, u32[]{:S(2)}, u32[]{:S(2)}) async-start(f32[32,8,128]{2,1,0:T(8,128)} %spread_sum.3), calls=%async_computation.5 | async-start | bytes 262144 | tf_op jit(solution)/shard_map/all_to_all | solution.py:191
  157.0 3.3 %block_product.3 = bf16[512,128]{1,0:T(8,128)(2,1)} custom-call(s32[4,8]{1,0:T(4,128)S(1)} %get-tuple-element.6.which_ref, s32[4,8]{1,0:T(4,128)S(1)} %get-tuple-element.2.offset_ref, bf16[4,8,128,128]{3,2,1,0:T(8,128)(2,1)S(1)} %copy-done.1, bf16[2560,128]{1,0:T(8,128)(2,1)S(1)} %bitcast.10, bf16[2560,128]{1,0:T(8,128)(2,1)S(1)} %collective-permute-done.1.rest_0_.rest_1_, ...), custom_call_target="tpu_custom_call" | custom-call | flops 134217728 | bytes 2097152 | tf_op jit(solution)/shard_map/block_product/pallas_call | solution.py:44
  160.2 6.1 %all-to-all-done.5.pieces_ref = f32[32,8,128]{2,1,0:T(8,128)S(1)} async-done(((f32[32,8,128]{2,1,0:T(8,128)}), f32[32,8,128]{2,1,0:T(8,128)S(1)}, u32[]{:S(2)}, u32[]{:S(2)}) %all-to-all-start.5) | async-done | bytes 131104 | tf_op jit(solution)/shard_map/all_to_all | solution.py:191
  166.4 0.7 settle.1
  (20 shorter events, 0.6 us)
Async XLA Ops:
  0.6 30.1 %copy-start = (bf16[1024,128]{1,0:T(8,128)(2,1)S(1)}, bf16[1024,128]{1,0:T(8,128)(2,1)}, u32[]{:S(2)}) copy-start(bf16[1024,128]{1,0:T(8,128)(2,1)} %param.10) | copy-start | bytes 786436
  23.1 6.9 %copy-start.5 = (s32[4,8]{1,0:T(4,128)S(1)}, s32[4,8]{1,0:T(4,128)}, u32[]{:S(2)}) copy-start(s32[4,8]{1,0:T(4,128)} %param.8) | copy-start | bytes 388
  23.1 6.9 %copy-start.4 = (bf16[256,256]{1,0:T(8,128)(2,1)S(1)}, bf16[256,256]{1,0:T(8,128)(2,1)}, u32[]{:S(2)}) copy-start(bf16[256,256]{1,0:T(8,128)(2,1)} %param.9) | copy-start | bytes 393220
  23.1 27.5 %copy-start.1 = (bf16[4,8,128,128]{3,2,1,0:T(8,128)(2,1)S(1)}, bf16[4,8,128,128]{3,2,1,0:T(8,128)(2,1)}, u32[]{:S(2)}) copy-start(bf16[4,8,128,128]{3,2,1,0:T(8,128)(2,1)} %adj_ref.3) | copy-start | bytes 3145732
  23.1 27.5 %all-to-all-start.1 = ((bf16[4,2048,128]{2,1,0:T(8,128)(2,1)}), bf16[4,2048,128]{2,1,0:T(8,128)(2,1)S(1)}, u32[]{:S(2)}, u32[]{:S(2)}) async-start(bf16[4,2048,128]{2,1,0:T(8,128)(2,1)} %broadcast_in_dim.8), calls=%async_computation.1 | async-start | bytes 4194304 | tf_op jit(solution)/shard_map/all_to_all | solution.py:164
  50.7 10.4 %copy-start.2 = (bf16[128,256]{1,0:T(8,128)(2,1)S(1)}, bf16[128,256]{1,0:T(8,128)(2,1)}, u32[]{:S(2)}) copy-start(bf16[128,256]{1,0:T(8,128)(2,1)} %get-tuple-element.4) | copy-start | bytes 196612
  50.7 10.4 %copy-start.3 = (bf16[128,256]{1,0:T(8,128)(2,1)S(1)}, bf16[128,256]{1,0:T(8,128)(2,1)}, u32[]{:S(2)}) copy-start(bf16[128,256]{1,0:T(8,128)(2,1)} %get-tuple-element.5) | copy-start | bytes 196612
  52.5 9.9 %collective-permute-start = (bf16[1024,128]{1,0:T(8,128)(2,1)}, bf16[1024,128]{1,0:T(8,128)(2,1)S(1)}, u32[]{:S(2)}, u32[]{:S(2)}) collective-permute-start(bf16[1024,128]{1,0:T(8,128)(2,1)} %block_product.2.here_ref), channel_id=1, source_target_pairs={{0,1},{1,0},{2,3},{3,2},{4,5},{5,4},{6,7},{7,6},{8,9},{9,8},{10,11... | collective-permute-start | bytes 786440 | tf_op jit(solution)/shard_map/ppermute | solution.py:216
  84.5 33.9 %collective-permute-start.1 = (bf16[2560,128]{1,0:T(8,128)(2,1)S(1)}, bf16[2560,128]{1,0:T(8,128)(2,1)S(1)}, u32[]{:S(2)}, u32[]{:S(2)}) collective-permute-start(bf16[2560,128]{1,0:T(8,128)(2,1)S(1)} %bitcast.7), channel_id=1, source_target_pairs={{2,0},{4,2},{6,4},{0,6},{10,8},{12,10},{14,12},{8,14},{18,16},{20,... | collective-permute-start | bytes 1966088 | tf_op jit(solution)/shard_map/ppermute | solution.py:173
  87.3 31.2 %collective-permute-start.2 = (bf16[2560,128]{1,0:T(8,128)(2,1)S(1)}, bf16[2560,128]{1,0:T(8,128)(2,1)S(1)}, u32[]{:S(2)}, u32[]{:S(2)}) collective-permute-start(bf16[2560,128]{1,0:T(8,128)(2,1)S(1)} %bitcast.8), channel_id=1, source_target_pairs={{6,0},{0,2},{2,4},{4,6},{14,8},{8,10},{10,12},{12,14},{22,16},{16,... | collective-permute-start | bytes 1966088 | tf_op jit(solution)/shard_map/ppermute | solution.py:173
  89.8 47.9 %collective-permute-start.3 = (bf16[2560,128]{1,0:T(8,128)(2,1)S(1)}, bf16[2560,128]{1,0:T(8,128)(2,1)}, u32[]{:S(2)}, u32[]{:S(2)}) collective-permute-start(bf16[2560,128]{1,0:T(8,128)(2,1)S(1)} %bitcast.9), channel_id=1, source_target_pairs={{4,0},{6,2},{0,4},{2,6},{12,8},{14,10},{8,12},{10,14},{20,16},{22,... | collective-permute-start | bytes 1966088 | tf_op jit(solution)/shard_map/ppermute | solution.py:173
  119.1 30.2 %all-to-all-start.4 = ((f32[16,8,128]{2,1,0:T(8,128)}), f32[16,8,128]{2,1,0:T(8,128)S(1)}, u32[]{:S(2)}, u32[]{:S(2)}) async-start(f32[16,8,128]{2,1,0:T(8,128)} %spread_sum.2), calls=%async_computation.4 | async-start | bytes 131072 | tf_op jit(solution)/shard_map/all_to_all | solution.py:190
  149.9 16.5 %all-to-all-start.5 = ((f32[32,8,128]{2,1,0:T(8,128)}), f32[32,8,128]{2,1,0:T(8,128)S(1)}, u32[]{:S(2)}, u32[]{:S(2)}) async-start(f32[32,8,128]{2,1,0:T(8,128)} %spread_sum.3), calls=%async_computation.5 | async-start | bytes 262144 | tf_op jit(solution)/shard_map/all_to_all | solution.py:191

commit v4 on v3

--- a/solution.py
+++ b/solution.py
@@ -57,7 +57,7 @@
     )(which, offsets, adj, *parts, *carried)
 
 
-def middle_kernel(here_ref, there_ref, weight_ref, parcel_ref):
+def middle_kernel(here_ref, there_ref, weight_ref, partial_ref, back_ref):
     half = here_ref.shape[1]
     rows = here_ref.shape[0] // 2
     own = here_ref[:rows, :]
@@ -70,27 +70,21 @@
     back = lax.dot_general(
         grad_out, weight_ref[:half, :], (((1,), (1,)), ((), ())), preferred_element_type=jnp.float32
     ).astype(jnp.bfloat16)
+    for y in range(back_ref.shape[0]):
+        back_ref[y] = back
     partial = lax.dot_general(own, grad_out, (((0,), (0,)), ((), ())), preferred_element_type=jnp.float32)
-    head = partial.astype(jnp.bfloat16)
-    rest = (partial - head.astype(jnp.float32)).astype(jnp.bfloat16)
-    count = parcel_ref.shape[0]
-    quarter = half // count
-    width = partial.shape[1]
-    for y in range(count):
-        parcel_ref[y, :rows, :] = back
-        start = rows
-        for values in (head, rest):
-            for first in range(0, width, half):
-                parcel_ref[y, start : start + quarter, :] = values[y * quarter : (y + 1) * quarter, first : first + half]
-                start += quarter
+    for index in range(partial_ref.shape[0]):
+        partial_ref[index] = partial[:, index * half : (index + 1) * half]
 
 
 def middle(here, there, weight):
     rows, half = here.shape[0] // 2, here.shape[1]
-    extra = 2 * weight.shape[1] // SIDE
     return pl.pallas_call(
         middle_kernel,
-        out_shape=jax.ShapeDtypeStruct((SIDE, rows + extra, half), jnp.bfloat16),
+        out_shape=(
+            jax.ShapeDtypeStruct((weight.shape[1] // half, half, half), jnp.float32),
+            jax.ShapeDtypeStruct((SIDE, rows, half), jnp.bfloat16),
+        ),
         compiler_params=pltpu.CompilerParams(vmem_limit_bytes=14 << 20),
         cost_estimate=pl.CostEstimate(
             flops=4 * rows * weight.size, bytes_accessed=12 * rows * half, transcendentals=rows * weight.shape[1]
@@ -103,24 +97,6 @@
 SMALL = pltpu.CompilerParams(vmem_limit_bytes=4 << 20)
 
 
-def open_kernel(skip, parcels_ref, out_ref):
-    count, rows, _ = parcels_ref.shape
-    pieces = parcels_ref[:, skip:, :].astype(jnp.float32)
-    both = pieces[:, : (rows - skip) // 2, :] + pieces[:, (rows - skip) // 2 :, :]
-    out_ref[...] = both.sum(0)
-
-
-def open_parcels(parcels, skip):
-    return pl.pallas_call(
-        functools.partial(open_kernel, skip),
-        out_shape=jax.ShapeDtypeStruct(((parcels.shape[1] - skip) // 2, parcels.shape[2]), jnp.float32),
-        in_specs=[WHOLE],
-        out_specs=WHOLE,
-        compiler_params=SMALL,
-        name="open_parcels",
-    )(parcels)
-
-
 def spread_kernel(pieces_ref, *rest):
     out_ref = rest[-1]
     total = pieces_ref[...].sum(0)
@@ -128,7 +104,7 @@
         out_ref[index] = total
 
 
-def spread_sum(pieces, count, after):
+def spread_sum(pieces, count, after=()):
     return pl.pallas_call(
         spread_kernel,
         out_shape=jax.ShapeDtypeStruct((count, *pieces.shape[1:]), pieces.dtype),
@@ -168,27 +144,15 @@
 ALONG_X = [[y * SIDE + x for x in range(SIDE)] for y in range(SIDE)]
 
 
-def from_x(value, dx):
-    pairs = [(y * SIDE + (x + dx) % SIDE, y * SIDE + x) for y in range(SIDE) for x in range(SIDE)]
-    return lax.ppermute(value, "col", pairs)
-
-
-def sum_weight(quarter, row_size, sides, far):
+def sum_weight(pieces, row_size):
     both = ("row", "col")
-    col_size = SIDE * SIDE
     layers = row_size // Y_LO
-    near = Y_LO * col_size
-    mates = [
-        [(z * Y_LO + lo) * col_size + y * SIDE + x for lo in range(Y_LO) for x in range(SIDE)]
-        for z in range(layers)
-        for y in range(SIDE)
-    ]
+    near = pieces.shape[0]
     depth = [[z * near + i for z in range(layers)] for i in range(near)]
     plane = [[z * near + i for i in range(near)] for z in range(layers)]
-    pieces = quarter.reshape(Y_LO * SIDE, -1, quarter.shape[1])
-    pieces = lax.all_to_all(pieces, both, 0, 0, axis_index_groups=mates)
-    pieces = lax.all_to_all(spread_sum(pieces, layers, sides), both, 0, 0, axis_index_groups=depth)
-    return lax.all_to_all(spread_sum(pieces, near, far), both, 0, 0, axis_index_groups=plane)
+    pieces = lax.all_to_all(pieces, both, 0, 0, axis_index_groups=plane)
+    pieces = lax.all_to_all(spread_sum(pieces, layers), both, 0, 0, axis_index_groups=depth)
+    return lax.all_to_all(spread_sum(pieces, near), both, 0, 0, axis_index_groups=plane)
 
 
 def per_device(features, adj, col_index, weight, centroid, labels):
@@ -215,15 +179,12 @@
     here = block_product(offsets, offsets, adj, [panels], (target,))
     there = lax.ppermute(here, "feat", [(0, 1), (1, 0)])
 
-    parcels = lax.all_to_all(middle(here, there, turned), "col", 0, 0, axis_index_groups=ALONG_Y)
-    stride = parcels.shape[1]
-    column = parcels.reshape(-1, half)
-    parts = [column] + [from_x(column, dx) for dx in range(1, SIDE)]
-    which = (owner_x - lax.axis_index("col")) % SIDE
-    feature_grad = block_product(which, owner_y * stride + within, adj, parts)
-
-    sides, far = (parts[1], parts[3]), (parts[2],)
-    pieces = sum_weight(open_parcels(parcels, row_count), row_size, sides, far)
+    partial, back = middle(here, there, turned)
+    column = lax.all_to_all(back, "col", 0, 0, axis_index_groups=ALONG_Y).reshape(-1, half)
+    gathered = lax.all_gather(column, "col", axis=0, tiled=True, axis_index_groups=ALONG_X)
+    feature_grad = block_product(offsets, offsets, adj, [gathered])
+
+    pieces = sum_weight(partial.reshape(Y_LO * col_size, -1, half), row_size)
     weight_grad = settle(feat, pieces, 1.0 / math.sqrt(node_count))
     return (weight_grad, feature_grad)
 

time: 170 us -> 159 us (0.935)
  starting transfers between devices: 48.8 us -> 15.4 us
  blocking collectives: 66.4 us -> 94.8 us
  waiting for transfers between devices: 36.9 us -> 19.9 us
  between operations: 0.77 us -> 14.1 us
  Pallas kernels: 8.72 us -> 5.93 us
    all_to_all x2 -> x4, blocking collectives: 46.6 us -> 75 us  [the longest x1 30 us: sum_weight(): lax.all_to_all(spread_sum(pieces, layers), both, 0, 0, axis_index_groups=...]
    all_to_all x2 -> x0, starting transfers between devices: 25.6 us -> none  [the longest x1 18.6 us: sum_weight(): lax.all_to_all(spread_sum(pieces, layers, sides), both, 0, 0, axis_index_...]
    all_to_all x2 -> x0, waiting for transfers between devices: 17.7 us -> none  [the longest x1 11.6 us: sum_weight(): lax.all_to_all(spread_sum(pieces, layers, sides), both, 0, 0, axis_index_...]
    ppermute x3 -> x0, starting transfers between devices: 7.8 us -> none  [from_x(): return lax.ppermute(value, 'col', pairs)]
  transfers between devices with their start and end apart: 7 -> 3, of which waited for: 4 -> 2; matrix products, arithmetic and copies ran while one was open for 2% -> 1% of each run, Pallas kernels for 2% -> 0%
where the time goes in v4:
time: 159 us; the launch traced here: 156 us
  blocking collectives  94.8 us (60%)
  waiting for transfers between devices  19.9 us (13%)
  starting transfers between devices  15.4 us (10%)
  between operations  14.1 us (9%)
  Pallas kernels  5.93 us (4%)
  local copies, waits for them, and re-layouts  4.9 us (3%)
    all_to_all x1, blocking collectives, sum_weight(): lax.all_to_all(spread_sum(pieces, layers), both, 0, 0, axis_index_groups=...  30 us
    all_to_all x1, blocking collectives, to_all(): return lax.all_to_all(copies, axis, 0, 0, axis_index_groups=groups)  19.9 us
    all_to_all x1, waiting for transfers between devices, to_all(): return lax.all_to_all(copies, axis, 0, 0, axis_index_groups=groups)  19.4 us
    all_to_all x1, blocking collectives, per_device(): lax.all_to_all(back, 'col', 0, 0, axis_index_groups=ALONG_Y)  18.5 us
    all_to_all x1, blocking collectives, sum_weight(): pieces = lax.all_to_all(pieces, both, 0, 0, axis_index_groups=plane)  14.1 us
    all_to_all x1, blocking collectives, sum_weight(): lax.all_to_all(spread_sum(pieces, near), both, 0, 0, axis_index_groups=pl...  12.4 us
    ppermute x1, starting transfers between devices, per_device(): there = lax.ppermute(here, 'feat', [(0, 1), (1, 0)])  8.53 us
    all_to_all x1, starting transfers between devices, to_all(): return lax.all_to_all(copies, axis, 0, 0, axis_index_groups=groups)  6.88 us
  transfers between devices with their start and end apart: 3, of which 2 were waited for; matrix products, arithmetic and copies ran while one was open for 1% of the time, Pallas kernels for 0%

profile of v4, /device:TPU:1, one launch (start us, length us, event | category | flops | bytes accessed | tf_op | source)
XLA Modules:
  0.0 156.5 jit_solution(7103527790648231428)
XLA Ops:
  7.2 0.0 copy-start
  7.2 1.0 broadcast_in_dim.6
  8.2 19.9 %all_to_all.30 = bf16[4,512,128]{2,1,0:T(8,128)(2,1)S(1)} all-to-all(bf16[4,512,128]{2,1,0:T(8,128)(2,1)S(1)} %broadcast_in_dim.6), channel_id=1, replica_groups={{0,8,16,24},{2,10,18,26},{4,12,20,28},{6,14,22,30},{1,9,17,25},{3,11,19..., dimensions={0} | all-to-all | bytes 1048576 | tf_op jit(solution)/shard_map/all_to_all | solution.py:140
  28.1 1.6 %broadcast_in_dim.8 = bf16[4,2048,128]{2,1,0:T(8,128)(2,1)} broadcast(bf16[2048,128]{1,0:T(8,128)(2,1)S(1)} %bitcast.8), dimensions={1,2} | broadcast | bytes 2621440 | tf_op jit(solution)/shard_map/broadcast_in_dim | solution.py:139
  29.7 6.9 %all-to-all-start.1 = ((bf16[4,2048,128]{2,1,0:T(8,128)(2,1)}), bf16[4,2048,128]{2,1,0:T(8,128)(2,1)S(1)}, u32[]{:S(2)}, u32[]{:S(2)}) async-start(bf16[4,2048,128]{2,1,0:T(8,128)(2,1)} %broadcast_in_dim.8), calls=%async_computation.1 | async-start | bytes 4194304 | tf_op jit(solution)/shard_map/all_to_all | solution.py:140
  36.6 0.0 all-gather.2.cloned.1.call-start
  36.6 0.0 copy-done.6
  36.6 0.0 copy-done.5
  36.6 0.7 fusion.15
  37.3 0.5 fusion.1.rest_1_
  37.8 19.4 %all-to-all-done.1 = bf16[4,2048,128]{2,1,0:T(8,128)(2,1)S(1)} async-done(((bf16[4,2048,128]{2,1,0:T(8,128)(2,1)}), bf16[4,2048,128]{2,1,0:T(8,128)(2,1)S(1)}, u32[]{:S(2)}, u32[]{:S(2)}) %all-to-all-start.1) | async-done | bytes 2097184 | tf_op jit(solution)/shard_map/all_to_all | solution.py:140
  57.2 1.8 %block_product.2.here_ref = bf16[1024,128]{1,0:T(8,128)(2,1)} custom-call(s32[4,8]{1,0:T(4,128)S(1)} %fusion.10.which_ref.offset_ref, s32[4,8]{1,0:T(4,128)S(1)} %fusion.10.which_ref.offset_ref, bf16[4,8,128,128]{3,2,1,0:T(8,128)(2,1)S(1)} %copy-done.1, bf16[8192,128]{1,0:T(8,128)(2,1)S(1)} %bitcast.6, bf16[512,128]{1,0:T(8,128)(2,1)S(1)} %fusion.1.rest_1_), custom_call_target="tpu_custom_call" | custom-call | flops 134217728 | bytes 2097152 | tf_op jit(solution)/shard_map/block_product/pallas_call | solution.py:44
  59.0 8.5 %collective-permute-start = (bf16[1024,128]{1,0:T(8,128)(2,1)}, bf16[1024,128]{1,0:T(8,128)(2,1)S(1)}, u32[]{:S(2)}, u32[]{:S(2)}) collective-permute-start(bf16[1024,128]{1,0:T(8,128)(2,1)} %block_product.2.here_ref), channel_id=1, source_target_pairs={{0,1},{1,0},{2,3},{3,2},{4,5},{5,4},{6,7},{7,6},{8,9},{9,8},{10,11... | collective-permute-start | bytes 786440 | tf_op jit(solution)/shard_map/ppermute | solution.py:180
  67.6 0.8 fusion.4.weight_ref
  68.4 0.5 collective-permute-done.there_ref
  68.9 1.6 %middle.1 = (f32[2,128,128]{2,1,0:T(8,128)S(1)}, bf16[4,512,128]{2,1,0:T(8,128)(2,1)S(1)}) custom-call(bf16[1024,128]{1,0:T(8,128)(2,1)} %block_product.2.here_ref, bf16[1024,128]{1,0:T(8,128)(2,1)S(1)} %collective-permute-done.there_ref, bf16[256,256]{1,0:T(8,128)(2,1)S(1)} %fusion.4.weight_ref), custom_call_target="tpu_custom_call" | custom-call | flops 134217728 | bytes 786432 | tf_op jit(solution)/shard_map/middle/pallas_call | solution.py:82
  70.5 18.5 %all_to_all.31 = bf16[4,512,128]{2,1,0:T(8,128)(2,1)} all-to-all(bf16[4,512,128]{2,1,0:T(8,128)(2,1)S(1)} %get-tuple-element.5), channel_id=1, replica_groups={{0,8,16,24},{2,10,18,26},{4,12,20,28},{6,14,22,30},{1,9,17,25},{3,11,19..., dimensions={0} | all-to-all | bytes 1048576 | tf_op jit(solution)/shard_map/all_to_all | solution.py:183
  89.0 0.0 all-gather.2.cloned.1.call-update
  89.0 14.1 %all_to_all.32.pieces_ref = f32[32,8,128]{2,1,0:T(8,128)S(1)} all-to-all(f32[32,8,128]{2,1,0:T(8,128)S(1)} %bitcast.7), channel_id=1, replica_groups={{0,2,4,6,8,10,12,14,16,18,20,22,24,26,28,30,32,34,36,38,40,42,44,46,48,..., dimensions={0} | all-to-all | bytes 262144 | tf_op jit(solution)/shard_map/all_to_all | solution.py:153
  103.1 30.0 %all_to_all.33.pieces_ref = f32[16,8,128]{2,1,0:T(8,128)S(1)} all-to-all(f32[16,8,128]{2,1,0:T(8,128)S(1)} %spread_sum.2), channel_id=1, replica_groups={{0,64,128,192,256,320,384,448,512,576,640,704,768,832,896,960},{2,66,13..., dimensions={0} | all-to-all | bytes 131072 | tf_op jit(solution)/shard_map/all_to_all | solution.py:154
  133.1 12.4 %all_to_all.34.pieces_ref = f32[32,8,128]{2,1,0:T(8,128)S(1)} all-to-all(f32[32,8,128]{2,1,0:T(8,128)S(1)} %spread_sum.3), channel_id=1, replica_groups={{0,2,4,6,8,10,12,14,16,18,20,22,24,26,28,30,32,34,36,38,40,42,44,46,48,..., dimensions={0} | all-to-all | bytes 262144 | tf_op jit(solution)/shard_map/all_to_all | solution.py:155
  145.6 0.7 settle.1
  146.2 1.6 %copy-done.2 = bf16[8192,128]{1,0:T(8,128)(2,1)S(1)} copy-done((bf16[8192,128]{1,0:T(8,128)(2,1)S(1)}, bf16[8192,128]{1,0:T(8,128)(2,1)}, u32[]{:S(2)}) %copy-start.2) | copy-done | bytes 2097176
  147.8 1.8 %block_product.3 = bf16[512,128]{1,0:T(8,128)(2,1)} custom-call(s32[4,8]{1,0:T(4,128)S(1)} %fusion.10.which_ref.offset_ref, s32[4,8]{1,0:T(4,128)S(1)} %fusion.10.which_ref.offset_ref, bf16[4,8,128,128]{3,2,1,0:T(8,128)(2,1)S(1)} %copy-done.1, bf16[8192,128]{1,0:T(8,128)(2,1)S(1)} %copy-done.2), custom_call_target="tpu_custom_call" | custom-call | flops 134217728 | bytes 2097152 | tf_op jit(solution)/shard_map/block_product/pallas_call | solution.py:44
  (17 shorter events, 0.1 us)
Async XLA Ops:
  7.2 30.1 %copy-start = (bf16[1024,128]{1,0:T(8,128)(2,1)S(1)}, bf16[1024,128]{1,0:T(8,128)(2,1)}, u32[]{:S(2)}) copy-start(bf16[1024,128]{1,0:T(8,128)(2,1)} %param.10) | copy-start | bytes 786436
  29.7 6.9 %copy-start.6 = (s32[4,8]{1,0:T(4,128)S(1)}, s32[4,8]{1,0:T(4,128)}, u32[]{:S(2)}) copy-start(s32[4,8]{1,0:T(4,128)} %param.8) | copy-start | bytes 388
  29.7 6.9 %copy-start.5 = (bf16[256,256]{1,0:T(8,128)(2,1)S(1)}, bf16[256,256]{1,0:T(8,128)(2,1)}, u32[]{:S(2)}) copy-start(bf16[256,256]{1,0:T(8,128)(2,1)} %param.9) | copy-start | bytes 393220
  29.7 7.6 %copy-start.7 = (s32[512]{0:T(512)S(1)}, s32[512]{0:T(512)}, u32[]{:S(2)}) copy-start(s32[512]{0:T(512)} %param.11) | copy-start | bytes 6148
  29.7 27.5 %copy-start.1 = (bf16[4,8,128,128]{3,2,1,0:T(8,128)(2,1)S(1)}, bf16[4,8,128,128]{3,2,1,0:T(8,128)(2,1)}, u32[]{:S(2)}) copy-start(bf16[4,8,128,128]{3,2,1,0:T(8,128)(2,1)} %adj_ref.3) | copy-start | bytes 3145732
  29.7 27.5 %all-to-all-start.1 = ((bf16[4,2048,128]{2,1,0:T(8,128)(2,1)}), bf16[4,2048,128]{2,1,0:T(8,128)(2,1)S(1)}, u32[]{:S(2)}, u32[]{:S(2)}) async-start(bf16[4,2048,128]{2,1,0:T(8,128)(2,1)} %broadcast_in_dim.8), calls=%async_computation.1 | async-start | bytes 4194304 | tf_op jit(solution)/shard_map/all_to_all | solution.py:140
  36.6 109.7 %all-gather.2.cloned.1.call-start = ((), (), s32[]{:S(2)}) async-start(), calls=%async_computation.6 | async-start | bytes 2621440 | tf_op jit(solution)/shard_map/all_gather | solution.py:184
  57.2 10.4 %copy-start.3 = (bf16[128,256]{1,0:T(8,128)(2,1)S(1)}, bf16[128,256]{1,0:T(8,128)(2,1)}, u32[]{:S(2)}) copy-start(bf16[128,256]{1,0:T(8,128)(2,1)} %get-tuple-element.6) | copy-start | bytes 196612
  57.2 10.4 %copy-start.4 = (bf16[128,256]{1,0:T(8,128)(2,1)S(1)}, bf16[128,256]{1,0:T(8,128)(2,1)}, u32[]{:S(2)}) copy-start(bf16[128,256]{1,0:T(8,128)(2,1)} %get-tuple-element.7) | copy-start | bytes 196612
  59.0 9.9 %collective-permute-start = (bf16[1024,128]{1,0:T(8,128)(2,1)}, bf16[1024,128]{1,0:T(8,128)(2,1)S(1)}, u32[]{:S(2)}, u32[]{:S(2)}) collective-permute-start(bf16[1024,128]{1,0:T(8,128)(2,1)} %block_product.2.here_ref), channel_id=1, source_target_pairs={{0,1},{1,0},{2,3},{3,2},{4,5},{5,4},{6,7},{7,6},{8,9},{9,8},{10,11... | collective-permute-start | bytes 786440 | tf_op jit(solution)/shard_map/ppermute | solution.py:180
  146.2 1.6 %copy-start.2 = (bf16[8192,128]{1,0:T(8,128)(2,1)S(1)}, bf16[8192,128]{1,0:T(8,128)(2,1)}, u32[]{:S(2)}) copy-start(bf16[8192,128]{1,0:T(8,128)(2,1)} %all-gather.2.cloned.1.call-done.rest_0_) | copy-start | bytes 6291460
Sparse Core Ops, SparseCore 0:
  89.1 44.2 all-gather.1

commit v5 on v3

--- a/solution.py
+++ b/solution.py
@@ -103,19 +103,25 @@
 SMALL = pltpu.CompilerParams(vmem_limit_bytes=4 << 20)
 
 
-def open_kernel(skip, parcels_ref, out_ref):
-    count, rows, _ = parcels_ref.shape
+def open_kernel(parcels_ref, quarter_ref, column_ref):
+    skip = parcels_ref.shape[1] - 2 * quarter_ref.shape[0]
+    half = (parcels_ref.shape[1] - skip) // 2
     pieces = parcels_ref[:, skip:, :].astype(jnp.float32)
-    both = pieces[:, : (rows - skip) // 2, :] + pieces[:, (rows - skip) // 2 :, :]
-    out_ref[...] = both.sum(0)
+    quarter_ref[...] = (pieces[:, :half, :] + pieces[:, half:, :]).sum(0)
+    for y in range(parcels_ref.shape[0]):
+        column_ref[y] = parcels_ref[y, :skip, :]
 
 
 def open_parcels(parcels, skip):
-    return pl.pallas_call(
-        functools.partial(open_kernel, skip),
-        out_shape=jax.ShapeDtypeStruct(((parcels.shape[1] - skip) // 2, parcels.shape[2]), jnp.float32),
+    count, rows, width = parcels.shape
+    return pl.pallas_call(
+        open_kernel,
+        out_shape=(
+            jax.ShapeDtypeStruct(((rows - skip) // 2, width), jnp.float32),
+            jax.ShapeDtypeStruct((count, skip, width), parcels.dtype),
+        ),
         in_specs=[WHOLE],
-        out_specs=WHOLE,
+        out_specs=(WHOLE, WHOLE),
         compiler_params=SMALL,
         name="open_parcels",
     )(parcels)
@@ -128,7 +134,7 @@
         out_ref[index] = total
 
 
-def spread_sum(pieces, count, after):
+def spread_sum(pieces, count, after=()):
     return pl.pallas_call(
         spread_kernel,
         out_shape=jax.ShapeDtypeStruct((count, *pieces.shape[1:]), pieces.dtype),
@@ -139,7 +145,7 @@
     )(pieces, *after)
 
 
-def settle_kernel(scale, feat_ref, pieces_ref, out_ref):
+def settle_kernel(scale, feat_ref, pieces_ref, after_ref, out_ref):
     halves, half = out_ref.shape[1] // pieces_ref.shape[2], pieces_ref.shape[2]
     per_half = pieces_ref.shape[0] // halves
     for index in range(halves):
@@ -147,16 +153,16 @@
         out_ref[:, index * half : (index + 1) * half] = values.reshape(out_ref.shape[0], half)
 
 
-def settle(feat, pieces, scale):
+def settle(feat, pieces, after, scale):
     count, rows, half = pieces.shape
     return pl.pallas_call(
         functools.partial(settle_kernel, scale),
         out_shape=jax.ShapeDtypeStruct((count * rows // 2, 2 * half), pieces.dtype),
-        in_specs=[pl.BlockSpec(memory_space=pltpu.SMEM), WHOLE],
+        in_specs=[pl.BlockSpec(memory_space=pltpu.SMEM), WHOLE, pl.BlockSpec(memory_space=pl.ANY)],
         out_specs=WHOLE,
         compiler_params=SMALL,
         name="settle",
-    )(feat.reshape(1), pieces)
+    )(feat.reshape(1), pieces, after)
 
 
 def to_all(value, axis, count, groups=None):
@@ -168,12 +174,7 @@
 ALONG_X = [[y * SIDE + x for x in range(SIDE)] for y in range(SIDE)]
 
 
-def from_x(value, dx):
-    pairs = [(y * SIDE + (x + dx) % SIDE, y * SIDE + x) for y in range(SIDE) for x in range(SIDE)]
-    return lax.ppermute(value, "col", pairs)
-
-
-def sum_weight(quarter, row_size, sides, far):
+def sum_weight(quarter, row_size):
     both = ("row", "col")
     col_size = SIDE * SIDE
     layers = row_size // Y_LO
@@ -187,8 +188,8 @@
     plane = [[z * near + i for i in range(near)] for z in range(layers)]
     pieces = quarter.reshape(Y_LO * SIDE, -1, quarter.shape[1])
     pieces = lax.all_to_all(pieces, both, 0, 0, axis_index_groups=mates)
-    pieces = lax.all_to_all(spread_sum(pieces, layers, sides), both, 0, 0, axis_index_groups=depth)
-    return lax.all_to_all(spread_sum(pieces, near, far), both, 0, 0, axis_index_groups=plane)
+    pieces = lax.all_to_all(spread_sum(pieces, layers), both, 0, 0, axis_index_groups=depth)
+    return lax.all_to_all(spread_sum(pieces, near), both, 0, 0, axis_index_groups=plane)
 
 
 def per_device(features, adj, col_index, weight, centroid, labels):
@@ -216,15 +217,12 @@
     there = lax.ppermute(here, "feat", [(0, 1), (1, 0)])
 
     parcels = lax.all_to_all(middle(here, there, turned), "col", 0, 0, axis_index_groups=ALONG_Y)
-    stride = parcels.shape[1]
-    column = parcels.reshape(-1, half)
-    parts = [column] + [from_x(column, dx) for dx in range(1, SIDE)]
-    which = (owner_x - lax.axis_index("col")) % SIDE
-    feature_grad = block_product(which, owner_y * stride + within, adj, parts)
-
-    sides, far = (parts[1], parts[3]), (parts[2],)
-    pieces = sum_weight(open_parcels(parcels, row_count), row_size, sides, far)
-    weight_grad = settle(feat, pieces, 1.0 / math.sqrt(node_count))
+    quarter, column = open_parcels(parcels, row_count)
+    column = column.reshape(-1, half)
+    gathered = lax.all_gather(column, "col", axis=0, tiled=True, axis_index_groups=ALONG_X)
+    feature_grad = block_product(offsets, offsets, adj, [gathered])
+
+    weight_grad = settle(feat, sum_weight(quarter, row_size), feature_grad, 1.0 / math.sqrt(node_count))
     return (weight_grad, feature_grad)
 
 

time: 170 us -> 156 us (0.918)
  starting transfers between devices: 48.8 us -> 20.9 us
  between operations: 0.77 us -> 14.1 us
  blocking collectives: 66.4 us -> 77.8 us
  waiting for transfers between devices: 36.9 us -> 25.9 us
  local copies, waits for them, and re-layouts: 3.31 us -> 5.81 us
    all_to_all x0 -> x1, blocking collectives: none -> 30 us  [sum_weight(): lax.all_to_all(spread_sum(pieces, layers), both, 0, 0, axis_index_groups=...]
    all_to_all x2 -> x1, starting transfers between devices: 25.6 us -> 5.49 us  [sum_weight(): lax.all_to_all(spread_sum(pieces, near), both, 0, 0, axis_index_groups=pl...]
    all_to_all x1, blocking collectives: 26.1 us -> 7.48 us  [sum_weight(): pieces = lax.all_to_all(pieces, both, 0, 0, axis_index_groups=mates)]
    all_to_all x2 -> x1, waiting for transfers between devices: 17.7 us -> 4.84 us  [sum_weight(): lax.all_to_all(spread_sum(pieces, near), both, 0, 0, axis_index_groups=pl...]
    ppermute x3 -> x0, starting transfers between devices: 7.8 us -> none  [from_x(): return lax.ppermute(value, 'col', pairs)]
    unnamed x12 -> x18, local copies, waits for them, and re-layouts: 0.03 us -> 2.53 us
  transfers between devices with their start and end apart: 7 -> 4, of which waited for: 4 -> 4; matrix products, arithmetic and copies ran while one was open for 2% -> 1% of each run, Pallas kernels for 2% -> 2%
where the time goes in v5:
time: 156 us; the launch traced here: 153 us
  blocking collectives  77.8 us (50%)
  waiting for transfers between devices  25.9 us (17%)
  starting transfers between devices  20.9 us (13%)
  between operations  14.1 us (9%)
  Pallas kernels  7.41 us (5%)
  local copies, waits for them, and re-layouts  5.81 us (4%)
    all_to_all x1, blocking collectives, sum_weight(): lax.all_to_all(spread_sum(pieces, layers), both, 0, 0, axis_index_groups=...  30 us
    all_to_all x1, blocking collectives, per_device(): lax.all_to_all(middle(here, there, turned), 'col', 0, 0, axis_index_group...  20.5 us
    all_to_all x1, blocking collectives, to_all(): return lax.all_to_all(copies, axis, 0, 0, axis_index_groups=groups)  19.9 us
    all_to_all x1, waiting for transfers between devices, to_all(): return lax.all_to_all(copies, axis, 0, 0, axis_index_groups=groups)  19.4 us
    ppermute x1, starting transfers between devices, per_device(): there = lax.ppermute(here, 'feat', [(0, 1), (1, 0)])  8.53 us
    all_to_all x1, blocking collectives, sum_weight(): pieces = lax.all_to_all(pieces, both, 0, 0, axis_index_groups=mates)  7.48 us
    all_to_all x1, starting transfers between devices, to_all(): return lax.all_to_all(copies, axis, 0, 0, axis_index_groups=groups)  6.88 us
    all_to_all x1, starting transfers between devices, sum_weight(): lax.all_to_all(spread_sum(pieces, near), both, 0, 0, axis_index_groups=pl...  5.49 us
  transfers between devices with their start and end apart: 4, of which 4 were waited for; matrix products, arithmetic and copies ran while one was open for 1% of the time, Pallas kernels for 2%

profile of v5, /device:TPU:1, one launch (start us, length us, event | category | flops | bytes accessed | tf_op | source)
XLA Modules:
  0.0 153.3 jit_solution(14521719527007638366)
XLA Ops:
  7.2 1.0 broadcast_in_dim.6
  8.2 19.9 %all_to_all.30 = bf16[4,512,128]{2,1,0:T(8,128)(2,1)S(1)} all-to-all(bf16[4,512,128]{2,1,0:T(8,128)(2,1)S(1)} %broadcast_in_dim.6), channel_id=1, replica_groups={{0,8,16,24},{2,10,18,26},{4,12,20,28},{6,14,22,30},{1,9,17,25},{3,11,19..., dimensions={0} | all-to-all | bytes 1048576 | tf_op jit(solution)/shard_map/all_to_all | solution.py:170
  28.1 1.6 %broadcast_in_dim.8 = bf16[4,2048,128]{2,1,0:T(8,128)(2,1)} broadcast(bf16[2048,128]{1,0:T(8,128)(2,1)S(1)} %bitcast.8), dimensions={1,2} | broadcast | bytes 2621440 | tf_op jit(solution)/shard_map/broadcast_in_dim | solution.py:169
  29.7 6.9 %all-to-all-start.1 = ((bf16[4,2048,128]{2,1,0:T(8,128)(2,1)}), bf16[4,2048,128]{2,1,0:T(8,128)(2,1)S(1)}, u32[]{:S(2)}, u32[]{:S(2)}) async-start(bf16[4,2048,128]{2,1,0:T(8,128)(2,1)} %broadcast_in_dim.8), calls=%async_computation.1 | async-start | bytes 4194304 | tf_op jit(solution)/shard_map/all_to_all | solution.py:170
  36.6 0.7 fusion.15
  37.3 0.5 fusion.1.rest_1_
  37.8 19.4 %all-to-all-done.1 = bf16[4,2048,128]{2,1,0:T(8,128)(2,1)S(1)} async-done(((bf16[4,2048,128]{2,1,0:T(8,128)(2,1)}), bf16[4,2048,128]{2,1,0:T(8,128)(2,1)S(1)}, u32[]{:S(2)}, u32[]{:S(2)}) %all-to-all-start.1) | async-done | bytes 2097184 | tf_op jit(solution)/shard_map/all_to_all | solution.py:170
  57.2 1.8 %block_product.2.here_ref = bf16[1024,128]{1,0:T(8,128)(2,1)} custom-call(s32[4,8]{1,0:T(4,128)S(1)} %fusion.10.which_ref.offset_ref, s32[4,8]{1,0:T(4,128)S(1)} %fusion.10.which_ref.offset_ref, bf16[4,8,128,128]{3,2,1,0:T(8,128)(2,1)S(1)} %copy-done.1, bf16[8192,128]{1,0:T(8,128)(2,1)S(1)} %bitcast.6, bf16[512,128]{1,0:T(8,128)(2,1)S(1)} %fusion.1.rest_1_), custom_call_target="tpu_custom_call" | custom-call | flops 134217728 | bytes 2097152 | tf_op jit(solution)/shard_map/block_product/pallas_call | solution.py:44
  59.1 8.5 %collective-permute-start = (bf16[1024,128]{1,0:T(8,128)(2,1)}, bf16[1024,128]{1,0:T(8,128)(2,1)S(1)}, u32[]{:S(2)}, u32[]{:S(2)}) collective-permute-start(bf16[1024,128]{1,0:T(8,128)(2,1)} %block_product.2.here_ref), channel_id=1, source_target_pairs={{0,1},{1,0},{2,3},{3,2},{4,5},{5,4},{6,7},{7,6},{8,9},{9,8},{10,11... | collective-permute-start | bytes 786440 | tf_op jit(solution)/shard_map/ppermute | solution.py:217
  67.6 0.8 fusion.4.weight_ref
  68.5 0.5 collective-permute-done.there_ref
  68.9 1.6 %middle.1 = bf16[4,640,128]{2,1,0:T(8,128)(2,1)S(1)} custom-call(bf16[1024,128]{1,0:T(8,128)(2,1)} %block_product.2.here_ref, bf16[1024,128]{1,0:T(8,128)(2,1)S(1)} %collective-permute-done.there_ref, bf16[256,256]{1,0:T(8,128)(2,1)S(1)} %fusion.4.weight_ref), custom_call_target="tpu_custom_call" | custom-call | flops 134217728 | bytes 786432 | tf_op jit(solution)/shard_map/middle/pallas_call | solution.py:91
  70.5 20.5 %all_to_all.31.parcels_ref = bf16[4,640,128]{2,1,0:T(8,128)(2,1)S(1)} all-to-all(bf16[4,640,128]{2,1,0:T(8,128)(2,1)S(1)} %middle.1), channel_id=1, replica_groups={{0,8,16,24},{2,10,18,26},{4,12,20,28},{6,14,22,30},{1,9,17,25},{3,11,19..., dimensions={0} | all-to-all | bytes 1310720 | tf_op jit(solution)/shard_map/all_to_all | solution.py:219
  91.0 0.8 open_parcels.1
  91.9 7.5 %all_to_all.32.pieces_ref = f32[8,8,128]{2,1,0:T(8,128)S(1)} all-to-all(f32[8,8,128]{2,1,0:T(8,128)S(1)} %bitcast.7), channel_id=1, replica_groups={{0,2,4,6,32,34,36,38},{8,10,12,14,40,42,44,46},{16,18,20,22,48,50,52,54..., dimensions={0} | all-to-all | bytes 65536 | tf_op jit(solution)/shard_map/all_to_all | solution.py:190
  99.4 30.0 %all_to_all.33.pieces_ref = f32[16,8,128]{2,1,0:T(8,128)S(1)} all-to-all(f32[16,8,128]{2,1,0:T(8,128)S(1)} %spread_sum.2), channel_id=1, replica_groups={{0,64,128,192,256,320,384,448,512,576,640,704,768,832,896,960},{2,66,13..., dimensions={0} | all-to-all | bytes 131072 | tf_op jit(solution)/shard_map/all_to_all | solution.py:191
  129.3 0.7 spread_sum.3
  130.0 5.5 %all-to-all-start.5 = ((f32[32,8,128]{2,1,0:T(8,128)}), f32[32,8,128]{2,1,0:T(8,128)S(1)}, u32[]{:S(2)}, u32[]{:S(2)}) async-start(f32[32,8,128]{2,1,0:T(8,128)} %spread_sum.3), calls=%async_computation.5 | async-start | bytes 262144 | tf_op jit(solution)/shard_map/all_to_all | solution.py:192
  135.5 1.2 all-gather.2.cloned.1.call-done.rest_0_
  136.7 1.6 %copy-done.2 = bf16[8192,128]{1,0:T(8,128)(2,1)S(1)} copy-done((bf16[8192,128]{1,0:T(8,128)(2,1)S(1)}, bf16[8192,128]{1,0:T(8,128)(2,1)}, u32[]{:S(2)}) %copy-start.2) | copy-done | bytes 2097176
  138.3 1.8 %block_product.3.after_ref = bf16[512,128]{1,0:T(8,128)(2,1)} custom-call(s32[4,8]{1,0:T(4,128)S(1)} %fusion.10.which_ref.offset_ref, s32[4,8]{1,0:T(4,128)S(1)} %fusion.10.which_ref.offset_ref, bf16[4,8,128,128]{3,2,1,0:T(8,128)(2,1)S(1)} %copy-done.1, bf16[8192,128]{1,0:T(8,128)(2,1)S(1)} %copy-done.2), custom_call_target="tpu_custom_call" | custom-call | flops 134217728 | bytes 2097152 | tf_op jit(solution)/shard_map/block_product/pallas_call | solution.py:44
  140.1 4.8 %all-to-all-done.5.pieces_ref = f32[32,8,128]{2,1,0:T(8,128)S(1)} async-done(((f32[32,8,128]{2,1,0:T(8,128)}), f32[32,8,128]{2,1,0:T(8,128)S(1)}, u32[]{:S(2)}, u32[]{:S(2)}) %all-to-all-start.5) | async-done | bytes 131104 | tf_op jit(solution)/shard_map/all_to_all | solution.py:192
  144.9 0.9 copy-done.3
  145.8 0.7 settle.1
  (21 shorter events, 0.1 us)
Async XLA Ops:
  7.2 30.1 %copy-start = (bf16[1024,128]{1,0:T(8,128)(2,1)S(1)}, bf16[1024,128]{1,0:T(8,128)(2,1)}, u32[]{:S(2)}) copy-start(bf16[1024,128]{1,0:T(8,128)(2,1)} %param.10) | copy-start | bytes 786436
  29.7 6.9 %copy-start.7 = (s32[4,8]{1,0:T(4,128)S(1)}, s32[4,8]{1,0:T(4,128)}, u32[]{:S(2)}) copy-start(s32[4,8]{1,0:T(4,128)} %param.8) | copy-start | bytes 388
  29.7 6.9 %copy-start.6 = (bf16[256,256]{1,0:T(8,128)(2,1)S(1)}, bf16[256,256]{1,0:T(8,128)(2,1)}, u32[]{:S(2)}) copy-start(bf16[256,256]{1,0:T(8,128)(2,1)} %param.9) | copy-start | bytes 393220
  29.7 7.6 %copy-start.8 = (s32[512]{0:T(512)S(1)}, s32[512]{0:T(512)}, u32[]{:S(2)}) copy-start(s32[512]{0:T(512)} %param.11) | copy-start | bytes 6148
  29.7 27.5 %copy-start.1 = (bf16[4,8,128,128]{3,2,1,0:T(8,128)(2,1)S(1)}, bf16[4,8,128,128]{3,2,1,0:T(8,128)(2,1)}, u32[]{:S(2)}) copy-start(bf16[4,8,128,128]{3,2,1,0:T(8,128)(2,1)} %adj_ref.3) | copy-start | bytes 3145732
  29.7 27.5 %all-to-all-start.1 = ((bf16[4,2048,128]{2,1,0:T(8,128)(2,1)}), bf16[4,2048,128]{2,1,0:T(8,128)(2,1)S(1)}, u32[]{:S(2)}, u32[]{:S(2)}) async-start(bf16[4,2048,128]{2,1,0:T(8,128)(2,1)} %broadcast_in_dim.8), calls=%async_computation.1 | async-start | bytes 4194304 | tf_op jit(solution)/shard_map/all_to_all | solution.py:170
  36.6 100.1 %all-gather.2.cloned.1.call-start = ((), (), s32[]{:S(2)}) async-start(), calls=%async_computation.6 | async-start | bytes 2621440 | tf_op jit(solution)/shard_map/all_gather | solution.py:222
  57.2 10.4 %copy-start.4 = (bf16[128,256]{1,0:T(8,128)(2,1)S(1)}, bf16[128,256]{1,0:T(8,128)(2,1)}, u32[]{:S(2)}) copy-start(bf16[128,256]{1,0:T(8,128)(2,1)} %get-tuple-element.6) | copy-start | bytes 196612
  57.2 10.4 %copy-start.5 = (bf16[128,256]{1,0:T(8,128)(2,1)S(1)}, bf16[128,256]{1,0:T(8,128)(2,1)}, u32[]{:S(2)}) copy-start(bf16[128,256]{1,0:T(8,128)(2,1)} %get-tuple-element.7) | copy-start | bytes 196612
  59.1 9.9 %collective-permute-start = (bf16[1024,128]{1,0:T(8,128)(2,1)}, bf16[1024,128]{1,0:T(8,128)(2,1)S(1)}, u32[]{:S(2)}, u32[]{:S(2)}) collective-permute-start(bf16[1024,128]{1,0:T(8,128)(2,1)} %block_product.2.here_ref), channel_id=1, source_target_pairs={{0,1},{1,0},{2,3},{3,2},{4,5},{5,4},{6,7},{7,6},{8,9},{9,8},{10,11... | collective-permute-start | bytes 786440 | tf_op jit(solution)/shard_map/ppermute | solution.py:217
  130.0 14.9 %all-to-all-start.5 = ((f32[32,8,128]{2,1,0:T(8,128)}), f32[32,8,128]{2,1,0:T(8,128)S(1)}, u32[]{:S(2)}, u32[]{:S(2)}) async-start(f32[32,8,128]{2,1,0:T(8,128)} %spread_sum.3), calls=%async_computation.5 | async-start | bytes 262144 | tf_op jit(solution)/shard_map/all_to_all | solution.py:192
  136.7 1.6 %copy-start.2 = (bf16[8192,128]{1,0:T(8,128)(2,1)S(1)}, bf16[8192,128]{1,0:T(8,128)(2,1)}, u32[]{:S(2)}) copy-start(bf16[8192,128]{1,0:T(8,128)(2,1)} %all-gather.2.cloned.1.call-done.rest_0_) | copy-start | bytes 6291460
  144.9 0.9 copy-start.3
Sparse Core Ops, SparseCore 0:
  92.0 44.6 all-gather.1

commit v6 on v5

--- a/solution.py
+++ b/solution.py
@@ -9,6 +9,9 @@
 from jax.sharding import PartitionSpec as P
 
 SIDE = 4
+WHOLE = pl.BlockSpec(memory_space=pltpu.VMEM)
+SMALL = pltpu.CompilerParams(vmem_limit_bytes=4 << 20)
+LARGE = 56 << 20
 Y_LO = 2
 
 
@@ -55,6 +58,79 @@
         ),
         name="block_product",
     )(which, offsets, adj, *parts, *carried)
+
+
+def fetch_kernel(offset_ref, feat_ref, adj_ref, panel_ref, out_ref, same_ref, adj_held, held, adj_sems, panel_sems):
+    block_rows, nonzero, block, _ = adj_held.shape
+    same_ref[0] = feat_ref[0]
+
+    def adj_copy(r):
+        return pltpu.make_async_copy(adj_ref.at[r], adj_held.at[r], adj_sems.at[r])
+
+    def panel_copy(r, k):
+        start = pl.multiple_of(offset_ref[r, k], block)
+        return pltpu.make_async_copy(
+            panel_ref.at[pl.ds(start, block)], held.at[r, pl.ds(k * block, block)], panel_sems.at[r, k]
+        )
+
+    for r in range(block_rows):
+        for k in range(nonzero):
+            panel_copy(r, k).start()
+        adj_copy(r).start()
+    for r in range(block_rows):
+        for k in range(nonzero):
+            panel_copy(r, k).wait()
+        adj_copy(r).wait()
+        left = jnp.concatenate([adj_held[r, k] for k in range(nonzero)], axis=1)
+        total = jnp.dot(left, held[r], preferred_element_type=jnp.float32)
+        out_ref[pl.ds(r * block, block), :] = total.astype(out_ref.dtype)
+
+
+def fetched_product(offsets, feat, adj, panels):
+    block_rows, nonzero, block, _ = adj.shape
+    width = panels.shape[1]
+    return pl.pallas_call(
+        fetch_kernel,
+        out_shape=(
+            jax.ShapeDtypeStruct((block_rows * block, width), jnp.bfloat16),
+            jax.ShapeDtypeStruct((1,), jnp.int32),
+        ),
+        in_specs=[pl.BlockSpec(memory_space=pltpu.SMEM)] * 2 + [pl.BlockSpec(memory_space=pl.ANY)] * 2,
+        out_specs=(WHOLE, pl.BlockSpec(memory_space=pltpu.SMEM)),
+        scratch_shapes=[
+            pltpu.VMEM(adj.shape, adj.dtype),
+            pltpu.VMEM((block_rows, nonzero * block, width), jnp.bfloat16),
+            pltpu.SemaphoreType.DMA((block_rows,)),
+            pltpu.SemaphoreType.DMA((block_rows, nonzero)),
+        ],
+        compiler_params=pltpu.CompilerParams(vmem_limit_bytes=LARGE),
+        cost_estimate=pl.CostEstimate(
+            flops=2 * block_rows * nonzero * block * block * width,
+            bytes_accessed=2 * (adj.size + block_rows * nonzero * block * width),
+            transcendentals=0,
+        ),
+        name="fetched_product",
+    )(offsets, feat.reshape(1), adj, panels)
+
+
+def copies_kernel(value_ref, out_ref, sems):
+    copies = [pltpu.make_async_copy(value_ref, out_ref.at[i], sems.at[i]) for i in range(out_ref.shape[0])]
+    for copy in copies:
+        copy.start()
+    for copy in copies:
+        copy.wait()
+
+
+def copies_of(value, count):
+    return pl.pallas_call(
+        copies_kernel,
+        out_shape=jax.ShapeDtypeStruct((count, *value.shape), value.dtype),
+        in_specs=[pl.BlockSpec(memory_space=pl.ANY)],
+        out_specs=pl.BlockSpec(memory_space=pl.ANY),
+        scratch_shapes=[pltpu.SemaphoreType.DMA((count,))],
+        compiler_params=SMALL,
+        name="copies_of",
+    )(value)
 
 
 def middle_kernel(here_ref, there_ref, weight_ref, parcel_ref):
@@ -99,10 +175,6 @@
     )(here, there, weight)
 
 
-WHOLE = pl.BlockSpec(memory_space=pltpu.VMEM)
-SMALL = pltpu.CompilerParams(vmem_limit_bytes=4 << 20)
-
-
 def open_kernel(parcels_ref, quarter_ref, column_ref):
     skip = parcels_ref.shape[1] - 2 * quarter_ref.shape[0]
     half = (parcels_ref.shape[1] - skip) // 2
@@ -145,7 +217,7 @@
     )(pieces, *after)
 
 
-def settle_kernel(scale, feat_ref, pieces_ref, after_ref, out_ref):
+def settle_kernel(scale, feat_ref, pieces_ref, out_ref):
     halves, half = out_ref.shape[1] // pieces_ref.shape[2], pieces_ref.shape[2]
     per_half = pieces_ref.shape[0] // halves
     for index in range(halves):
@@ -153,16 +225,16 @@
         out_ref[:, index * half : (index + 1) * half] = values.reshape(out_ref.shape[0], half)
 
 
-def settle(feat, pieces, after, scale):
+def settle(feat, pieces, scale):
     count, rows, half = pieces.shape
     return pl.pallas_call(
         functools.partial(settle_kernel, scale),
         out_shape=jax.ShapeDtypeStruct((count * rows // 2, 2 * half), pieces.dtype),
-        in_specs=[pl.BlockSpec(memory_space=pltpu.SMEM), WHOLE, pl.BlockSpec(memory_space=pl.ANY)],
+        in_specs=[pl.BlockSpec(memory_space=pltpu.SMEM), WHOLE],
         out_specs=WHOLE,
         compiler_params=SMALL,
         name="settle",
-    )(feat.reshape(1), pieces, after)
+    )(feat, pieces)
 
 
 def to_all(value, axis, count, groups=None):
@@ -211,7 +283,7 @@
     turned = jnp.where(feat == 0, weight, swapped)
 
     column = to_all(features, "col", SIDE, ALONG_Y).reshape(-1, half)
-    panels = to_all(column, "col", SIDE, ALONG_X).reshape(-1, half)
+    panels = lax.all_to_all(copies_of(column, SIDE), "col", 0, 0, axis_index_groups=ALONG_X).reshape(-1, half)
     offsets = (owner_x * SIDE + owner_y) * row_count + within
     here = block_product(offsets, offsets, adj, [panels], (target,))
     there = lax.ppermute(here, "feat", [(0, 1), (1, 0)])
@@ -220,9 +292,9 @@
     quarter, column = open_parcels(parcels, row_count)
     column = column.reshape(-1, half)
     gathered = lax.all_gather(column, "col", axis=0, tiled=True, axis_index_groups=ALONG_X)
-    feature_grad = block_product(offsets, offsets, adj, [gathered])
-
-    weight_grad = settle(feat, sum_weight(quarter, row_size), feature_grad, 1.0 / math.sqrt(node_count))
+    feature_grad, same = fetched_product(offsets, feat, adj, gathered)
+
+    weight_grad = settle(same, sum_weight(quarter, row_size), 1.0 / math.sqrt(node_count))
     return (weight_grad, feature_grad)
 
 

time: 156 us -> 156 us (level)
  Pallas kernels: 7.41 us -> 11.5 us
  local copies, waits for them, and re-layouts: 5.81 us -> 1.73 us
    pallas_call x0 -> x2, Pallas kernels: none -> 5.33 us  [the longest x1 3.96 us: fetched_product(): pl.pallas_call(fetch_kernel, out_shape=(jax.ShapeDtypeStruct((block_rows...]
    unnamed x18 -> x16, local copies, waits for them, and re-layouts: 2.53 us -> 0.05 us
    pallas_call x2 -> x1, Pallas kernels: 3.62 us -> 1.83 us  [block_product(): pl.pallas_call(functools.partial(product_kernel, len(parts)), out_shape=j...]
    broadcast_in_dim x2 -> x1, local copies, waits for them, and re-layouts: 2.62 us -> 1.01 us  [to_all(): copies = jnp.broadcast_to(value[None], (count, *value.shape))]
  transfers between devices with their start and end apart: 4 -> 4, of which waited for: 4 -> 4; matrix products, arithmetic and copies ran while one was open for 1% -> 1% of each run, Pallas kernels for 2% -> 3%
where the time goes in v6:
time: 156 us; the launch traced here: 153 us
  blocking collectives  77.8 us (50%)
  waiting for transfers between devices  25.3 us (16%)
  starting transfers between devices  20.9 us (13%)
  between operations  14.2 us (9%)
  Pallas kernels  11.5 us (7%)
  local copies, waits for them, and re-layouts  1.73 us (1%)
    all_to_all x1, blocking collectives, sum_weight(): lax.all_to_all(spread_sum(pieces, layers), both, 0, 0, axis_index_groups=...  29.9 us
    all_to_all x1, blocking collectives, per_device(): lax.all_to_all(middle(here, there, turned), 'col', 0, 0, axis_index_group...  20.5 us
    all_to_all x1, blocking collectives, to_all(): return lax.all_to_all(copies, axis, 0, 0, axis_index_groups=groups)  19.9 us
    all_to_all x1, waiting for transfers between devices, per_device(): lax.all_to_all(copies_of(column, SIDE), 'col', 0, 0, axis_index_groups=AL...  19.4 us
    ppermute x1, starting transfers between devices, per_device(): there = lax.ppermute(here, 'feat', [(0, 1), (1, 0)])  8.53 us
    all_to_all x1, blocking collectives, sum_weight(): pieces = lax.all_to_all(pieces, both, 0, 0, axis_index_groups=mates)  7.48 us
    all_to_all x1, starting transfers between devices, per_device(): lax.all_to_all(copies_of(column, SIDE), 'col', 0, 0, axis_index_groups=AL...  6.88 us
    all_to_all x1, starting transfers between devices, sum_weight(): lax.all_to_all(spread_sum(pieces, near), both, 0, 0, axis_index_groups=pl...  5.49 us
  transfers between devices with their start and end apart: 4, of which 4 were waited for; matrix products, arithmetic and copies ran while one was open for 1% of the time, Pallas kernels for 3%

profile of v6, /device:TPU:1, one launch (start us, length us, event | category | flops | bytes accessed | tf_op | source)
XLA Modules:
  0.0 152.8 jit_solution(4717752745318999022)
XLA Ops:
  7.2 0.0 copy-start
  7.2 1.0 broadcast_in_dim.2
  8.2 19.9 %all_to_all.30 = bf16[4,512,128]{2,1,0:T(8,128)(2,1)S(1)} all-to-all(bf16[4,512,128]{2,1,0:T(8,128)(2,1)S(1)} %broadcast_in_dim.2), channel_id=1, replica_groups={{0,8,16,24},{2,10,18,26},{4,12,20,28},{6,14,22,30},{1,9,17,25},{3,11,19..., dimensions={0} | all-to-all | bytes 1048576 | tf_op jit(solution)/shard_map/all_to_all | solution.py:242
  28.1 1.4 copies_of.1
  29.5 6.9 %all-to-all-start.1 = ((bf16[4,2048,128]{2,1,0:T(8,128)(2,1)}), bf16[4,2048,128]{2,1,0:T(8,128)(2,1)S(1)}, u32[]{:S(2)}, u32[]{:S(2)}) async-start(bf16[4,2048,128]{2,1,0:T(8,128)(2,1)} %copies_of.1), calls=%async_computation.1 | async-start | bytes 4194304 | tf_op jit(solution)/shard_map/all_to_all | solution.py:286
  36.4 0.7 fusion.15
  37.1 0.5 fusion.1.rest_1_
  37.6 19.4 %all-to-all-done.1 = bf16[4,2048,128]{2,1,0:T(8,128)(2,1)S(1)} async-done(((bf16[4,2048,128]{2,1,0:T(8,128)(2,1)}), bf16[4,2048,128]{2,1,0:T(8,128)(2,1)S(1)}, u32[]{:S(2)}, u32[]{:S(2)}) %all-to-all-start.1) | async-done | bytes 2097184 | tf_op jit(solution)/shard_map/all_to_all | solution.py:286
  57.0 1.8 %block_product.1.here_ref = bf16[1024,128]{1,0:T(8,128)(2,1)} custom-call(s32[4,8]{1,0:T(4,128)S(1)} %fusion.10.which_ref.offset_ref, s32[4,8]{1,0:T(4,128)S(1)} %fusion.10.which_ref.offset_ref, bf16[4,8,128,128]{3,2,1,0:T(8,128)(2,1)S(1)} %copy-done.1, bf16[8192,128]{1,0:T(8,128)(2,1)S(1)} %bitcast.6, bf16[512,128]{1,0:T(8,128)(2,1)S(1)} %fusion.1.rest_1_), custom_call_target="tpu_custom_call" | custom-call | flops 134217728 | bytes 2097152 | tf_op jit(solution)/shard_map/block_product/pallas_call | solution.py:47
  58.9 8.5 %collective-permute-start = (bf16[1024,128]{1,0:T(8,128)(2,1)}, bf16[1024,128]{1,0:T(8,128)(2,1)S(1)}, u32[]{:S(2)}, u32[]{:S(2)}) collective-permute-start(bf16[1024,128]{1,0:T(8,128)(2,1)} %block_product.1.here_ref), channel_id=1, source_target_pairs={{0,1},{1,0},{2,3},{3,2},{4,5},{5,4},{6,7},{7,6},{8,9},{9,8},{10,11... | collective-permute-start | bytes 786440 | tf_op jit(solution)/shard_map/ppermute | solution.py:289
  67.4 0.8 fusion.4.weight_ref
  68.3 0.5 collective-permute-done.there_ref
  68.7 1.6 %middle.1 = bf16[4,640,128]{2,1,0:T(8,128)(2,1)S(1)} custom-call(bf16[1024,128]{1,0:T(8,128)(2,1)} %block_product.1.here_ref, bf16[1024,128]{1,0:T(8,128)(2,1)S(1)} %collective-permute-done.there_ref, bf16[256,256]{1,0:T(8,128)(2,1)S(1)} %fusion.4.weight_ref), custom_call_target="tpu_custom_call" | custom-call | flops 134217728 | bytes 786432 | tf_op jit(solution)/shard_map/middle/pallas_call | solution.py:167
  70.3 20.5 %all_to_all.31.parcels_ref = bf16[4,640,128]{2,1,0:T(8,128)(2,1)S(1)} all-to-all(bf16[4,640,128]{2,1,0:T(8,128)(2,1)S(1)} %middle.1), channel_id=1, replica_groups={{0,8,16,24},{2,10,18,26},{4,12,20,28},{6,14,22,30},{1,9,17,25},{3,11,19..., dimensions={0} | all-to-all | bytes 1310720 | tf_op jit(solution)/shard_map/all_to_all | solution.py:291
  90.8 0.8 open_parcels.1
  91.7 0.0 all-gather.2.cloned.1.call-update
  91.7 7.5 %all_to_all.32.pieces_ref = f32[8,8,128]{2,1,0:T(8,128)S(1)} all-to-all(f32[8,8,128]{2,1,0:T(8,128)S(1)} %bitcast.8), channel_id=1, replica_groups={{0,2,4,6,32,34,36,38},{8,10,12,14,40,42,44,46},{16,18,20,22,48,50,52,54..., dimensions={0} | all-to-all | bytes 65536 | tf_op jit(solution)/shard_map/all_to_all | solution.py:262
  99.2 29.9 %all_to_all.33.pieces_ref = f32[16,8,128]{2,1,0:T(8,128)S(1)} all-to-all(f32[16,8,128]{2,1,0:T(8,128)S(1)} %spread_sum.2), channel_id=1, replica_groups={{0,64,128,192,256,320,384,448,512,576,640,704,768,832,896,960},{2,66,13..., dimensions={0} | all-to-all | bytes 131072 | tf_op jit(solution)/shard_map/all_to_all | solution.py:263
  129.1 0.7 spread_sum.3
  129.8 5.5 %all-to-all-start.5 = ((f32[32,8,128]{2,1,0:T(8,128)}), f32[32,8,128]{2,1,0:T(8,128)S(1)}, u32[]{:S(2)}, u32[]{:S(2)}) async-start(f32[32,8,128]{2,1,0:T(8,128)} %spread_sum.3), calls=%async_computation.5 | async-start | bytes 262144 | tf_op jit(solution)/shard_map/all_to_all | solution.py:264
  135.3 1.2 all-gather.2.cloned.1.call-done.panel_ref
  136.5 4.0 %fetched_product.1 = (bf16[512,128]{1,0:T(8,128)(2,1)}, s32[1]{0:T(128)}) custom-call(s32[4,8]{1,0:T(4,128)} %copy-done.2, s32[1]{0:T(128)} %bitcast.feat_ref, bf16[4,8,128,128]{3,2,1,0:T(8,128)(2,1)} %adj_ref.3, bf16[8192,128]{1,0:T(8,128)(2,1)} %all-gather.2.cloned.1.call-done.panel_ref), custom_call_target="tpu_custom_call" | custom-call | flops 134217728 | bytes 2097152 | tf_op jit(solution)/shard_map/fetched_product/pallas_call | solution.py:92
  140.5 4.2 %all-to-all-done.5.pieces_ref = f32[32,8,128]{2,1,0:T(8,128)S(1)} async-done(((f32[32,8,128]{2,1,0:T(8,128)}), f32[32,8,128]{2,1,0:T(8,128)S(1)}, u32[]{:S(2)}, u32[]{:S(2)}) %all-to-all-start.5) | async-done | bytes 131104 | tf_op jit(solution)/shard_map/all_to_all | solution.py:264
  144.7 1.2 settle.1
  (19 shorter events, 0.1 us)
Async XLA Ops:
  7.2 29.9 %copy-start = (bf16[1024,128]{1,0:T(8,128)(2,1)S(1)}, bf16[1024,128]{1,0:T(8,128)(2,1)}, u32[]{:S(2)}) copy-start(bf16[1024,128]{1,0:T(8,128)(2,1)} %param.10) | copy-start | bytes 786436
  29.4 6.9 %copy-start.6 = (s32[4,8]{1,0:T(4,128)S(1)}, s32[4,8]{1,0:T(4,128)}, u32[]{:S(2)}) copy-start(s32[4,8]{1,0:T(4,128)} %param.8) | copy-start | bytes 388
  29.4 7.0 %copy-start.5 = (bf16[256,256]{1,0:T(8,128)(2,1)S(1)}, bf16[256,256]{1,0:T(8,128)(2,1)}, u32[]{:S(2)}) copy-start(bf16[256,256]{1,0:T(8,128)(2,1)} %param.9) | copy-start | bytes 393220
  29.5 7.6 %copy-start.7 = (s32[512]{0:T(512)S(1)}, s32[512]{0:T(512)}, u32[]{:S(2)}) copy-start(s32[512]{0:T(512)} %param.11) | copy-start | bytes 6148
  29.5 27.5 %copy-start.1 = (bf16[4,8,128,128]{3,2,1,0:T(8,128)(2,1)S(1)}, bf16[4,8,128,128]{3,2,1,0:T(8,128)(2,1)}, u32[]{:S(2)}) copy-start(bf16[4,8,128,128]{3,2,1,0:T(8,128)(2,1)} %adj_ref.3) | copy-start | bytes 3145732
  29.5 27.5 %all-to-all-start.1 = ((bf16[4,2048,128]{2,1,0:T(8,128)(2,1)}), bf16[4,2048,128]{2,1,0:T(8,128)(2,1)S(1)}, u32[]{:S(2)}, u32[]{:S(2)}) async-start(bf16[4,2048,128]{2,1,0:T(8,128)(2,1)} %copies_of.1), calls=%async_computation.1 | async-start | bytes 4194304 | tf_op jit(solution)/shard_map/all_to_all | solution.py:286
  36.4 100.1 %all-gather.2.cloned.1.call-start = ((), (), s32[]{:S(2)}) async-start(), calls=%async_computation.6 | async-start | bytes 2621440 | tf_op jit(solution)/shard_map/all_gather | solution.py:294
  36.4 22.4 %copy-start.2 = (s32[4,8]{1,0:T(4,128)}, s32[4,8]{1,0:T(4,128)S(1)}, u32[]{:S(2)}) copy-start(s32[4,8]{1,0:T(4,128)S(1)} %fusion.10.which_ref.offset_ref) | copy-start | bytes 388
  57.0 10.4 %copy-start.3 = (bf16[128,256]{1,0:T(8,128)(2,1)S(1)}, bf16[128,256]{1,0:T(8,128)(2,1)}, u32[]{:S(2)}) copy-start(bf16[128,256]{1,0:T(8,128)(2,1)} %get-tuple-element.10) | copy-start | bytes 196612
  57.0 10.4 %copy-start.4 = (bf16[128,256]{1,0:T(8,128)(2,1)S(1)}, bf16[128,256]{1,0:T(8,128)(2,1)}, u32[]{:S(2)}) copy-start(bf16[128,256]{1,0:T(8,128)(2,1)} %get-tuple-element.11) | copy-start | bytes 196612
  58.9 9.9 %collective-permute-start = (bf16[1024,128]{1,0:T(8,128)(2,1)}, bf16[1024,128]{1,0:T(8,128)(2,1)S(1)}, u32[]{:S(2)}, u32[]{:S(2)}) collective-permute-start(bf16[1024,128]{1,0:T(8,128)(2,1)} %block_product.1.here_ref), channel_id=1, source_target_pairs={{0,1},{1,0},{2,3},{3,2},{4,5},{5,4},{6,7},{7,6},{8,9},{9,8},{10,11... | collective-permute-start | bytes 786440 | tf_op jit(solution)/shard_map/ppermute | solution.py:289
  129.8 14.9 %all-to-all-start.5 = ((f32[32,8,128]{2,1,0:T(8,128)}), f32[32,8,128]{2,1,0:T(8,128)S(1)}, u32[]{:S(2)}, u32[]{:S(2)}) async-start(f32[32,8,128]{2,1,0:T(8,128)} %spread_sum.3), calls=%async_computation.5 | async-start | bytes 262144 | tf_op jit(solution)/shard_map/all_to_all | solution.py:264
Sparse Core Ops, SparseCore 0:
  91.8 44.6 all-gather.1

commit v7 on v4

--- a/solution.py
+++ b/solution.py
@@ -9,6 +9,7 @@
 from jax.sharding import PartitionSpec as P
 
 SIDE = 4
+BOTH = 2
 Y_LO = 2
 
 
@@ -57,7 +58,7 @@
     )(which, offsets, adj, *parts, *carried)
 
 
-def middle_kernel(here_ref, there_ref, weight_ref, partial_ref, back_ref):
+def middle_kernel(here_ref, there_ref, weight_ref, partial_ref, *back_refs):
     half = here_ref.shape[1]
     rows = here_ref.shape[0] // 2
     own = here_ref[:rows, :]
@@ -70,8 +71,10 @@
     back = lax.dot_general(
         grad_out, weight_ref[:half, :], (((1,), (1,)), ((), ())), preferred_element_type=jnp.float32
     ).astype(jnp.bfloat16)
-    for y in range(back_ref.shape[0]):
-        back_ref[y] = back
+    start = 0
+    for back_ref in back_refs:
+        back_ref[...] = back[start : start + back_ref.shape[0], :]
+        start += back_ref.shape[0]
     partial = lax.dot_general(own, grad_out, (((0,), (0,)), ((), ())), preferred_element_type=jnp.float32)
     for index in range(partial_ref.shape[0]):
         partial_ref[index] = partial[:, index * half : (index + 1) * half]
@@ -83,7 +86,7 @@
         middle_kernel,
         out_shape=(
             jax.ShapeDtypeStruct((weight.shape[1] // half, half, half), jnp.float32),
-            jax.ShapeDtypeStruct((SIDE, rows, half), jnp.bfloat16),
+            *[jax.ShapeDtypeStruct((rows // BOTH, half), jnp.bfloat16)] * BOTH,
         ),
         compiler_params=pltpu.CompilerParams(vmem_limit_bytes=14 << 20),
         cost_estimate=pl.CostEstimate(
@@ -179,10 +182,11 @@
     here = block_product(offsets, offsets, adj, [panels], (target,))
     there = lax.ppermute(here, "feat", [(0, 1), (1, 0)])
 
-    partial, back = middle(here, there, turned)
-    column = lax.all_to_all(back, "col", 0, 0, axis_index_groups=ALONG_Y).reshape(-1, half)
-    gathered = lax.all_gather(column, "col", axis=0, tiled=True, axis_index_groups=ALONG_X)
-    feature_grad = block_product(offsets, offsets, adj, [gathered])
+    partial, *backs = middle(here, there, turned)
+    gathered = [lax.all_gather(back, "col", axis=0, tiled=True) for back in backs]
+    within_rows = row_count // BOTH
+    part_offsets = owner * within_rows + within % within_rows
+    feature_grad = block_product(within // within_rows, part_offsets, adj, gathered)
 
     pieces = sum_weight(partial.reshape(Y_LO * col_size, -1, half), row_size)
     weight_grad = settle(feat, pieces, 1.0 / math.sqrt(node_count))

time: 159 us -> 226 us (1.42)
  waiting for transfers between devices: 19.9 us -> 104 us
  blocking collectives: 94.8 us -> 77.4 us
    all_gather x1 -> x2, waiting for transfers between devices: 0.01 us -> 83.4 us  [per_device(): lax.all_gather(back, 'col', axis=0, tiled=True)]
    all_to_all x1 -> x0, blocking collectives: 18.5 us -> none  [per_device(): lax.all_to_all(back, 'col', 0, 0, axis_index_groups=ALONG_Y)]
  transfers between devices with their start and end apart: 3 -> 4, of which waited for: 2 -> 4; matrix products, arithmetic and copies ran while one was open for 1% -> 1% of each run, Pallas kernels for 0% -> 0%
where the time goes in v7:
time: 226 us; the launch traced here: 225 us
  waiting for transfers between devices  104 us (46%)
  blocking collectives  77.4 us (34%)
  starting transfers between devices  15.5 us (7%)
  between operations  14.1 us (6%)
  Pallas kernels  6.93 us (3%)
  local copies, waits for them, and re-layouts  5.76 us (3%)
    all_gather x2, waiting for transfers between devices, per_device(): lax.all_gather(back, 'col', axis=0, tiled=True)  83.4 us
    all_to_all x1, blocking collectives, sum_weight(): lax.all_to_all(spread_sum(pieces, layers), both, 0, 0, axis_index_groups=...  30.1 us
    all_to_all x1, blocking collectives, to_all(): return lax.all_to_all(copies, axis, 0, 0, axis_index_groups=groups)  19.9 us
    all_to_all x1, waiting for transfers between devices, to_all(): return lax.all_to_all(copies, axis, 0, 0, axis_index_groups=groups)  19.4 us
    all_to_all x1, blocking collectives, sum_weight(): pieces = lax.all_to_all(pieces, both, 0, 0, axis_index_groups=plane)  14.2 us
    all_to_all x1, blocking collectives, sum_weight(): lax.all_to_all(spread_sum(pieces, near), both, 0, 0, axis_index_groups=pl...  13.3 us
    ppermute x1, starting transfers between devices, per_device(): there = lax.ppermute(here, 'feat', [(0, 1), (1, 0)])  8.53 us
    all_to_all x1, starting transfers between devices, to_all(): return lax.all_to_all(copies, axis, 0, 0, axis_index_groups=groups)  6.88 us
  transfers between devices with their start and end apart: 4, of which 4 were waited for; matrix products, arithmetic and copies ran while one was open for 1% of the time, Pallas kernels for 0%

profile of v7, /device:TPU:1, one launch (start us, length us, event | category | flops | bytes accessed | tf_op | source)
XLA Modules:
  0.0 225.1 jit_solution(8286266164523185091)
XLA Ops:
  7.2 1.0 broadcast_in_dim.6
  8.2 19.9 %all_to_all.25 = bf16[4,512,128]{2,1,0:T(8,128)(2,1)S(1)} all-to-all(bf16[4,512,128]{2,1,0:T(8,128)(2,1)S(1)} %broadcast_in_dim.6), channel_id=1, replica_groups={{0,8,16,24},{2,10,18,26},{4,12,20,28},{6,14,22,30},{1,9,17,25},{3,11,19..., dimensions={0} | all-to-all | bytes 1048576 | tf_op jit(solution)/shard_map/all_to_all | solution.py:143
  28.1 1.6 broadcast_in_dim.8
  29.7 6.9 %all-to-all-start.1 = ((bf16[4,2048,128]{2,1,0:T(8,128)(2,1)}), bf16[4,2048,128]{2,1,0:T(8,128)(2,1)S(1)}, u32[]{:S(2)}, u32[]{:S(2)}) async-start(bf16[4,2048,128]{2,1,0:T(8,128)(2,1)} %broadcast_in_dim.8), calls=%async_computation.1 | async-start | bytes 4194304 | tf_op jit(solution)/shard_map/all_to_all | solution.py:143
  36.6 0.7 fusion.18
  37.3 0.5 fusion.1.rest_1_
  37.8 19.4 %all-to-all-done.1 = bf16[4,2048,128]{2,1,0:T(8,128)(2,1)S(1)} async-done(((bf16[4,2048,128]{2,1,0:T(8,128)(2,1)}), bf16[4,2048,128]{2,1,0:T(8,128)(2,1)S(1)}, u32[]{:S(2)}, u32[]{:S(2)}) %all-to-all-start.1) | async-done | bytes 2097184 | tf_op jit(solution)/shard_map/all_to_all | solution.py:143
  57.2 1.8 block_product.2.here_ref
  59.0 8.5 %collective-permute-start = (bf16[1024,128]{1,0:T(8,128)(2,1)}, bf16[1024,128]{1,0:T(8,128)(2,1)S(1)}, u32[]{:S(2)}, u32[]{:S(2)}) collective-permute-start(bf16[1024,128]{1,0:T(8,128)(2,1)} %block_product.2.here_ref), channel_id=1, source_target_pairs={{0,1},{1,0},{2,3},{3,2},{4,5},{5,4},{6,7},{7,6},{8,9},{9,8},{10,11... | collective-permute-start | bytes 786440 | tf_op jit(solution)/shard_map/ppermute | solution.py:183
  67.6 0.8 fusion.4.weight_ref
  68.4 0.5 collective-permute-done.there_ref
  68.9 2.1 middle.1
  71.1 0.0 all-gather.3.cloned.1.call-update
  71.1 0.0 all-gather.5.cloned.1.call-start
  71.1 0.7 all-gather.5.cloned.1.call-update
  71.8 14.2 %all_to_all.26.pieces_ref = f32[32,8,128]{2,1,0:T(8,128)S(1)} all-to-all(f32[32,8,128]{2,1,0:T(8,128)S(1)} %bitcast.6), channel_id=1, replica_groups={{0,2,4,6,8,10,12,14,16,18,20,22,24,26,28,30,32,34,36,38,40,42,44,46,48,..., dimensions={0} | all-to-all | bytes 262144 | tf_op jit(solution)/shard_map/all_to_all | solution.py:156
  86.1 30.1 %all_to_all.27.pieces_ref = f32[16,8,128]{2,1,0:T(8,128)S(1)} all-to-all(f32[16,8,128]{2,1,0:T(8,128)S(1)} %spread_sum.2), channel_id=1, replica_groups={{0,64,128,192,256,320,384,448,512,576,640,704,768,832,896,960},{2,66,13..., dimensions={0} | all-to-all | bytes 131072 | tf_op jit(solution)/shard_map/all_to_all | solution.py:157
  116.2 13.3 %all_to_all.28.pieces_ref = f32[32,8,128]{2,1,0:T(8,128)S(1)} all-to-all(f32[32,8,128]{2,1,0:T(8,128)S(1)} %spread_sum.3), channel_id=1, replica_groups={{0,2,4,6,8,10,12,14,16,18,20,22,24,26,28,30,32,34,36,38,40,42,44,46,48,..., dimensions={0} | all-to-all | bytes 262144 | tf_op jit(solution)/shard_map/all_to_all | solution.py:158
  129.5 0.7 settle.1
  130.2 12.1 %all-gather.3.cloned.1.call-done.rest_0_ = bf16[4096,128]{1,0:T(8,128)(2,1)} async-done(((bf16[256,128]{1,0:T(8,128)(2,1)}), bf16[4096,128]{1,0:T(8,128)(2,1)}) %all-gather.3.cloned.1.call-update) | async-done | bytes 1048592 | tf_op jit(solution)/shard_map/all_gather | solution.py:186
  142.3 71.3 %all-gather.5.cloned.1.call-done.rest_1_ = bf16[4096,128]{1,0:T(8,128)(2,1)} async-done(((bf16[256,128]{1,0:T(8,128)(2,1)}), bf16[4096,128]{1,0:T(8,128)(2,1)}) %all-gather.5.cloned.1.call-update) | async-done | bytes 1048592 | tf_op jit(solution)/shard_map/all_gather | solution.py:186
  213.6 1.2 copy-done.2
  214.8 1.2 copy-done.3
  216.1 2.2 block_product.3
  (22 shorter events, 0.1 us)
Async XLA Ops:
  7.2 30.1 %copy-start = (bf16[1024,128]{1,0:T(8,128)(2,1)S(1)}, bf16[1024,128]{1,0:T(8,128)(2,1)}, u32[]{:S(2)}) copy-start(bf16[1024,128]{1,0:T(8,128)(2,1)} %param.10) | copy-start | bytes 786436
  29.7 6.9 %copy-start.7 = (s32[4,8]{1,0:T(4,128)S(1)}, s32[4,8]{1,0:T(4,128)}, u32[]{:S(2)}) copy-start(s32[4,8]{1,0:T(4,128)} %param.8) | copy-start | bytes 388
  29.7 6.9 %copy-start.6 = (bf16[256,256]{1,0:T(8,128)(2,1)S(1)}, bf16[256,256]{1,0:T(8,128)(2,1)}, u32[]{:S(2)}) copy-start(bf16[256,256]{1,0:T(8,128)(2,1)} %param.9) | copy-start | bytes 393220
  29.7 7.6 %copy-start.8 = (s32[512]{0:T(512)S(1)}, s32[512]{0:T(512)}, u32[]{:S(2)}) copy-start(s32[512]{0:T(512)} %param.11) | copy-start | bytes 6148
  29.7 27.5 %copy-start.1 = (bf16[4,8,128,128]{3,2,1,0:T(8,128)(2,1)S(1)}, bf16[4,8,128,128]{3,2,1,0:T(8,128)(2,1)}, u32[]{:S(2)}) copy-start(bf16[4,8,128,128]{3,2,1,0:T(8,128)(2,1)} %adj_ref.3) | copy-start | bytes 3145732
  29.7 27.5 %all-to-all-start.1 = ((bf16[4,2048,128]{2,1,0:T(8,128)(2,1)}), bf16[4,2048,128]{2,1,0:T(8,128)(2,1)S(1)}, u32[]{:S(2)}, u32[]{:S(2)}) async-start(bf16[4,2048,128]{2,1,0:T(8,128)(2,1)} %broadcast_in_dim.8), calls=%async_computation.1 | async-start | bytes 4194304 | tf_op jit(solution)/shard_map/all_to_all | solution.py:143
  36.6 105.7 %all-gather.3.cloned.1.call-start = ((), (), s32[]{:S(2)}) async-start(), calls=%async_computation.5 | async-start | bytes 1114112 | tf_op jit(solution)/shard_map/all_gather | solution.py:186
  57.2 10.4 %copy-start.4 = (bf16[128,256]{1,0:T(8,128)(2,1)S(1)}, bf16[128,256]{1,0:T(8,128)(2,1)}, u32[]{:S(2)}) copy-start(bf16[128,256]{1,0:T(8,128)(2,1)} %get-tuple-element.11) | copy-start | bytes 196612
  57.2 10.4 %copy-start.5 = (bf16[128,256]{1,0:T(8,128)(2,1)S(1)}, bf16[128,256]{1,0:T(8,128)(2,1)}, u32[]{:S(2)}) copy-start(bf16[128,256]{1,0:T(8,128)(2,1)} %get-tuple-element.12) | copy-start | bytes 196612
  59.0 9.9 %collective-permute-start = (bf16[1024,128]{1,0:T(8,128)(2,1)}, bf16[1024,128]{1,0:T(8,128)(2,1)S(1)}, u32[]{:S(2)}, u32[]{:S(2)}) collective-permute-start(bf16[1024,128]{1,0:T(8,128)(2,1)} %block_product.2.here_ref), channel_id=1, source_target_pairs={{0,1},{1,0},{2,3},{3,2},{4,5},{5,4},{6,7},{7,6},{8,9},{9,8},{10,11... | collective-permute-start | bytes 786440 | tf_op jit(solution)/shard_map/ppermute | solution.py:183
  71.1 142.5 %all-gather.5.cloned.1.call-start = ((), (), s32[]{:S(2)}) async-start(), calls=%async_computation.6 | async-start | bytes 1114112 | tf_op jit(solution)/shard_map/all_gather | solution.py:186
  213.6 1.2 copy-start.2
  214.8 1.2 copy-start.3
Sparse Core Ops, SparseCore 0:
  71.2 71.0 all-gather.2
  146.4 67.1 all-gather.4

commit v8 on v5

--- a/solution.py
+++ b/solution.py
@@ -9,43 +9,36 @@
 from jax.sharding import PartitionSpec as P
 
 SIDE = 4
+WHOLE = pl.BlockSpec(memory_space=pltpu.VMEM)
+SMALL = pltpu.CompilerParams(vmem_limit_bytes=4 << 20)
 Y_LO = 2
 
 
-def product_kernel(count, which_ref, offset_ref, adj_ref, *rest):
-    parts, carried = rest[:count], rest[count:-2]
-    out_ref, held = rest[-2:]
+def product_kernel(offset_ref, feat_ref, adj_ref, panels_ref, out_ref, same_ref, held):
     block_rows, nonzero, block, _ = adj_ref.shape
-
-    def place(part, r, k, start):
-        held[r, pl.ds(k * block, block), :] = part[pl.ds(start, block), :]
-
+    same_ref[0] = feat_ref[0]
     for r in range(block_rows):
         for k in range(nonzero):
             start = pl.multiple_of(offset_ref[r, k], block)
-            if count == 1:
-                place(parts[0], r, k, start)
-            else:
-                for index, part in enumerate(parts):
-                    pl.when(which_ref[r, k] == index)(functools.partial(place, part, r, k, start))
-    for array in carried:
-        out_ref[pl.ds(block_rows * block, array.shape[0]), :] = array[...]
+            held[r, pl.ds(k * block, block), :] = panels_ref[pl.ds(start, block), :]
     for r in range(block_rows):
         left = jnp.concatenate([adj_ref[r, k] for k in range(nonzero)], axis=1)
         total = jnp.dot(left, held[r], preferred_element_type=jnp.float32)
         out_ref[pl.ds(r * block, block), :] = total.astype(out_ref.dtype)
 
 
-def block_product(which, offsets, adj, parts, carried=()):
+def block_product(offsets, feat, adj, panels):
     block_rows, nonzero, block, _ = adj.shape
-    width = parts[0].shape[1]
-    rows = block_rows * block + sum(array.shape[0] for array in carried)
-    whole = pl.BlockSpec(memory_space=pltpu.VMEM)
-    return pl.pallas_call(
-        functools.partial(product_kernel, len(parts)),
-        out_shape=jax.ShapeDtypeStruct((rows, width), jnp.bfloat16),
-        in_specs=[pl.BlockSpec(memory_space=pltpu.SMEM)] * 2 + [whole] * (1 + len(parts) + len(carried)),
-        out_specs=whole,
+    width = panels.shape[1]
+    scalar = pl.BlockSpec(memory_space=pltpu.SMEM)
+    return pl.pallas_call(
+        product_kernel,
+        out_shape=(
+            jax.ShapeDtypeStruct((block_rows * block, width), jnp.bfloat16),
+            jax.ShapeDtypeStruct((1,), jnp.int32),
+        ),
+        in_specs=[scalar, scalar, WHOLE, WHOLE],
+        out_specs=(WHOLE, scalar),
         scratch_shapes=[pltpu.VMEM((block_rows, nonzero * block, width), jnp.bfloat16)],
         compiler_params=pltpu.CompilerParams(vmem_limit_bytes=14 << 20),
         cost_estimate=pl.CostEstimate(
@@ -54,16 +47,35 @@
             transcendentals=0,
         ),
         name="block_product",
-    )(which, offsets, adj, *parts, *carried)
-
-
-def middle_kernel(here_ref, there_ref, weight_ref, parcel_ref):
-    half = here_ref.shape[1]
-    rows = here_ref.shape[0] // 2
-    own = here_ref[:rows, :]
+    )(offsets, feat.reshape(1), adj, panels)
+
+
+def copies_kernel(value_ref, out_ref, sems):
+    copies = [pltpu.make_async_copy(value_ref, out_ref.at[i], sems.at[i]) for i in range(out_ref.shape[0])]
+    for copy in copies:
+        copy.start()
+    for copy in copies:
+        copy.wait()
+
+
+def copies_of(value, count):
+    return pl.pallas_call(
+        copies_kernel,
+        out_shape=jax.ShapeDtypeStruct((count, *value.shape), value.dtype),
+        in_specs=[pl.BlockSpec(memory_space=pl.ANY)],
+        out_specs=pl.BlockSpec(memory_space=pl.ANY),
+        scratch_shapes=[pltpu.SemaphoreType.DMA((count,))],
+        compiler_params=SMALL,
+        name="copies_of",
+    )(value)
+
+
+def middle_kernel(own_ref, other_ref, mine_ref, theirs_ref, weight_ref, parcel_ref):
+    rows, half = own_ref.shape
+    own = own_ref[...]
     logits = jnp.dot(own, weight_ref[:half, :], preferred_element_type=jnp.float32)
-    logits += jnp.dot(there_ref[:rows, :], weight_ref[half:, :], preferred_element_type=jnp.float32)
-    target = jnp.concatenate([here_ref[rows:, :], there_ref[rows:, :]], axis=1).astype(jnp.float32)
+    logits += jnp.dot(other_ref[...], weight_ref[half:, :], preferred_element_type=jnp.float32)
+    target = jnp.concatenate([mine_ref[...], theirs_ref[...]], axis=1).astype(jnp.float32)
     logistic = jax.nn.sigmoid(logits)
     slope = logistic * (1.0 + logits * (1.0 - logistic))
     grad_out = ((logits * logistic - target) * slope).astype(jnp.bfloat16)
@@ -85,8 +97,8 @@
                 start += quarter
 
 
-def middle(here, there, weight):
-    rows, half = here.shape[0] // 2, here.shape[1]
+def middle(own, other, mine, theirs, weight):
+    rows, half = own.shape
     extra = 2 * weight.shape[1] // SIDE
     return pl.pallas_call(
         middle_kernel,
@@ -96,11 +108,7 @@
             flops=4 * rows * weight.size, bytes_accessed=12 * rows * half, transcendentals=rows * weight.shape[1]
         ),
         name="middle",
-    )(here, there, weight)
-
-
-WHOLE = pl.BlockSpec(memory_space=pltpu.VMEM)
-SMALL = pltpu.CompilerParams(vmem_limit_bytes=4 << 20)
+    )(own, other, mine, theirs, weight)
 
 
 def open_kernel(parcels_ref, quarter_ref, column_ref):
@@ -145,7 +153,7 @@
     )(pieces, *after)
 
 
-def settle_kernel(scale, feat_ref, pieces_ref, after_ref, out_ref):
+def settle_kernel(scale, feat_ref, pieces_ref, out_ref):
     halves, half = out_ref.shape[1] // pieces_ref.shape[2], pieces_ref.shape[2]
     per_half = pieces_ref.shape[0] // halves
     for index in range(halves):
@@ -153,16 +161,16 @@
         out_ref[:, index * half : (index + 1) * half] = values.reshape(out_ref.shape[0], half)
 
 
-def settle(feat, pieces, after, scale):
+def settle(feat, pieces, scale):
     count, rows, half = pieces.shape
     return pl.pallas_call(
         functools.partial(settle_kernel, scale),
         out_shape=jax.ShapeDtypeStruct((count * rows // 2, 2 * half), pieces.dtype),
-        in_specs=[pl.BlockSpec(memory_space=pltpu.SMEM), WHOLE, pl.BlockSpec(memory_space=pl.ANY)],
+        in_specs=[pl.BlockSpec(memory_space=pltpu.SMEM), WHOLE],
         out_specs=WHOLE,
         compiler_params=SMALL,
         name="settle",
-    )(feat.reshape(1), pieces, after)
+    )(feat, pieces)
 
 
 def to_all(value, axis, count, groups=None):
@@ -207,22 +215,23 @@
         labels[:, None] == jnp.arange(centroid.shape[0], dtype=jnp.int32)[None, :]
     ).astype(jnp.bfloat16)
     target = jnp.dot(label_table, centroid, preferred_element_type=jnp.float32).astype(jnp.bfloat16)
+    theirs = lax.ppermute(target, "feat", [(0, 1), (1, 0)])
     swapped = jnp.roll(weight, (half, centroid.shape[1]), (0, 1))
     turned = jnp.where(feat == 0, weight, swapped)
 
     column = to_all(features, "col", SIDE, ALONG_Y).reshape(-1, half)
-    panels = to_all(column, "col", SIDE, ALONG_X).reshape(-1, half)
+    panels = lax.all_to_all(copies_of(column, SIDE), "col", 0, 0, axis_index_groups=ALONG_X).reshape(-1, half)
     offsets = (owner_x * SIDE + owner_y) * row_count + within
-    here = block_product(offsets, offsets, adj, [panels], (target,))
-    there = lax.ppermute(here, "feat", [(0, 1), (1, 0)])
-
-    parcels = lax.all_to_all(middle(here, there, turned), "col", 0, 0, axis_index_groups=ALONG_Y)
+    own, _ = block_product(offsets, feat, adj, panels)
+    other = lax.ppermute(own, "feat", [(0, 1), (1, 0)])
+
+    parcels = lax.all_to_all(middle(own, other, target, theirs, turned), "col", 0, 0, axis_index_groups=ALONG_Y)
     quarter, column = open_parcels(parcels, row_count)
     column = column.reshape(-1, half)
     gathered = lax.all_gather(column, "col", axis=0, tiled=True, axis_index_groups=ALONG_X)
-    feature_grad = block_product(offsets, offsets, adj, [gathered])
-
-    weight_grad = settle(feat, sum_weight(quarter, row_size), feature_grad, 1.0 / math.sqrt(node_count))
+    feature_grad, same = block_product(offsets, feat, adj, gathered)
+
+    weight_grad = settle(same, sum_weight(quarter, row_size), 1.0 / math.sqrt(node_count))
     return (weight_grad, feature_grad)
 
 

time: 156 us -> 155 us (level)
  waiting for transfers between devices: 25.9 us -> 18 us
  starting transfers between devices: 20.9 us -> 28.2 us
  local copies, waits for them, and re-layouts: 5.81 us -> 3.55 us
    all_to_all x1, waiting for transfers between devices: 19.4 us -> 11.1 us  [per_device(): lax.all_to_all(copies_of(column, SIDE), 'col', 0, 0, axis_index_groups=AL...]
    ppermute x1 -> x2, starting transfers between devices: 8.53 us -> 16 us  [the longest x1 8.55 us: per_device(): other = lax.ppermute(own, 'feat', [(0, 1), (1, 0)])]
    broadcast_in_dim x2 -> x1, local copies, waits for them, and re-layouts: 2.62 us -> 1.01 us  [to_all(): copies = jnp.broadcast_to(value[None], (count, *value.shape))]
    pallas_call x2 -> x3, Pallas kernels: 3.62 us -> 4.44 us  [the longest x2 3.08 us: block_product(): pl.pallas_call(product_kernel, out_shape=(jax.ShapeDtypeStruct((block_row...]
  transfers between devices with their start and end apart: 4 -> 5, of which waited for: 4 -> 4; matrix products, arithmetic and copies ran while one was open for 1% -> 1% of each run, Pallas kernels for 2% -> 2%
where the time goes in v8:
time: 155 us; the launch traced here: 152 us
  blocking collectives  77.9 us (50%)
  starting transfers between devices  28.2 us (18%)
  waiting for transfers between devices  18 us (12%)
  between operations  14.2 us (9%)
  Pallas kernels  8.78 us (6%)
  local copies, waits for them, and re-layouts  3.55 us (2%)
    all_to_all x1, blocking collectives, sum_weight(): lax.all_to_all(spread_sum(pieces, layers), both, 0, 0, axis_index_groups=...  30.1 us
    all_to_all x1, blocking collectives, per_device(): lax.all_to_all(middle(own, other, target, theirs, turned), 'col', 0, 0, a...  20.5 us
    all_to_all x1, blocking collectives, to_all(): return lax.all_to_all(copies, axis, 0, 0, axis_index_groups=groups)  19.9 us
    all_to_all x1, waiting for transfers between devices, per_device(): lax.all_to_all(copies_of(column, SIDE), 'col', 0, 0, axis_index_groups=AL...  11.1 us
    ppermute x1, starting transfers between devices, per_device(): other = lax.ppermute(own, 'feat', [(0, 1), (1, 0)])  8.55 us
    all_to_all x1, blocking collectives, sum_weight(): pieces = lax.all_to_all(pieces, both, 0, 0, axis_index_groups=mates)  7.48 us
    ppermute x1, starting transfers between devices, per_device(): theirs = lax.ppermute(target, 'feat', [(0, 1), (1, 0)])  7.43 us
    all_to_all x1, starting transfers between devices, per_device(): lax.all_to_all(copies_of(column, SIDE), 'col', 0, 0, axis_index_groups=AL...  6.88 us
  transfers between devices with their start and end apart: 5, of which 4 were waited for; matrix products, arithmetic and copies ran while one was open for 1% of the time, Pallas kernels for 2%

profile of v8, /device:TPU:1, one launch (start us, length us, event | category | flops | bytes accessed | tf_op | source)
XLA Modules:
  0.0 151.9 jit_solution(1981867019951442250)
XLA Ops:
  7.2 1.0 broadcast_in_dim.2
  8.2 19.9 %all_to_all.30 = bf16[4,512,128]{2,1,0:T(8,128)(2,1)S(1)} all-to-all(bf16[4,512,128]{2,1,0:T(8,128)(2,1)S(1)} %broadcast_in_dim.2), channel_id=1, replica_groups={{0,8,16,24},{2,10,18,26},{4,12,20,28},{6,14,22,30},{1,9,17,25},{3,11,19..., dimensions={0} | all-to-all | bytes 1048576 | tf_op jit(solution)/shard_map/all_to_all | solution.py:178
  28.1 1.4 copies_of.1
  29.5 6.9 %all-to-all-start.1 = ((bf16[4,2048,128]{2,1,0:T(8,128)(2,1)}), bf16[4,2048,128]{2,1,0:T(8,128)(2,1)S(1)}, u32[]{:S(2)}, u32[]{:S(2)}) async-start(bf16[4,2048,128]{2,1,0:T(8,128)(2,1)} %copies_of.1), calls=%async_computation.1 | async-start | bytes 4194304 | tf_op jit(solution)/shard_map/all_to_all | solution.py:223
  36.4 0.5 fusion.1.mine_ref
  36.9 7.4 %collective-permute-start.1 = (bf16[512,128]{1,0:T(8,128)(2,1)S(1)}, bf16[512,128]{1,0:T(8,128)(2,1)}, u32[]{:S(2)}, u32[]{:S(2)}) collective-permute-start(bf16[512,128]{1,0:T(8,128)(2,1)S(1)} %fusion.1.mine_ref), channel_id=1, source_target_pairs={{0,1},{1,0},{2,3},{3,2},{4,5},{5,4},{6,7},{7,6},{8,9},{9,8},{10,11... | collective-permute-start | bytes 393224 | tf_op jit(solution)/shard_map/ppermute | solution.py:218
  44.3 0.9 fusion.15
  45.2 0.6 fusion.5
  45.9 11.1 %all-to-all-done.1 = bf16[4,2048,128]{2,1,0:T(8,128)(2,1)S(1)} async-done(((bf16[4,2048,128]{2,1,0:T(8,128)(2,1)}), bf16[4,2048,128]{2,1,0:T(8,128)(2,1)S(1)}, u32[]{:S(2)}, u32[]{:S(2)}) %all-to-all-start.1) | async-done | bytes 2097184 | tf_op jit(solution)/shard_map/all_to_all | solution.py:223
  57.0 1.3 block_product.2
  58.3 8.5 %collective-permute-start = (bf16[512,128]{1,0:T(8,128)(2,1)S(1)}, bf16[512,128]{1,0:T(8,128)(2,1)S(1)}, u32[]{:S(2)}, u32[]{:S(2)}) collective-permute-start(bf16[512,128]{1,0:T(8,128)(2,1)S(1)} %get-tuple-element.7.own_ref), channel_id=1, source_target_pairs={{0,1},{1,0},{2,3},{3,2},{4,5},{5,4},{6,7},{7,6},{8,9},{9,8},{10,11... | collective-permute-start | bytes 393224 | tf_op jit(solution)/shard_map/ppermute | solution.py:226
  67.0 0.9 collective-permute-done.other_ref
  67.9 1.5 %middle.1 = bf16[4,640,128]{2,1,0:T(8,128)(2,1)S(1)} custom-call(bf16[512,128]{1,0:T(8,128)(2,1)S(1)} %get-tuple-element.7.own_ref, bf16[512,128]{1,0:T(8,128)(2,1)S(1)} %collective-permute-done.other_ref, bf16[512,128]{1,0:T(8,128)(2,1)S(1)} %fusion.1.mine_ref, bf16[512,128]{1,0:T(8,128)(2,1)} %collective-permute-done.1.theirs_ref, ...), custom_call_target="tpu_custom_call" | custom-call | flops 134217728 | bytes 786432 | tf_op jit(solution)/shard_map/middle/pallas_call | solution.py:103
  69.4 20.5 %all_to_all.31.parcels_ref = bf16[4,640,128]{2,1,0:T(8,128)(2,1)S(1)} all-to-all(bf16[4,640,128]{2,1,0:T(8,128)(2,1)S(1)} %middle.1), channel_id=1, replica_groups={{0,8,16,24},{2,10,18,26},{4,12,20,28},{6,14,22,30},{1,9,17,25},{3,11,19..., dimensions={0} | all-to-all | bytes 1310720 | tf_op jit(solution)/shard_map/all_to_all | solution.py:228
  89.9 0.8 open_parcels.1
  90.7 7.5 %all_to_all.32.pieces_ref = f32[8,8,128]{2,1,0:T(8,128)S(1)} all-to-all(f32[8,8,128]{2,1,0:T(8,128)S(1)} %bitcast.8), channel_id=1, replica_groups={{0,2,4,6,32,34,36,38},{8,10,12,14,40,42,44,46},{16,18,20,22,48,50,52,54..., dimensions={0} | all-to-all | bytes 65536 | tf_op jit(solution)/shard_map/all_to_all | solution.py:198
  98.2 30.1 %all_to_all.33.pieces_ref = f32[16,8,128]{2,1,0:T(8,128)S(1)} all-to-all(f32[16,8,128]{2,1,0:T(8,128)S(1)} %spread_sum.2), channel_id=1, replica_groups={{0,64,128,192,256,320,384,448,512,576,640,704,768,832,896,960},{2,66,13..., dimensions={0} | all-to-all | bytes 131072 | tf_op jit(solution)/shard_map/all_to_all | solution.py:199
  128.3 0.7 spread_sum.3
  129.0 5.4 %all-to-all-start.5 = ((f32[32,8,128]{2,1,0:T(8,128)}), f32[32,8,128]{2,1,0:T(8,128)S(1)}, u32[]{:S(2)}, u32[]{:S(2)}) async-start(f32[32,8,128]{2,1,0:T(8,128)} %spread_sum.3), calls=%async_computation.5 | async-start | bytes 262144 | tf_op jit(solution)/shard_map/all_to_all | solution.py:200
  134.4 1.2 all-gather.2.cloned.1.call-done.panels_ref
  135.5 1.6 %copy-done.2 = bf16[8192,128]{1,0:T(8,128)(2,1)S(1)} copy-done((bf16[8192,128]{1,0:T(8,128)(2,1)S(1)}, bf16[8192,128]{1,0:T(8,128)(2,1)}, u32[]{:S(2)}) %copy-start.2) | copy-done | bytes 2097176
  137.1 1.8 %block_product.3 = (bf16[512,128]{1,0:T(8,128)(2,1)}, s32[1]{0:T(128)}) custom-call(s32[4,8]{1,0:T(4,128)S(1)} %fusion.10.offset_ref, s32[1]{0:T(128)} %bitcast.feat_ref, bf16[4,8,128,128]{3,2,1,0:T(8,128)(2,1)S(1)} %copy-done.1, bf16[8192,128]{1,0:T(8,128)(2,1)S(1)} %copy-done.2), custom_call_target="tpu_custom_call" | custom-call | flops 134217728 | bytes 2097152 | tf_op jit(solution)/shard_map/block_product/pallas_call | solution.py:34
  138.9 4.9 %all-to-all-done.5.pieces_ref = f32[32,8,128]{2,1,0:T(8,128)S(1)} async-done(((f32[32,8,128]{2,1,0:T(8,128)}), f32[32,8,128]{2,1,0:T(8,128)S(1)}, u32[]{:S(2)}, u32[]{:S(2)}) %all-to-all-start.5) | async-done | bytes 131104 | tf_op jit(solution)/shard_map/all_to_all | solution.py:200
  143.7 1.3 settle.1
  (27 shorter events, 0.2 us)
Async XLA Ops:
  7.2 29.2 %copy-start = (bf16[1024,128]{1,0:T(8,128)(2,1)S(1)}, bf16[1024,128]{1,0:T(8,128)(2,1)}, u32[]{:S(2)}) copy-start(bf16[1024,128]{1,0:T(8,128)(2,1)} %param.10) | copy-start | bytes 786436
  29.4 6.9 %copy-start.10 = (s32[512]{0:T(512)S(1)}, s32[512]{0:T(512)}, u32[]{:S(2)}) copy-start(s32[512]{0:T(512)} %param.11) | copy-start | bytes 6148
  29.4 16.4 %copy-start.9 = (s32[4,8]{1,0:T(4,128)S(1)}, s32[4,8]{1,0:T(4,128)}, u32[]{:S(2)}) copy-start(s32[4,8]{1,0:T(4,128)} %param.8) | copy-start | bytes 388
  29.4 27.6 %copy-start.1 = (bf16[4,8,128,128]{3,2,1,0:T(8,128)(2,1)S(1)}, bf16[4,8,128,128]{3,2,1,0:T(8,128)(2,1)}, u32[]{:S(2)}) copy-start(bf16[4,8,128,128]{3,2,1,0:T(8,128)(2,1)} %adj_ref.3) | copy-start | bytes 3145732
  29.5 27.5 %all-to-all-start.1 = ((bf16[4,2048,128]{2,1,0:T(8,128)(2,1)}), bf16[4,2048,128]{2,1,0:T(8,128)(2,1)S(1)}, u32[]{:S(2)}, u32[]{:S(2)}) async-start(bf16[4,2048,128]{2,1,0:T(8,128)(2,1)} %copies_of.1), calls=%async_computation.1 | async-start | bytes 4194304 | tf_op jit(solution)/shard_map/all_to_all | solution.py:223
  36.3 99.2 %all-gather.2.cloned.1.call-start = ((), (), s32[]{:S(2)}) async-start(), calls=%async_computation.6 | async-start | bytes 2621440 | tf_op jit(solution)/shard_map/all_gather | solution.py:231
  36.9 30.1 %collective-permute-start.1 = (bf16[512,128]{1,0:T(8,128)(2,1)S(1)}, bf16[512,128]{1,0:T(8,128)(2,1)}, u32[]{:S(2)}, u32[]{:S(2)}) collective-permute-start(bf16[512,128]{1,0:T(8,128)(2,1)S(1)} %fusion.1.mine_ref), channel_id=1, source_target_pairs={{0,1},{1,0},{2,3},{3,2},{4,5},{5,4},{6,7},{7,6},{8,9},{9,8},{10,11... | collective-permute-start | bytes 393224 | tf_op jit(solution)/shard_map/ppermute | solution.py:218
  45.2 0.7 copy-start.3
  45.2 0.6 copy-start.5
  57.0 9.9 %copy-start.4 = (bf16[128,256]{1,0:T(8,128)(2,1)S(1)}, bf16[128,256]{1,0:T(8,128)(2,1)}, u32[]{:S(2)}) copy-start(bf16[128,256]{1,0:T(8,128)(2,1)} %copy-done.3) | copy-start | bytes 196612
  57.0 9.9 %copy-start.6 = (bf16[128,256]{1,0:T(8,128)(2,1)S(1)}, bf16[128,256]{1,0:T(8,128)(2,1)}, u32[]{:S(2)}) copy-start(bf16[128,256]{1,0:T(8,128)(2,1)} %copy-done.5) | copy-start | bytes 196612
  57.0 9.9 %copy-start.7 = (bf16[256,256]{1,0:T(8,128)(2,1)S(1)}, bf16[256,256]{1,0:T(8,128)(2,1)}, u32[]{:S(2)}) copy-start(bf16[256,256]{1,0:T(8,128)(2,1)} %param.9) | copy-start | bytes 393220
  57.0 9.9 %copy-start.8 = (bf16[256,128]{1,0:T(8,128)(2,1)S(1)}, bf16[256,128]{1,0:T(8,128)(2,1)}, u32[]{:S(2)}) copy-start(bf16[256,128]{1,0:T(8,128)(2,1)} %fusion.5) | copy-start | bytes 196612
  58.3 9.5 %collective-permute-start = (bf16[512,128]{1,0:T(8,128)(2,1)S(1)}, bf16[512,128]{1,0:T(8,128)(2,1)S(1)}, u32[]{:S(2)}, u32[]{:S(2)}) collective-permute-start(bf16[512,128]{1,0:T(8,128)(2,1)S(1)} %get-tuple-element.7.own_ref), channel_id=1, source_target_pairs={{0,1},{1,0},{2,3},{3,2},{4,5},{5,4},{6,7},{7,6},{8,9},{9,8},{10,11... | collective-permute-start | bytes 393224 | tf_op jit(solution)/shard_map/ppermute | solution.py:226
  129.0 14.8 %all-to-all-start.5 = ((f32[32,8,128]{2,1,0:T(8,128)}), f32[32,8,128]{2,1,0:T(8,128)S(1)}, u32[]{:S(2)}, u32[]{:S(2)}) async-start(f32[32,8,128]{2,1,0:T(8,128)} %spread_sum.3), calls=%async_computation.5 | async-start | bytes 262144 | tf_op jit(solution)/shard_map/all_to_all | solution.py:200
  135.5 1.6 %copy-start.2 = (bf16[8192,128]{1,0:T(8,128)(2,1)S(1)}, bf16[8192,128]{1,0:T(8,128)(2,1)}, u32[]{:S(2)}) copy-start(bf16[8192,128]{1,0:T(8,128)(2,1)} %all-gather.2.cloned.1.call-done.panels_ref) | copy-start | bytes 6291460
Sparse Core Ops, SparseCore 0:
  90.9 44.6 all-gather.1

commit v9 on v8

--- a/solution.py
+++ b/solution.py
@@ -14,9 +14,8 @@
 Y_LO = 2
 
 
-def product_kernel(offset_ref, feat_ref, adj_ref, panels_ref, out_ref, same_ref, held):
+def product_kernel(offset_ref, adj_ref, panels_ref, out_ref, last_ref, held):
     block_rows, nonzero, block, _ = adj_ref.shape
-    same_ref[0] = feat_ref[0]
     for r in range(block_rows):
         for k in range(nonzero):
             start = pl.multiple_of(offset_ref[r, k], block)
@@ -25,20 +24,20 @@
         left = jnp.concatenate([adj_ref[r, k] for k in range(nonzero)], axis=1)
         total = jnp.dot(left, held[r], preferred_element_type=jnp.float32)
         out_ref[pl.ds(r * block, block), :] = total.astype(out_ref.dtype)
-
-
-def block_product(offsets, feat, adj, panels):
+    last_ref[...] = total[block - last_ref.shape[0] :, :]
+
+
+def block_product(offsets, adj, panels):
     block_rows, nonzero, block, _ = adj.shape
     width = panels.shape[1]
-    scalar = pl.BlockSpec(memory_space=pltpu.SMEM)
     return pl.pallas_call(
         product_kernel,
         out_shape=(
             jax.ShapeDtypeStruct((block_rows * block, width), jnp.bfloat16),
-            jax.ShapeDtypeStruct((1,), jnp.int32),
-        ),
-        in_specs=[scalar, scalar, WHOLE, WHOLE],
-        out_specs=(WHOLE, scalar),
+            jax.ShapeDtypeStruct((8, width), jnp.float32),
+        ),
+        in_specs=[pl.BlockSpec(memory_space=pltpu.SMEM), WHOLE, WHOLE],
+        out_specs=(WHOLE, WHOLE),
         scratch_shapes=[pltpu.VMEM((block_rows, nonzero * block, width), jnp.bfloat16)],
         compiler_params=pltpu.CompilerParams(vmem_limit_bytes=14 << 20),
         cost_estimate=pl.CostEstimate(
@@ -47,7 +46,7 @@
             transcendentals=0,
         ),
         name="block_product",
-    )(offsets, feat.reshape(1), adj, panels)
+    )(offsets, adj, panels)
 
 
 def copies_kernel(value_ref, out_ref, sems):
@@ -153,7 +152,7 @@
     )(pieces, *after)
 
 
-def settle_kernel(scale, feat_ref, pieces_ref, out_ref):
+def settle_kernel(scale, feat_ref, pieces_ref, last_ref, out_ref):
     halves, half = out_ref.shape[1] // pieces_ref.shape[2], pieces_ref.shape[2]
     per_half = pieces_ref.shape[0] // halves
     for index in range(halves):
@@ -161,16 +160,16 @@
         out_ref[:, index * half : (index + 1) * half] = values.reshape(out_ref.shape[0], half)
 
 
-def settle(feat, pieces, scale):
+def settle(feat, pieces, last, scale):
     count, rows, half = pieces.shape
     return pl.pallas_call(
         functools.partial(settle_kernel, scale),
         out_shape=jax.ShapeDtypeStruct((count * rows // 2, 2 * half), pieces.dtype),
-        in_specs=[pl.BlockSpec(memory_space=pltpu.SMEM), WHOLE],
+        in_specs=[pl.BlockSpec(memory_space=pltpu.SMEM), WHOLE, WHOLE],
         out_specs=WHOLE,
         compiler_params=SMALL,
         name="settle",
-    )(feat, pieces)
+    )(feat.reshape(1), pieces, last)
 
 
 def to_all(value, axis, count, groups=None):
@@ -222,16 +221,16 @@
     column = to_all(features, "col", SIDE, ALONG_Y).reshape(-1, half)
     panels = lax.all_to_all(copies_of(column, SIDE), "col", 0, 0, axis_index_groups=ALONG_X).reshape(-1, half)
     offsets = (owner_x * SIDE + owner_y) * row_count + within
-    own, _ = block_product(offsets, feat, adj, panels)
+    own, _ = block_product(offsets, adj, panels)
     other = lax.ppermute(own, "feat", [(0, 1), (1, 0)])
 
     parcels = lax.all_to_all(middle(own, other, target, theirs, turned), "col", 0, 0, axis_index_groups=ALONG_Y)
     quarter, column = open_parcels(parcels, row_count)
     column = column.reshape(-1, half)
     gathered = lax.all_gather(column, "col", axis=0, tiled=True, axis_index_groups=ALONG_X)
-    feature_grad, same = block_product(offsets, feat, adj, gathered)
-
-    weight_grad = settle(same, sum_weight(quarter, row_size), 1.0 / math.sqrt(node_count))
+    feature_grad, last = block_product(offsets, adj, gathered)
+
+    weight_grad = settle(feat, sum_weight(quarter, row_size), last, 1.0 / math.sqrt(node_count))
     return (weight_grad, feature_grad)
 
 

time: 155 us -> 154 us (level)
  transfers between devices with their start and end apart: 5 -> 5, of which waited for: 4 -> 4; matrix products, arithmetic and copies ran while one was open for 1% -> 1% of each run, Pallas kernels for 2% -> 3%
where the time goes in v9:
time: 154 us; the launch traced here: 152 us
  blocking collectives  77.9 us (51%)
  starting transfers between devices  28.2 us (18%)
  waiting for transfers between devices  18 us (12%)
  between operations  14.2 us (9%)
  Pallas kernels  8.53 us (6%)
  local copies, waits for them, and re-layouts  3.55 us (2%)
    all_to_all x1, blocking collectives, sum_weight(): lax.all_to_all(spread_sum(pieces, layers), both, 0, 0, axis_index_groups=...  30.1 us
    all_to_all x1, blocking collectives, per_device(): lax.all_to_all(middle(own, other, target, theirs, turned), 'col', 0, 0, a...  20.5 us
    all_to_all x1, blocking collectives, to_all(): return lax.all_to_all(copies, axis, 0, 0, axis_index_groups=groups)  19.9 us
    all_to_all x1, waiting for transfers between devices, per_device(): lax.all_to_all(copies_of(column, SIDE), 'col', 0, 0, axis_index_groups=AL...  11.1 us
    ppermute x1, starting transfers between devices, per_device(): other = lax.ppermute(own, 'feat', [(0, 1), (1, 0)])  8.53 us
    all_to_all x1, blocking collectives, sum_weight(): pieces = lax.all_to_all(pieces, both, 0, 0, axis_index_groups=mates)  7.48 us
    ppermute x1, starting transfers between devices, per_device(): theirs = lax.ppermute(target, 'feat', [(0, 1), (1, 0)])  7.43 us
    all_to_all x1, starting transfers between devices, per_device(): lax.all_to_all(copies_of(column, SIDE), 'col', 0, 0, axis_index_groups=AL...  6.88 us
  transfers between devices with their start and end apart: 5, of which 4 were waited for; matrix products, arithmetic and copies ran while one was open for 1% of the time, Pallas kernels for 3%

profile of v9, /device:TPU:1, one launch (start us, length us, event | category | flops | bytes accessed | tf_op | source)
XLA Modules:
  0.0 151.6 jit_solution(4726417091043599638)
XLA Ops:
  7.2 1.0 broadcast_in_dim.2
  8.2 19.9 %all_to_all.30 = bf16[4,512,128]{2,1,0:T(8,128)(2,1)S(1)} all-to-all(bf16[4,512,128]{2,1,0:T(8,128)(2,1)S(1)} %broadcast_in_dim.2), channel_id=1, replica_groups={{0,8,16,24},{2,10,18,26},{4,12,20,28},{6,14,22,30},{1,9,17,25},{3,11,19..., dimensions={0} | all-to-all | bytes 1048576 | tf_op jit(solution)/shard_map/all_to_all | solution.py:177
  28.1 1.4 copies_of.1
  29.5 6.9 %all-to-all-start.1 = ((bf16[4,2048,128]{2,1,0:T(8,128)(2,1)}), bf16[4,2048,128]{2,1,0:T(8,128)(2,1)S(1)}, u32[]{:S(2)}, u32[]{:S(2)}) async-start(bf16[4,2048,128]{2,1,0:T(8,128)(2,1)} %copies_of.1), calls=%async_computation.1 | async-start | bytes 4194304 | tf_op jit(solution)/shard_map/all_to_all | solution.py:222
  36.4 0.5 fusion.1.mine_ref
  36.9 7.4 %collective-permute-start.1 = (bf16[512,128]{1,0:T(8,128)(2,1)S(1)}, bf16[512,128]{1,0:T(8,128)(2,1)}, u32[]{:S(2)}, u32[]{:S(2)}) collective-permute-start(bf16[512,128]{1,0:T(8,128)(2,1)S(1)} %fusion.1.mine_ref), channel_id=1, source_target_pairs={{0,1},{1,0},{2,3},{3,2},{4,5},{5,4},{6,7},{7,6},{8,9},{9,8},{10,11... | collective-permute-start | bytes 393224 | tf_op jit(solution)/shard_map/ppermute | solution.py:217
  44.3 0.9 fusion.15
  45.2 0.6 fusion.5
  45.9 11.1 %all-to-all-done.1 = bf16[4,2048,128]{2,1,0:T(8,128)(2,1)S(1)} async-done(((bf16[4,2048,128]{2,1,0:T(8,128)(2,1)}), bf16[4,2048,128]{2,1,0:T(8,128)(2,1)S(1)}, u32[]{:S(2)}, u32[]{:S(2)}) %all-to-all-start.1) | async-done | bytes 2097184 | tf_op jit(solution)/shard_map/all_to_all | solution.py:222
  57.0 1.7 %block_product.2 = (bf16[512,128]{1,0:T(8,128)(2,1)S(1)}, f32[8,128]{1,0:T(8,128)}) custom-call(s32[4,8]{1,0:T(4,128)S(1)} %fusion.10.offset_ref, bf16[4,8,128,128]{3,2,1,0:T(8,128)(2,1)S(1)} %copy-done.1, bf16[8192,128]{1,0:T(8,128)(2,1)S(1)} %bitcast.6), custom_call_target="tpu_custom_call" | custom-call | flops 134217728 | bytes 2097152 | tf_op jit(solution)/shard_map/block_product/pallas_call | solution.py:33
  58.7 8.5 %collective-permute-start = (bf16[512,128]{1,0:T(8,128)(2,1)S(1)}, bf16[512,128]{1,0:T(8,128)(2,1)S(1)}, u32[]{:S(2)}, u32[]{:S(2)}) collective-permute-start(bf16[512,128]{1,0:T(8,128)(2,1)S(1)} %get-tuple-element.7.own_ref), channel_id=1, source_target_pairs={{0,1},{1,0},{2,3},{3,2},{4,5},{5,4},{6,7},{7,6},{8,9},{9,8},{10,11... | collective-permute-start | bytes 393224 | tf_op jit(solution)/shard_map/ppermute | solution.py:225
  67.3 0.9 collective-permute-done.other_ref
  68.2 1.5 %middle.1 = bf16[4,640,128]{2,1,0:T(8,128)(2,1)S(1)} custom-call(bf16[512,128]{1,0:T(8,128)(2,1)S(1)} %get-tuple-element.7.own_ref, bf16[512,128]{1,0:T(8,128)(2,1)S(1)} %collective-permute-done.other_ref, bf16[512,128]{1,0:T(8,128)(2,1)S(1)} %fusion.1.mine_ref, bf16[512,128]{1,0:T(8,128)(2,1)} %collective-permute-done.1.theirs_ref, ...), custom_call_target="tpu_custom_call" | custom-call | flops 134217728 | bytes 786432 | tf_op jit(solution)/shard_map/middle/pallas_call | solution.py:102
  69.8 20.5 %all_to_all.31.parcels_ref = bf16[4,640,128]{2,1,0:T(8,128)(2,1)S(1)} all-to-all(bf16[4,640,128]{2,1,0:T(8,128)(2,1)S(1)} %middle.1), channel_id=1, replica_groups={{0,8,16,24},{2,10,18,26},{4,12,20,28},{6,14,22,30},{1,9,17,25},{3,11,19..., dimensions={0} | all-to-all | bytes 1310720 | tf_op jit(solution)/shard_map/all_to_all | solution.py:227
  90.2 0.8 open_parcels.1
  91.1 7.5 %all_to_all.32.pieces_ref = f32[8,8,128]{2,1,0:T(8,128)S(1)} all-to-all(f32[8,8,128]{2,1,0:T(8,128)S(1)} %bitcast.8), channel_id=1, replica_groups={{0,2,4,6,32,34,36,38},{8,10,12,14,40,42,44,46},{16,18,20,22,48,50,52,54..., dimensions={0} | all-to-all | bytes 65536 | tf_op jit(solution)/shard_map/all_to_all | solution.py:197
  98.6 30.1 %all_to_all.33.pieces_ref = f32[16,8,128]{2,1,0:T(8,128)S(1)} all-to-all(f32[16,8,128]{2,1,0:T(8,128)S(1)} %spread_sum.2), channel_id=1, replica_groups={{0,64,128,192,256,320,384,448,512,576,640,704,768,832,896,960},{2,66,13..., dimensions={0} | all-to-all | bytes 131072 | tf_op jit(solution)/shard_map/all_to_all | solution.py:198
  128.6 0.7 spread_sum.3
  129.3 5.4 %all-to-all-start.5 = ((f32[32,8,128]{2,1,0:T(8,128)}), f32[32,8,128]{2,1,0:T(8,128)S(1)}, u32[]{:S(2)}, u32[]{:S(2)}) async-start(f32[32,8,128]{2,1,0:T(8,128)} %spread_sum.3), calls=%async_computation.5 | async-start | bytes 262144 | tf_op jit(solution)/shard_map/all_to_all | solution.py:199
  134.7 1.2 all-gather.2.cloned.1.call-done.panels_ref
  135.9 1.6 %copy-done.2 = bf16[8192,128]{1,0:T(8,128)(2,1)S(1)} copy-done((bf16[8192,128]{1,0:T(8,128)(2,1)S(1)}, bf16[8192,128]{1,0:T(8,128)(2,1)}, u32[]{:S(2)}) %copy-start.2) | copy-done | bytes 2097176
  137.5 1.8 %block_product.3 = (bf16[512,128]{1,0:T(8,128)(2,1)}, f32[8,128]{1,0:T(8,128)S(1)}) custom-call(s32[4,8]{1,0:T(4,128)S(1)} %fusion.10.offset_ref, bf16[4,8,128,128]{3,2,1,0:T(8,128)(2,1)S(1)} %copy-done.1, bf16[8192,128]{1,0:T(8,128)(2,1)S(1)} %copy-done.2), custom_call_target="tpu_custom_call" | custom-call | flops 134217728 | bytes 2097152 | tf_op jit(solution)/shard_map/block_product/pallas_call | solution.py:33
  139.2 4.9 %all-to-all-done.5.pieces_ref = f32[32,8,128]{2,1,0:T(8,128)S(1)} async-done(((f32[32,8,128]{2,1,0:T(8,128)}), f32[32,8,128]{2,1,0:T(8,128)S(1)}, u32[]{:S(2)}, u32[]{:S(2)}) %all-to-all-start.5) | async-done | bytes 131104 | tf_op jit(solution)/shard_map/all_to_all | solution.py:199
  144.1 0.7 settle.1
  (27 shorter events, 0.2 us)
Async XLA Ops:
  7.2 29.2 %copy-start = (bf16[1024,128]{1,0:T(8,128)(2,1)S(1)}, bf16[1024,128]{1,0:T(8,128)(2,1)}, u32[]{:S(2)}) copy-start(bf16[1024,128]{1,0:T(8,128)(2,1)} %param.10) | copy-start | bytes 786436
  29.4 6.9 %copy-start.10 = (s32[512]{0:T(512)S(1)}, s32[512]{0:T(512)}, u32[]{:S(2)}) copy-start(s32[512]{0:T(512)} %param.11) | copy-start | bytes 6148
  29.4 16.4 %copy-start.9 = (s32[4,8]{1,0:T(4,128)S(1)}, s32[4,8]{1,0:T(4,128)}, u32[]{:S(2)}) copy-start(s32[4,8]{1,0:T(4,128)} %param.8) | copy-start | bytes 388
  29.4 27.6 %copy-start.1 = (bf16[4,8,128,128]{3,2,1,0:T(8,128)(2,1)S(1)}, bf16[4,8,128,128]{3,2,1,0:T(8,128)(2,1)}, u32[]{:S(2)}) copy-start(bf16[4,8,128,128]{3,2,1,0:T(8,128)(2,1)} %adj_ref.3) | copy-start | bytes 3145732
  29.5 27.5 %all-to-all-start.1 = ((bf16[4,2048,128]{2,1,0:T(8,128)(2,1)}), bf16[4,2048,128]{2,1,0:T(8,128)(2,1)S(1)}, u32[]{:S(2)}, u32[]{:S(2)}) async-start(bf16[4,2048,128]{2,1,0:T(8,128)(2,1)} %copies_of.1), calls=%async_computation.1 | async-start | bytes 4194304 | tf_op jit(solution)/shard_map/all_to_all | solution.py:222
  36.3 99.5 %all-gather.2.cloned.1.call-start = ((), (), s32[]{:S(2)}) async-start(), calls=%async_computation.6 | async-start | bytes 2621440 | tf_op jit(solution)/shard_map/all_gather | solution.py:230
  36.9 30.5 %collective-permute-start.1 = (bf16[512,128]{1,0:T(8,128)(2,1)S(1)}, bf16[512,128]{1,0:T(8,128)(2,1)}, u32[]{:S(2)}, u32[]{:S(2)}) collective-permute-start(bf16[512,128]{1,0:T(8,128)(2,1)S(1)} %fusion.1.mine_ref), channel_id=1, source_target_pairs={{0,1},{1,0},{2,3},{3,2},{4,5},{5,4},{6,7},{7,6},{8,9},{9,8},{10,11... | collective-permute-start | bytes 393224 | tf_op jit(solution)/shard_map/ppermute | solution.py:217
  45.2 0.7 copy-start.3
  45.2 0.6 copy-start.5
  57.0 10.3 %copy-start.4 = (bf16[128,256]{1,0:T(8,128)(2,1)S(1)}, bf16[128,256]{1,0:T(8,128)(2,1)}, u32[]{:S(2)}) copy-start(bf16[128,256]{1,0:T(8,128)(2,1)} %copy-done.3) | copy-start | bytes 196612
  57.0 10.3 %copy-start.6 = (bf16[128,256]{1,0:T(8,128)(2,1)S(1)}, bf16[128,256]{1,0:T(8,128)(2,1)}, u32[]{:S(2)}) copy-start(bf16[128,256]{1,0:T(8,128)(2,1)} %copy-done.5) | copy-start | bytes 196612
  57.0 10.3 %copy-start.7 = (bf16[256,256]{1,0:T(8,128)(2,1)S(1)}, bf16[256,256]{1,0:T(8,128)(2,1)}, u32[]{:S(2)}) copy-start(bf16[256,256]{1,0:T(8,128)(2,1)} %param.9) | copy-start | bytes 393220
  57.0 10.3 %copy-start.8 = (bf16[256,128]{1,0:T(8,128)(2,1)S(1)}, bf16[256,128]{1,0:T(8,128)(2,1)}, u32[]{:S(2)}) copy-start(bf16[256,128]{1,0:T(8,128)(2,1)} %fusion.5) | copy-start | bytes 196612
  58.7 9.5 %collective-permute-start = (bf16[512,128]{1,0:T(8,128)(2,1)S(1)}, bf16[512,128]{1,0:T(8,128)(2,1)S(1)}, u32[]{:S(2)}, u32[]{:S(2)}) collective-permute-start(bf16[512,128]{1,0:T(8,128)(2,1)S(1)} %get-tuple-element.7.own_ref), channel_id=1, source_target_pairs={{0,1},{1,0},{2,3},{3,2},{4,5},{5,4},{6,7},{7,6},{8,9},{9,8},{10,11... | collective-permute-start | bytes 393224 | tf_op jit(solution)/shard_map/ppermute | solution.py:225
  129.3 14.8 %all-to-all-start.5 = ((f32[32,8,128]{2,1,0:T(8,128)}), f32[32,8,128]{2,1,0:T(8,128)S(1)}, u32[]{:S(2)}, u32[]{:S(2)}) async-start(f32[32,8,128]{2,1,0:T(8,128)} %spread_sum.3), calls=%async_computation.5 | async-start | bytes 262144 | tf_op jit(solution)/shard_map/all_to_all | solution.py:199
  135.9 1.6 %copy-start.2 = (bf16[8192,128]{1,0:T(8,128)(2,1)S(1)}, bf16[8192,128]{1,0:T(8,128)(2,1)}, u32[]{:S(2)}) copy-start(bf16[8192,128]{1,0:T(8,128)(2,1)} %all-gather.2.cloned.1.call-done.panels_ref) | copy-start | bytes 6291460
Sparse Core Ops, SparseCore 0:
  91.2 44.6 all-gather.1
